TPU v7x, 32 devices: a whole 2x2x4 slice. The times are simulated.
32 devices in a mesh: row: 4 (over z), col: 8 (over y, x, core).
Axes of the slice: x: 2, y: 2, z: 4, core: 2. Of those that a mesh axis runs over, the one named last changes fastest.
Arguments:
- inputs: bfloat16 [384, 6144], P('col', 'row'), may hold values from -6 to 6
- cotangent: bfloat16 [384, 6144], P('col', 'row'), may hold values from -4 to 4
- gate_pre: bfloat16 [384, 16384], P('row', 'col'), may hold values from -10 to 10
- up_pre: bfloat16 [384, 16384], P('row', 'col'), may hold values from -6 to 6
- gate_weight: bfloat16 [6144, 16384], P('row', 'col'), may hold values from -0.078125 to 0.078125
- up_weight: bfloat16 [6144, 16384], P('row', 'col'), may hold values from -0.078125 to 0.078125
- down_weight: bfloat16 [16384, 6144], P('col', 'row'), may hold values from -0.046875 to 0.046875
Outputs:
- input_grad: bfloat16 [384, 6144], P('col', 'row')
- gate_grad: bfloat16 [6144, 16384], P('row', 'col')
- up_grad: bfloat16 [6144, 16384], P('row', 'col')
- down_grad: bfloat16 [16384, 6144], P('col', 'row')
All inputs are finite; a program needn't handle non-finite values.
Results may differ from a plain program's by a relative error of at most 0.033.
Values may be sent and summed in bfloat16 or wider, within the bound.
No kernel may reach another device: no remote copies, remote signals or barrier semaphores. Data moves between devices by JAX's collectives and lax.ppermute only.
A program may use at most 128 MiB of HBM per device.

v0:
```python
import jax
import jax.numpy as jnp
from jax import lax
from jax.sharding import PartitionSpec as P


def activate(gate_part, up_part, grad_part):
    gate_value = gate_part.astype(jnp.float32)
    up_value = up_part.astype(jnp.float32)
    sigma = jax.nn.sigmoid(gate_value)
    silu_value = gate_value * sigma
    hidden = (silu_value * up_value).astype(jnp.bfloat16)
    gate_delta = (grad_part * up_value * sigma * (1.0 + gate_value * (1.0 - sigma))).astype(
        jnp.bfloat16
    )
    up_delta = (grad_part * silu_value).astype(jnp.bfloat16)
    return (hidden, gate_delta, up_delta)


def over_tokens(left, right):
    return lax.dot_general(
        left, right, (((0,), (0,)), ((), ())), preferred_element_type=jnp.float32
    )


def over_columns(left, right):
    return lax.dot_general(
        left, right, (((1,), (1,)), ((), ())), preferred_element_type=jnp.float32
    )


def on_device(inputs, cotangent, gate_pre, up_pre, gate_weight, up_weight, down_weight):
    cotangent_all = lax.all_gather(cotangent, "col", axis=0, tiled=True)
    grad_share = lax.psum_scatter(
        over_columns(cotangent_all, down_weight).astype(jnp.bfloat16),
        "row",
        scatter_dimension=0,
        tiled=True,
    ).astype(jnp.float32)
    hidden, gate_delta, up_delta = activate(gate_pre, up_pre, grad_share)
    hidden_all, gate_all, up_all = (
        lax.all_gather(hidden, "row", axis=0, tiled=True),
        lax.all_gather(gate_delta, "row", axis=0, tiled=True),
        lax.all_gather(up_delta, "row", axis=0, tiled=True),
    )
    inputs_all = lax.all_gather(inputs, "col", axis=0, tiled=True)
    down_grad = over_tokens(hidden_all, cotangent_all).astype(jnp.bfloat16)
    gate_grad = over_tokens(inputs_all, gate_all).astype(jnp.bfloat16)
    up_grad = over_tokens(inputs_all, up_all).astype(jnp.bfloat16)
    input_grad = lax.psum_scatter(
        (over_columns(gate_all, gate_weight) + over_columns(up_all, up_weight)).astype(
            jnp.bfloat16
        ),
        "col",
        scatter_dimension=0,
        tiled=True,
    )
    return (input_grad, gate_grad, up_grad, down_grad)


def solution(mesh):
    placed = (
        P("col", "row"),
        P("col", "row"),
        P("row", "col"),
        P("row", "col"),
        P("row", "col"),
        P("row", "col"),
        P("col", "row"),
    )
    return jax.shard_map(
        on_device,
        mesh=mesh,
        in_specs=placed,
        out_specs=(P("col", "row"), P("row", "col"), P("row", "col"), P("col", "row")),
        check_vma=False,
    )
```

profile of v0, /device:TPU:0, one launch (start us, length us, event | category | flops | bytes accessed | tf_op | source)
XLA Modules:
  0.0 265.3 jit_solution(16717544471265479957)
XLA Ops:
  7.2 0.0 all-gather.6.cloned.1.call-start
  7.2 0.7 all-gather.6.cloned.1.call-update
  7.9 0.0 reduce-scatter.3.cloned.1.call-start
  7.9 28.7 %all-gather.6.cloned.1.call-done = bf16[384,1536]{1,0:T(8,128)(2,1)} async-done(((bf16[48,1536]{1,0:T(8,128)(2,1)}), bf16[384,1536]{1,0:T(8,128)(2,1)}) %all-gather.6.cloned.1.call-update) | async-done | bytes 1179664 | tf_op jit(solution)/shard_map/all_gather | solution.py:33
  36.7 6.9 %convolution_convert_fusion.3 = bf16[384,2048]{1,0:T(8,128)(2,1)} fusion(bf16[384,1536]{1,0:T(8,128)(2,1)} %all-gather.6.cloned.1.call-done, bf16[2048,1536]{1,0:T(8,128)(2,1)} %param.13), kind=kOutput, calls=%fused_computation.7 | convolution fusion | flops 2416705536 | bytes 9043968 | tf_op jit(solution)/shard_map/dot_general | solution.py:27
  43.6 0.0 copy-start
  43.6 0.0 copy-start.1
  43.6 0.0 reduce-scatter.3.cloned.1.call-update
  43.6 0.0 all-gather.8.cloned.1.call-start
  43.7 35.4 %reduce-scatter.3.cloned.1.call-done = bf16[96,2048]{1,0:T(8,128)(2,1)} async-done(((bf16[384,2048]{1,0:T(8,128)(2,1)}), bf16[96,2048]{1,0:T(8,128)(2,1)}) %reduce-scatter.3.cloned.1.call-update) | async-done | bytes 393232 | tf_op jit(solution)/shard_map/reduce_scatter | solution.py:34
  79.1 0.0 copy-done
  79.1 0.0 copy-done.1
  79.1 2.4 fusion.7
  81.5 0.0 all-gather.8.cloned.1.call-update
  81.6 0.0 all-gather.10.cloned.1.call-start
  81.6 0.5 all-gather.10.cloned.1.call-update
  82.1 0.0 all-gather.12.cloned.1.call-start
  82.2 0.5 all-gather.12.cloned.1.call-update
  82.7 0.0 all-gather.14.cloned.1.call-start
  82.8 0.5 all-gather.14.cloned.1.call-update
  83.3 0.2 reduce-scatter.5.cloned.1.call-start
  83.5 34.2 %all-gather.8.cloned.1.call-done = bf16[384,2048]{1,0:T(8,128)(2,1)} async-done(((bf16[96,2048]{1,0:T(8,128)(2,1)}), bf16[384,2048]{1,0:T(8,128)(2,1)}) %all-gather.8.cloned.1.call-update) | async-done | bytes 1572880 | tf_op jit(solution)/shard_map/all_gather | solution.py:43
  117.8 7.3 %fusion.12 = f32[384,1536]{1,0:T(8,128)} fusion(bf16[384,2048]{1,0:T(8,128)(2,1)} %all-gather.8.cloned.1.call-done, bf16[1536,2048]{1,0:T(8,128)(2,1)} %param.11), kind=kOutput, calls=%fused_computation.23 | convolution fusion | flops 2415919104 | bytes 10223616 | tf_op jit(solution)/shard_map/dot_general | solution.py:27
  125.1 0.0 copy-start.2
  125.1 30.7 %all-gather.10.cloned.1.call-done = bf16[384,2048]{1,0:T(8,128)(2,1)} async-done(((bf16[96,2048]{1,0:T(8,128)(2,1)}), bf16[384,2048]{1,0:T(8,128)(2,1)}) %all-gather.10.cloned.1.call-update) | async-done | bytes 1572880 | tf_op jit(solution)/shard_map/all_gather | solution.py:44
  155.8 7.6 %fusion.2 = bf16[384,1536]{1,0:T(8,128)(2,1)} fusion(f32[384,1536]{1,0:T(8,128)} %fusion.12, bf16[384,2048]{1,0:T(8,128)(2,1)} %all-gather.10.cloned.1.call-done, bf16[1536,2048]{1,0:T(8,128)(2,1)} %param.12), kind=kOutput, calls=%fused_computation.6 | convolution fusion | flops 2417098752 | bytes 11403264 | tf_op jit(solution)/shard_map/dot_general | solution.py:27
  163.4 0.0 reduce-scatter.5.cloned.1.call-update
  163.4 17.1 %all-gather.12.cloned.1.call-done = bf16[384,1536]{1,0:T(8,128)(2,1)} async-done(((bf16[48,1536]{1,0:T(8,128)(2,1)}), bf16[384,1536]{1,0:T(8,128)(2,1)}) %all-gather.12.cloned.1.call-update) | async-done | bytes 1179664 | tf_op jit(solution)/shard_map/all_gather | solution.py:46
  180.4 0.0 copy-done.2
  180.4 6.6 %fusion = bf16[1536,2048]{0,1:T(8,128)(2,1)} fusion(bf16[384,2048]{1,0:T(8,128)(2,1)S(1)} %copy-done.2, bf16[384,1536]{1,0:T(8,128)(2,1)} %all-gather.12.cloned.1.call-done), kind=kOutput, calls=%fused_computation.3 | convolution fusion | flops 2419064832 | bytes 9043968 | tf_op jit(solution)/shard_map/dot_general | solution.py:21
  187.1 0.0 copy-start.3
  187.1 0.0 copy-start.5
  187.1 8.8 %copy.11 = bf16[1536,2048]{1,0:T(8,128)(2,1)} copy(bf16[1536,2048]{0,1:T(8,128)(2,1)} %fusion) | data formatting | bytes 12582912
  195.9 0.0 copy-done.3
  195.9 0.0 copy-done.5
  195.9 5.4 %fusion.1 = bf16[1536,2048]{0,1:T(8,128)(2,1)} fusion(bf16[384,2048]{1,0:T(8,128)(2,1)S(1)} %copy-done.3, bf16[384,1536]{1,0:T(8,128)(2,1)S(1)} %copy-done.5), kind=kOutput, calls=%fused_computation.4 | convolution fusion | flops 2419064832 | bytes 9043968 | tf_op jit(solution)/shard_map/dot_general | solution.py:21
  201.2 0.0 copy-start.4
  201.2 8.7 %copy.12 = bf16[1536,2048]{1,0:T(8,128)(2,1)} copy(bf16[1536,2048]{0,1:T(8,128)(2,1)} %fusion.1) | data formatting | bytes 12582912
  210.0 9.0 %all-gather.14.cloned.1.call-done = bf16[384,2048]{1,0:T(8,128)(2,1)} async-done(((bf16[96,2048]{1,0:T(8,128)(2,1)}), bf16[384,2048]{1,0:T(8,128)(2,1)}) %all-gather.14.cloned.1.call-update) | async-done | bytes 1572880 | tf_op jit(solution)/shard_map/all_gather | solution.py:42
  219.0 0.0 copy-done.4
  219.0 6.8 %convolution_convert_fusion = bf16[2048,1536]{1,0:T(8,128)(2,1)} fusion(bf16[384,2048]{1,0:T(8,128)(2,1)} %all-gather.14.cloned.1.call-done, bf16[384,1536]{1,0:T(8,128)(2,1)S(1)} %copy-done.4), kind=kOutput, calls=%fused_computation | convolution fusion | flops 2419064832 | bytes 9043968 | tf_op jit(solution)/shard_map/dot_general | solution.py:21
  225.8 32.7 %reduce-scatter.5.cloned.1.call-done = bf16[48,1536]{1,0:T(8,128)(2,1)} async-done(((bf16[384,1536]{1,0:T(8,128)(2,1)}), bf16[48,1536]{1,0:T(8,128)(2,1)}) %reduce-scatter.5.cloned.1.call-update) | async-done | bytes 147472 | tf_op jit(solution)/shard_map/reduce_scatter | solution.py:50
Async XLA Ops:
  7.2 29.5 %all-gather.6.cloned.1.call-start = ((), (), s32[]{:S(2)}) async-start(), calls=%async_computation.2 | async-start | bytes 1327104 | tf_op jit(solution)/shard_map/all_gather | solution.py:33
  7.9 71.2 %reduce-scatter.3.cloned.1.call-start = ((), (), s32[]{:S(2)}) async-start(), calls=%async_computation.3 | async-start | bytes 1966080 | tf_op jit(solution)/shard_map/reduce_scatter | solution.py:34
  43.6 35.5 %copy-start = (bf16[96,2048]{1,0:T(8,128)(2,1)S(1)}, bf16[96,2048]{1,0:T(8,128)(2,1)}, u32[]{:S(2)}) copy-start(bf16[96,2048]{1,0:T(8,128)(2,1)} %param.10) | copy-start | bytes 1179652
  43.6 35.5 %copy-start.1 = (bf16[96,2048]{1,0:T(8,128)(2,1)S(1)}, bf16[96,2048]{1,0:T(8,128)(2,1)}, u32[]{:S(2)}) copy-start(bf16[96,2048]{1,0:T(8,128)(2,1)} %param.9) | copy-start | bytes 1179652
  43.6 74.1 %all-gather.8.cloned.1.call-start = ((), (), s32[]{:S(2)}) async-start(), calls=%async_computation.4 | async-start | bytes 1966080 | tf_op jit(solution)/shard_map/all_gather | solution.py:43
  81.6 74.2 %all-gather.10.cloned.1.call-start = ((), (), s32[]{:S(2)}) async-start(), calls=%async_computation.5 | async-start | bytes 1966080 | tf_op jit(solution)/shard_map/all_gather | solution.py:44
  82.1 98.3 %all-gather.12.cloned.1.call-start = ((), (), s32[]{:S(2)}) async-start(), calls=%async_computation.7 | async-start | bytes 1327104 | tf_op jit(solution)/shard_map/all_gather | solution.py:46
  82.7 136.3 %all-gather.14.cloned.1.call-start = ((), (), s32[]{:S(2)}) async-start(), calls=%async_computation.8 | async-start | bytes 1966080 | tf_op jit(solution)/shard_map/all_gather | solution.py:42
  83.3 175.2 %reduce-scatter.5.cloned.1.call-start = ((), (), s32[]{:S(2)}) async-start(), calls=%async_computation.6 | async-start | bytes 1327104 | tf_op jit(solution)/shard_map/reduce_scatter | solution.py:50
  125.1 55.4 %copy-start.2 = (bf16[384,2048]{1,0:T(8,128)(2,1)S(1)}, bf16[384,2048]{1,0:T(8,128)(2,1)}, u32[]{:S(2)}) copy-start(bf16[384,2048]{1,0:T(8,128)(2,1)} %all-gather.8.cloned.1.call-done) | copy-start | bytes 4718596
  187.1 8.8 %copy-start.3 = (bf16[384,2048]{1,0:T(8,128)(2,1)S(1)}, bf16[384,2048]{1,0:T(8,128)(2,1)}, u32[]{:S(2)}) copy-start(bf16[384,2048]{1,0:T(8,128)(2,1)} %all-gather.10.cloned.1.call-done) | copy-start | bytes 4718596
  187.1 8.8 %copy-start.5 = (bf16[384,1536]{1,0:T(8,128)(2,1)S(1)}, bf16[384,1536]{1,0:T(8,128)(2,1)}, u32[]{:S(2)}) copy-start(bf16[384,1536]{1,0:T(8,128)(2,1)} %all-gather.12.cloned.1.call-done) | copy-start | bytes 3538948
  201.2 17.8 %copy-start.4 = (bf16[384,1536]{1,0:T(8,128)(2,1)S(1)}, bf16[384,1536]{1,0:T(8,128)(2,1)}, u32[]{:S(2)}) copy-start(bf16[384,1536]{1,0:T(8,128)(2,1)} %all-gather.6.cloned.1.call-done) | copy-start | bytes 3538948
Sparse Core Ops, SparseCore 0:
  9.9 26.7 all-gather.5
  43.8 35.2 reduce-scatter.2
  81.7 36.0 all-gather.7
  119.8 35.9 all-gather.9
  157.5 22.9 all-gather.11
  181.9 37.0 all-gather.13
  222.8 35.6 reduce-scatter.4
where the time goes:
time: 266 us; the launch traced here: 265 us
  waiting for transfers between devices  190 us (71%)
  matrix products  40.6 us (15%)
  local copies, waits for them, and re-layouts  17.5 us (7%)
  between operations  14.1 us (5%)
    reduce_scatter x1, waiting for transfers between devices, on_device(): lax.psum_scatter(over_columns(cotangent_all, down_weight).astype(jnp.bflo...  35.4 us
    all_gather x1, waiting for transfers between devices, on_device(): lax.all_gather(gate_delta, 'row', axis=0, tiled=True)  34.2 us
    reduce_scatter x1, waiting for transfers between devices, on_device(): lax.psum_scatter((over_columns(gate_all, gate_weight) + over_columns(up_a...  32.7 us
    all_gather x1, waiting for transfers between devices, on_device(): lax.all_gather(up_delta, 'row', axis=0, tiled=True)  30.7 us
    all_gather x1, waiting for transfers between devices, on_device(): cotangent_all = lax.all_gather(cotangent, 'col', axis=0, tiled=True)  28.7 us
    dot_general x3, matrix products, over_columns(): lax.dot_general(left, right, (((1,), (1,)), ((), ())), preferred_element_...  21.8 us
    dot_general x3, matrix products, over_tokens(): lax.dot_general(left, right, (((0,), (0,)), ((), ())), preferred_element_...  18.7 us
    unnamed x14, local copies, waits for them, and re-layouts  17.5 us
  transfers between devices with their start and end apart: 7, of which 7 were waited for; matrix products, arithmetic and copies ran while one was open for 19% of the time, Pallas kernels for 0%

commit v1 on v0

v1 whole, which is shorter than its diff:
```python
import functools

import jax
import jax.numpy as jnp
from jax import lax
from jax.experimental import pallas as pl
from jax.experimental.pallas import tpu as pltpu
from jax.sharding import PartitionSpec as P

F32 = jnp.float32
BF16 = jnp.bfloat16
MIB = 1024 * 1024
NO_COST = pl.CostEstimate(flops=0, bytes_accessed=0, transcendentals=0)
CHUNKS = 4


def contract(left, right, left_dim, right_dim):
    return lax.dot_general(
        left, right, (((left_dim,), (right_dim,)), ((), ())), preferred_element_type=F32
    )


def whole(shape):
    return pl.BlockSpec(shape, lambda *_: (0,) * len(shape))


def tile_of(size, most):
    tile = min(size, most)
    while size % tile:
        tile //= 2
    return tile


def after(value, *others):
    return lax.optimization_barrier((value, *others))[0]


def inward(places, n):
    return [pair for p in places for pair in ((p, p + 1), (n - 1 - p, n - 2 - p))]


def outward(places, n):
    return [(target, source) for source, target in inward(places, n)]


def across(n):
    return [(n // 2 - 1, n // 2), (n // 2, n // 2 - 1)]


def own_half(block, n):
    half = n // 2
    ins, outs = [block], [block]
    for step in range(1, half):
        if half == 2:
            met = lax.ppermute(block, "row", inward([0], n) + outward([0], n))
            ins.append(met)
            outs.append(met)
        else:
            ins.append(lax.ppermute(ins[-1], "row", inward(range(step - 1, half - 1), n)))
            outs.append(lax.ppermute(outs[-1], "row", outward(range(half - step), n)))
    return ins, outs


def sent_out(block, place, n):
    got = block
    for step in reversed(range(n // 2 - 1)):
        if step < n // 2 - 2:
            block = jnp.where(place == step + 1, got, block)
        got = lax.ppermute(block, "row", outward([step], n))
    return block, got


def cube_bits(n):
    bits, bit = [], 1
    while bit < n:
        bits.append(bit)
        bit *= 2
    return bits


def cube_gather(block, n):
    pieces = {0: block}
    for bit in reversed(cube_bits(n)):
        pairs = [(i, i ^ bit) for i in range(n)]
        for slot in list(pieces):
            pieces[slot | bit] = lax.ppermute(pieces[slot], "col", pairs)
    return [pieces[k] for k in range(n)]


def rows_at(start, rows):
    return pl.ds(pl.multiple_of(start, 16), rows)


def spread(pieces, col, which, target):
    for slot, piece in enumerate(pieces):
        rows = piece.shape[0] // 2
        block = piece[which * rows : (which + 1) * rows, :]
        target[rows_at(jnp.bitwise_xor(col, slot) * rows, rows), :] = block


def in_hbm(array):
    return pltpu.with_memory_space_constraint(array, pltpu.HBM)


def join_kernel(*refs):
    arrived = refs[-1]
    count = len(refs) // 3
    copies = []
    for number, block in enumerate(refs[: 2 * count]):
        rows = block.shape[0]
        target = refs[2 * count + number // 2].at[pl.ds(number % 2 * rows, rows)]
        copies.append(pltpu.make_async_copy(block, target, arrived.at[number]))
    for copy in copies:
        copy.start()
    for copy in copies:
        copy.wait()


def joined(*pairs):
    blocks = [in_hbm(block) for pair in pairs for block in pair]
    return pl.pallas_call(
        join_kernel,
        in_specs=[pl.BlockSpec(memory_space=pl.ANY)] * len(blocks),
        out_specs=[pl.BlockSpec(memory_space=pltpu.VMEM)] * len(pairs),
        out_shape=[
            jax.ShapeDtypeStruct((2 * first.shape[0], first.shape[1]), first.dtype)
            for first, _ in pairs
        ],
        scratch_shapes=[pltpu.SemaphoreType.DMA((len(blocks),))],
        compiler_params=pltpu.CompilerParams(vmem_limit_bytes=16 * MIB),
        cost_estimate=pl.CostEstimate(
            flops=0,
            bytes_accessed=sum(8 * first.size for first, _ in pairs),
            transcendentals=0,
        ),
        name="join",
    )(*blocks)


def transpose_kernel(n_col, ids, *refs):
    pieces, (out, held) = refs[:n_col], refs[n_col:]
    spread(pieces, ids[1], 1, held)
    out[...] = held[...].T


def transpose(ids, pieces):
    n_col = len(pieces)
    rows, depth = pieces[0].shape
    total = rows // 2 * n_col
    return pl.pallas_call(
        functools.partial(transpose_kernel, n_col),
        grid_spec=pltpu.PrefetchScalarGridSpec(
            num_scalar_prefetch=1,
            grid=(1,),
            in_specs=[whole((rows, depth))] * n_col,
            out_specs=whole((depth, total)),
            scratch_shapes=[pltpu.VMEM((total, depth), BF16)],
        ),
        out_shape=jax.ShapeDtypeStruct((depth, total), BF16),
        compiler_params=pltpu.CompilerParams(vmem_limit_bytes=16 * MIB),
        cost_estimate=pl.CostEstimate(
            flops=0, bytes_accessed=4 * total * depth, transcendentals=0
        ),
        name="inputs_transposed",
    )(ids, *pieces)


def partial_kernel(n_pieces, ids, *refs):
    pieces, weight, refs = refs[:n_pieces], refs[n_pieces], refs[n_pieces + 1 :]
    if n_pieces > 1:
        *outs, tokens = refs

        @pl.when(pl.program_id(0) == 0)
        def _():
            spread(pieces, ids[1], 0, tokens)
    else:
        tokens, outs = pieces[0], refs
    term = contract(tokens[...], weight[...], 1, 1).astype(BF16)
    for number, out in enumerate(outs):

        @pl.when(pl.program_id(0) == number)
        def _():
            out[...] = term


def partials(ids, pieces, weight, first, count):
    rows, depth = pieces[0].shape
    total = rows * len(pieces) // (2 if len(pieces) > 1 else 1)
    units = weight.shape[0] // CHUNKS
    shapes = [(total, units)] * count
    if len(pieces) > 1:
        shapes.append((total, depth))
    return pl.pallas_call(
        functools.partial(partial_kernel, len(pieces)),
        grid_spec=pltpu.PrefetchScalarGridSpec(
            num_scalar_prefetch=1,
            grid=(count,),
            in_specs=[whole((rows, depth))] * len(pieces)
            + [pl.BlockSpec((units, depth), lambda j, *_: (first + j, 0))],
            out_specs=[whole(shape) for shape in shapes],
        ),
        out_shape=[jax.ShapeDtypeStruct(shape, BF16) for shape in shapes],
        compiler_params=pltpu.CompilerParams(vmem_limit_bytes=16 * MIB),
        cost_estimate=pl.CostEstimate(
            flops=2 * total * depth * units * count,
            bytes_accessed=2 * (units * depth * count + total * units * count + total * depth),
            transcendentals=0,
        ),
        name="hidden_grad_partials",
    )(ids, *pieces, in_hbm(weight))


def filled(before):
    before = list(before or [])
    return before, [pl.BlockSpec(memory_space=pl.ANY)] * len(before)


def row_blocks(me, n):
    half = n // 2
    left = me < half
    place = jnp.where(left, me, n - 1 - me)
    near = [lax.rem(place + step, half) for step in range(half)]
    near = [jnp.where(left, at, n - 1 - at) for at in near]
    far = [jnp.where(left, n - 1 - at, at) for at in reversed(range(half))]
    return near + far


def factor_kernel(n, count, ids, *refs):
    sources, outs = refs[:-3], refs[-3:]
    sources = list(sources)
    rows = sources[0].shape[0] // 2
    half = n // 2
    place = jnp.where(ids[0] < half, ids[0], n - 1 - ids[0])
    for number, inner in enumerate(count):
        block = sources.pop(0)[...]
        if inner is not None:
            block = jnp.where(place >= inner[0], block, sources.pop(0)[...])
        gate = block[:rows].astype(F32)
        up = block[rows:].astype(F32)
        sigma = 1.0 / (1.0 + jnp.exp(-gate))
        silu = gate * sigma
        part = pl.ds(number * rows, rows)
        outs[0][part, :] = (up * sigma * (1.0 + gate * (1.0 - sigma))).astype(BF16)
        outs[1][part, :] = silu.astype(BF16)
        outs[2][part, :] = (silu * up).astype(BF16)


def factors_of(ids, sources, n):
    operands, count = [], []
    for source in sources:
        if isinstance(source, tuple):
            inner, block, other = source
            operands += [block, other]
            count.append((inner,))
        else:
            operands.append(source)
            count.append(None)
    rows, width = operands[0].shape
    rows = rows // 2 * len(sources)
    tile = tile_of(width, 512)
    out = pl.BlockSpec((rows, tile), lambda j, *_: (0, j))
    return pl.pallas_call(
        functools.partial(factor_kernel, n, count),
        grid_spec=pltpu.PrefetchScalarGridSpec(
            num_scalar_prefetch=1,
            grid=(width // tile,),
            in_specs=[pl.BlockSpec((operands[0].shape[0], tile), lambda j, *_: (0, j))]
            * len(operands),
            out_specs=[out] * 3,
        ),
        out_shape=[jax.ShapeDtypeStruct((rows, width), BF16)] * 3,
        compiler_params=pltpu.CompilerParams(vmem_limit_bytes=16 * MIB),
        cost_estimate=pl.CostEstimate(
            flops=10 * rows * width,
            bytes_accessed=4 * rows * width + 6 * rows * width,
            transcendentals=rows * width,
        ),
        name="factors",
    )(ids, *operands)


def down_kernel(n, ids, early, late, cotangent, out, hidden):
    rows = late.shape[0]
    for number, block in enumerate(row_blocks(ids[0], n)):
        source = late if number == n - 1 else early
        part = pl.ds(0 if number == n - 1 else number * rows, rows)
        hidden[rows_at(block * rows, rows), :] = source[part, :]
    out[...] = contract(hidden[...], cotangent[...], 0, 0).astype(BF16)


def down_grads(ids, early, late, cotangent, n):
    total, depth = cotangent.shape
    width = late.shape[1]
    tile = tile_of(width, 512)
    return pl.pallas_call(
        functools.partial(down_kernel, n),
        grid_spec=pltpu.PrefetchScalarGridSpec(
            num_scalar_prefetch=1,
            grid=(width // tile,),
            in_specs=[
                pl.BlockSpec((early.shape[0], tile), lambda j, *_: (0, j)),
                pl.BlockSpec((late.shape[0], tile), lambda j, *_: (0, j)),
                whole((total, depth)),
            ],
            out_specs=pl.BlockSpec((tile, depth), lambda j, *_: (j, 0)),
            scratch_shapes=[pltpu.VMEM((total, tile), BF16)],
        ),
        out_shape=jax.ShapeDtypeStruct((width, depth), BF16),
        compiler_params=pltpu.CompilerParams(vmem_limit_bytes=20 * MIB),
        cost_estimate=pl.CostEstimate(
            flops=2 * total * depth * width,
            bytes_accessed=2 * (width * depth + total * depth + total * width),
            transcendentals=0,
        ),
        name="down_grad",
    )(ids, early, late, cotangent)


def delta_kernel(n, n_col, first, last, ids, *refs):
    middle, got, *factors, gate_weight, up_weight = refs[:8]
    refs = list(refs[8:])
    before = None if first else refs.pop(0)
    gate_out, up_out = refs[:2]

    @pl.when(pl.program_id(0) == 0)
    def _():
        outer = jnp.logical_or(ids[0] == 0, ids[0] == n - 1)
        rows = middle.shape[0] // n
        for number, block in enumerate(row_blocks(ids[0], n)):
            part = rows_at(block * rows, rows)
            grad = jnp.where(outer, got[part, :], middle[part, :]).astype(F32)
            late = number == n - 1
            source = pl.ds(0 if late else number * rows, rows)
            gate_factor, up_factor = factors[2:] if late else factors[:2]
            gate_out[part, :] = (grad * gate_factor[source, :].astype(F32)).astype(BF16)
            up_out[part, :] = (grad * up_factor[source, :].astype(F32)).astype(BF16)

    term = contract(gate_out[...], gate_weight[...], 1, 1) + contract(
        up_out[...], up_weight[...], 1, 1
    )
    if not first:
        term += before[...]
    if not last:
        refs[2][...] = term
        return
    keep, send, result = refs[2:]
    result[...] = term
    rows = keep.shape[1]
    for slot in range(n_col):
        out = send if slot % 2 else keep
        start = jnp.bitwise_xor(ids[1], slot) * rows
        out[slot // 2] = result[rows_at(start, rows), :].astype(BF16)


def deltas(ids, grads, factors, weights, n, n_col, chunk, before):
    total, units = grads[0].shape
    depth = weights[0].shape[0]
    rows = total // n_col
    tile = tile_of(depth, 512)
    tall = whole((total, units))
    wide = pl.BlockSpec((tile, units), lambda j, *_: (j, chunk))
    running = pl.BlockSpec((total, tile), lambda j, *_: (0, j))
    delta_shape = jax.ShapeDtypeStruct((total, units), BF16)
    last = chunk == CHUNKS - 1
    if last:
        half = pl.BlockSpec((n_col // 2, rows, tile), lambda j, *_: (0, 0, j))
        out_specs = [half, half]
        out_shape = [jax.ShapeDtypeStruct((n_col // 2, rows, depth), BF16)] * 2
        scratch = [pltpu.VMEM((total, tile), F32)]
    else:
        out_specs, scratch = [running], []
        out_shape = [jax.ShapeDtypeStruct((total, depth), F32)]
    more = [] if before is None else [before]
    factor_specs = [
        pl.BlockSpec((factor.shape[0], units), lambda j, *_: (0, chunk)) for factor in factors
    ]
    return pl.pallas_call(
        functools.partial(delta_kernel, n, n_col, before is None, last),
        grid_spec=pltpu.PrefetchScalarGridSpec(
            num_scalar_prefetch=1,
            grid=(depth // tile,),
            in_specs=[tall] * 2 + factor_specs + [wide] * 2 + [running] * len(more),
            out_specs=[tall, tall] + out_specs,
            scratch_shapes=scratch,
        ),
        out_shape=[delta_shape, delta_shape] + out_shape,
        compiler_params=pltpu.CompilerParams(vmem_limit_bytes=28 * MIB),
        cost_estimate=NO_COST,
        name="deltas_and_input_grad",
    )(ids, *grads, *factors, *weights, *more)


def weight_grad_kernel(inputs, gate_delta, up_delta, *refs):
    gate_out, up_out = refs[-2:]
    gate_out[...] = contract(inputs[...], gate_delta[...], 1, 0).astype(BF16)
    up_out[...] = contract(inputs[...], up_delta[...], 1, 0).astype(BF16)


def weight_grads(inputs_t, gate_delta, up_delta, chunk, before):
    depth, total = inputs_t.shape
    units = gate_delta.shape[1]
    tile = tile_of(depth, 512)
    more, more_specs = filled(before)
    out = pl.BlockSpec((tile, units), lambda j: (j, chunk))
    cost = NO_COST
    if chunk == CHUNKS - 1:
        cost = pl.CostEstimate(
            flops=4 * total * depth * units,
            bytes_accessed=4 * units * depth + 4 * total * units + 2 * total * depth,
            transcendentals=0,
        )
    return pl.pallas_call(
        weight_grad_kernel,
        grid=(depth // tile,),
        in_specs=[pl.BlockSpec((tile, total), lambda j: (j, 0))]
        + [whole((total, units))] * 2
        + more_specs,
        out_specs=[out, out],
        out_shape=[jax.ShapeDtypeStruct((depth, units * CHUNKS), BF16)] * 2,
        input_output_aliases={3: 0, 4: 1} if more else {},
        compiler_params=pltpu.CompilerParams(vmem_limit_bytes=16 * MIB),
        cost_estimate=cost,
        name="gate_and_up_grad",
    )(inputs_t, gate_delta, up_delta, *more)


def add(left, right):
    return (left.astype(F32) + right.astype(F32)).astype(BF16)


def on_device(
    n_row, n_col, inputs, cotangent, gate_pre, up_pre, gate_weight, up_weight, down_weight
):
    me = lax.axis_index("row")
    ids = jnp.stack([me, lax.axis_index("col")]).astype(jnp.int32)
    half = n_row // 2
    place = jnp.where(me < half, me, n_row - 1 - me)

    pre, token_block = joined((gate_pre, up_pre), (cotangent, inputs))
    ins, outs = own_half(pre, n_row)
    sources = [pre]
    for step in range(1, half):
        sources.append(outs[step] if half == 2 else (half - step, ins[half - step], outs[step]))
    far = [lax.ppermute(block, "row", across(n_row)) for block in ins]
    away = [sent_out(block, place, n_row) for block in far]
    sources += [(1, *pair) for pair in away]

    pieces = cube_gather(token_block, n_col)
    term, tokens = partials(ids, pieces, down_weight, 0, 1)
    tokens = after(tokens, ins[-1], far[0])
    terms = [term, *partials(ids, [tokens], down_weight, 1, CHUNKS - 1)]
    inputs_t = transpose(ids, pieces)

    early = factors_of(ids, sources[:-1], n_row)
    late = factors_of(ids, sources[-1:], n_row)
    factors = [*early[:2], *late[:2]]
    before = {0: early, 2: late}
    running = weight_out = met = None
    sent = []

    def work_on(chunk, running, weight_out):
        gate_delta, up_delta, *running = deltas(
            ids,
            sent[chunk],
            factors,
            (gate_weight, up_weight),
            n_row,
            n_col,
            chunk,
            running,
        )
        weight_out = weight_grads(inputs_t, gate_delta, up_delta, chunk, weight_out)
        if chunk == CHUNKS - 1:
            return running, weight_out
        running, *weight_out = lax.optimization_barrier((running[0], *weight_out))
        return running, weight_out

    for chunk, held in enumerate(terms):
        for step in range(half - 1):
            if met is not None:
                held = after(held, met)
            got = met = lax.ppermute(held, "row", inward([step], n_row))
            if chunk == 0:
                got = after(got, terms[-1], far[-1], away[0][1], inputs_t)
            held = add(held, got)
        got = lax.ppermute(held, "row", across(n_row))
        if chunk == CHUNKS - 1:
            sent[0] = (sent[0][0], after(sent[0][1], sent[2][0]))
            running, weight_out = work_on(0, None, None)
            got, running, *weight_out = lax.optimization_barrier((got, running, *weight_out))
        elif chunk in before:
            got = after(got, *before[chunk])
        held = add(held, got)
        if chunk == 1:
            held = after(held, away[-1][1])
        sent.append(sent_out(held, place, n_row))

    for chunk in range(1, CHUNKS):
        if chunk == CHUNKS - 2:
            hidden = after(late[2], running)
            down_grad = down_grads(ids, early[2], hidden, tokens, n_row)
            running, down_grad = lax.optimization_barrier((running, down_grad))
        running, weight_out = work_on(chunk, running, weight_out)
    gate_grad, up_grad = weight_out
    keep, send = running

    keep = add(keep, lax.ppermute(send, "col", [(i, i ^ 1) for i in range(n_col)]))
    input_grad = keep[0].astype(F32)
    for number in range(1, n_col // 2):
        pairs = [(i, i ^ (2 * number)) for i in range(n_col)]
        input_grad += lax.ppermute(keep[number], "col", pairs).astype(F32)
    input_grad = input_grad.astype(BF16)
    return (input_grad, gate_grad, up_grad, down_grad)


def solution(mesh):
    placed = (
        P("col", "row"),
        P("col", "row"),
        P("row", "col"),
        P("row", "col"),
        P("row", "col"),
        P("row", "col"),
        P("col", "row"),
    )
    return jax.shard_map(
        functools.partial(on_device, mesh.shape["row"], mesh.shape["col"]),
        mesh=mesh,
        in_specs=placed,
        out_specs=(P("col", "row"), P("row", "col"), P("row", "col"), P("col", "row")),
        check_vma=False,
    )
```

time: 266 us -> 138 us (0.52)
  waiting for transfers between devices: 190 us -> 37 us
  starting transfers between devices: 0.45 us -> 50 us
  Pallas kernels: 0 us -> 47 us
  matrix products: 40.6 us -> 0 us
  local copies, waits for them, and re-layouts: 17.5 us -> 0.95 us
  between operations: 14.1 us -> 1.03 us
    all_gather x5 -> x0, waiting for transfers between devices: 120 us -> none  [the longest x1 34.2 us: on_device(): lax.all_gather(gate_delta, 'row', axis=0, tiled=True)]
    reduce_scatter x2 -> x0, waiting for transfers between devices: 68.1 us -> none  [the longest x1 35.4 us: on_device(): lax.psum_scatter(over_columns(cotangent_all, down_weight).astype(jnp.bflo...]
    ppermute x0 -> x28, starting transfers between devices: none -> 50 us  [the longest x4 23.1 us: on_device(): got = met = lax.ppermute(held, 'row', inward([step], n_row))]
    pallas_call x0 -> x15, Pallas kernels: none -> 47 us  [the longest x4 12.9 us: deltas(): pl.pallas_call(functools.partial(delta_kernel, n, n_col, before is None,...]
    dot_general x6 -> x0, matrix products: 40.6 us -> none  [the longest x3 21.8 us: over_columns(): lax.dot_general(left, right, (((1,), (1,)), ((), ())), preferred_element_...]
    ppermute x0 -> x28, waiting for transfers between devices: none -> 37 us  [the longest x4 12.6 us: on_device(): got = met = lax.ppermute(held, 'row', inward([step], n_row))]
    unnamed x14 -> x12, local copies, waits for them, and re-layouts: 17.5 us -> 0.92 us
  transfers between devices with their start and end apart: 7 -> 28, of which waited for: 7 -> 13; matrix products, arithmetic and copies ran while one was open for 19% -> 1% of each run, Pallas kernels for 0% -> 31%
where the time goes in v1:
time: 138 us
  starting transfers between devices  50 us (36%)
  Pallas kernels  47 us (34%)
  waiting for transfers between devices  37 us (27%)
  other arithmetic  1.77 us (1%)
    ppermute x4, starting transfers between devices, on_device(): got = met = lax.ppermute(held, 'row', inward([step], n_row))  23.1 us
    pallas_call x4, Pallas kernels, deltas(): pl.pallas_call(functools.partial(delta_kernel, n, n_col, before is None,...  12.9 us
    ppermute x4, waiting for transfers between devices, on_device(): got = met = lax.ppermute(held, 'row', inward([step], n_row))  12.6 us
    pallas_call x4, Pallas kernels, weight_grads(): pl.pallas_call(weight_grad_kernel, grid=(depth // tile,), in_specs=[pl.Bl...  12.3 us
    ppermute x7, waiting for transfers between devices, cube_gather(): pieces[slot | bit] = lax.ppermute(pieces[slot], 'col', pairs)  10.7 us
    pallas_call x2, Pallas kernels, partials(): pl.pallas_call(functools.partial(partial_kernel, len(pieces)), grid_spec=...  8.13 us
    ppermute x6, starting transfers between devices, sent_out(): got = lax.ppermute(block, 'row', outward([step], n))  7.91 us
    ppermute x6, waiting for transfers between devices, sent_out(): got = lax.ppermute(block, 'row', outward([step], n))  6.89 us
  transfers between devices with their start and end apart: 28, of which 13 were waited for; matrix products, arithmetic and copies ran while one was open for 1% of the time, Pallas kernels for 31%

profile of v1, /device:TPU:0, one launch (start us, length us, event | category | flops | bytes accessed | tf_op | source)
XLA Modules:
  0.0 137.7 jit_solution(17577434359121620464)
XLA Ops:
  0.6 1.2 join.1
  1.9 1.6 %collective-permute-start.8 = (bf16[192,2048]{1,0:T(8,128)(2,1)S(1)}, bf16[192,2048]{1,0:T(8,128)(2,1)}, u32[]{:S(2)}, u32[]{:S(2)}) collective-permute-start(bf16[192,2048]{1,0:T(8,128)(2,1)S(1)} %get-tuple-element.65.refs_0_), channel_id=1, source_target_pairs={{8,16},{16,8},{9,17},{17,9},{10,18},{18,10},{11,19},{19,11},{12,20... | collective-permute-start | bytes 2359304 | tf_op jit(solution)/shard_map/ppermute | solution.py:444
  3.4 5.0 %collective-permute-start.7 = (bf16[192,2048]{1,0:T(8,128)(2,1)S(1)}, bf16[192,2048]{1,0:T(8,128)(2,1)}, u32[]{:S(2)}, u32[]{:S(2)}) collective-permute-start(bf16[192,2048]{1,0:T(8,128)(2,1)S(1)} %get-tuple-element.65.refs_0_), channel_id=1, source_target_pairs={{0,8},{24,16},{8,0},{16,24},{1,9},{25,17},{9,1},{17,25},{2,10},{26... | collective-permute-start | bytes 2359304 | tf_op jit(solution)/shard_map/ppermute | solution.py:55
  8.5 0.9 copy-done
  9.3 1.5 %collective-permute-start.3 = (bf16[96,1536]{1,0:T(8,128)(2,1)S(1)}, bf16[96,1536]{1,0:T(8,128)(2,1)S(1)}, u32[]{:S(2)}, u32[]{:S(2)}) collective-permute-start(bf16[96,1536]{1,0:T(8,128)(2,1)S(1)} %get-tuple-element.63.refs_0_), channel_id=1, source_target_pairs={{0,4},{1,5},{2,6},{3,7},{4,0},{5,1},{6,2},{7,3},{8,12},{9,13},{10,... | collective-permute-start | bytes 884744 | tf_op jit(solution)/shard_map/ppermute | solution.py:86
  10.8 1.5 %collective-permute-start.1 = (bf16[96,1536]{1,0:T(8,128)(2,1)S(1)}, bf16[96,1536]{1,0:T(8,128)(2,1)S(1)}, u32[]{:S(2)}, u32[]{:S(2)}) collective-permute-start(bf16[96,1536]{1,0:T(8,128)(2,1)S(1)} %get-tuple-element.63.refs_0_), channel_id=1, source_target_pairs={{0,2},{1,3},{2,0},{3,1},{4,6},{5,7},{6,4},{7,5},{8,10},{9,11},{10,... | collective-permute-start | bytes 884744 | tf_op jit(solution)/shard_map/ppermute | solution.py:86
  12.3 5.2 %collective-permute-done.3.refs_4_ = bf16[96,1536]{1,0:T(8,128)(2,1)S(1)} collective-permute-done((bf16[96,1536]{1,0:T(8,128)(2,1)S(1)}, bf16[96,1536]{1,0:T(8,128)(2,1)S(1)}, u32[]{:S(2)}, u32[]{:S(2)}) %collective-permute-start.3) | collective-permute-done | bytes 294944 | tf_op jit(solution)/shard_map/ppermute | solution.py:86
  17.5 1.5 %collective-permute-start.5 = (bf16[96,1536]{1,0:T(8,128)(2,1)S(1)}, bf16[96,1536]{1,0:T(8,128)(2,1)S(1)}, u32[]{:S(2)}, u32[]{:S(2)}) collective-permute-start(bf16[96,1536]{1,0:T(8,128)(2,1)S(1)} %collective-permute-done.3.refs_4_), channel_id=1, source_target_pairs={{0,2},{1,3},{2,0},{3,1},{4,6},{5,7},{6,4},{7,5},{8,10},{9,11},{10,... | collective-permute-start | bytes 884744 | tf_op jit(solution)/shard_map/ppermute | solution.py:86
  19.5 5.5 %collective-permute-done.5.refs_6_ = bf16[96,1536]{1,0:T(8,128)(2,1)S(1)} collective-permute-done((bf16[96,1536]{1,0:T(8,128)(2,1)S(1)}, bf16[96,1536]{1,0:T(8,128)(2,1)S(1)}, u32[]{:S(2)}, u32[]{:S(2)}) %collective-permute-start.5) | collective-permute-done | bytes 294944 | tf_op jit(solution)/shard_map/ppermute | solution.py:86
  25.1 1.3 collective-permute-start.15
  26.4 0.7 collective-permute-start.14
  27.2 2.8 %hidden_grad_partials.2 = (bf16[384,512]{1,0:T(8,128)(2,1)S(1)}, bf16[384,1536]{1,0:T(8,128)(2,1)S(1)}) custom-call(s32[2]{0:T(128)S(1)} %pad_add_fusion.ids, bf16[96,1536]{1,0:T(8,128)(2,1)S(1)} %get-tuple-element.63.refs_0_, bf16[96,1536]{1,0:T(8,128)(2,1)S(1)} %collective-permute-done.refs_1_, bf16[96,1536]{1,0:T(8,128)(2,1)S(1)} %collective-permute-done.1.refs_2_, ...), custom_call_target="tpu_custom_call" | custom-call | flops 603979776 | bytes 3145728 | tf_op jit(solution)/shard_map/hidden_grad_partials/pallas_call | solution.py:193
  30.0 7.2 %collective-permute-start.9 = (bf16[384,512]{1,0:T(8,128)(2,1)S(1)}, bf16[384,512]{1,0:T(8,128)(2,1)S(1)}, u32[]{:S(2)}, u32[]{:S(2)}) collective-permute-start(bf16[384,512]{1,0:T(8,128)(2,1)S(1)} %get-tuple-element.70), channel_id=1, source_target_pairs={{0,8},{24,16},{1,9},{25,17},{2,10},{26,18},{3,11},{27,19},{4,12},{... | collective-permute-start | bytes 1179656 | tf_op jit(solution)/shard_map/ppermute | solution.py:482
  37.2 5.3 %hidden_grad_partials.3 = (bf16[384,512]{1,0:T(8,128)(2,1)S(1)}, bf16[384,512]{1,0:T(8,128)(2,1)S(1)}, bf16[384,512]{1,0:T(8,128)(2,1)S(1)}) custom-call(s32[2]{0:T(128)S(1)} %pad_add_fusion.ids, bf16[384,1536]{1,0:T(8,128)(2,1)S(1)} %get-tuple-element.66.refs_0_.cotangent, bf16[2048,1536]{1,0:T(8,128)(2,1)} %refs_1_.3), custom_call_target="tpu_custom_call" | custom-call | flops 1811939328 | bytes 7077888 | tf_op jit(solution)/shard_map/hidden_grad_partials/pallas_call | solution.py:193
  42.6 3.1 %collective-permute-done.9 = bf16[384,512]{1,0:T(8,128)(2,1)S(1)} collective-permute-done((bf16[384,512]{1,0:T(8,128)(2,1)S(1)}, bf16[384,512]{1,0:T(8,128)(2,1)S(1)}, u32[]{:S(2)}, u32[]{:S(2)}) %collective-permute-start.9) | collective-permute-done | bytes 393248 | tf_op jit(solution)/shard_map/ppermute | solution.py:482
  45.7 4.4 %collective-permute-start.10 = (bf16[384,512]{1,0:T(8,128)(2,1)S(1)}, bf16[384,512]{1,0:T(8,128)(2,1)S(1)}, u32[]{:S(2)}, u32[]{:S(2)}) collective-permute-start(bf16[384,512]{1,0:T(8,128)(2,1)S(1)} %get-tuple-element.71), channel_id=1, source_target_pairs={{0,8},{24,16},{1,9},{25,17},{2,10},{26,18},{3,11},{27,19},{4,12},{... | collective-permute-start | bytes 1179656 | tf_op jit(solution)/shard_map/ppermute | solution.py:482
  50.1 1.0 inputs_transposed.1.inputs
  51.2 0.8 collective-permute-start.16
  52.0 5.6 %collective-permute-done.10 = bf16[384,512]{1,0:T(8,128)(2,1)S(1)} collective-permute-done((bf16[384,512]{1,0:T(8,128)(2,1)S(1)}, bf16[384,512]{1,0:T(8,128)(2,1)S(1)}, u32[]{:S(2)}, u32[]{:S(2)}) %collective-permute-start.10) | collective-permute-done | bytes 393248 | tf_op jit(solution)/shard_map/ppermute | solution.py:482
  57.7 4.4 %collective-permute-start.11 = (bf16[384,512]{1,0:T(8,128)(2,1)S(1)}, bf16[384,512]{1,0:T(8,128)(2,1)S(1)}, u32[]{:S(2)}, u32[]{:S(2)}) collective-permute-start(bf16[384,512]{1,0:T(8,128)(2,1)S(1)} %get-tuple-element.72), channel_id=1, source_target_pairs={{0,8},{24,16},{1,9},{25,17},{2,10},{26,18},{3,11},{27,19},{4,12},{... | collective-permute-start | bytes 1179656 | tf_op jit(solution)/shard_map/ppermute | solution.py:482
  62.1 1.3 collective-permute-start.19
  63.4 4.1 %factors.2 = (bf16[288,2048]{1,0:T(8,128)(2,1)S(1)}, bf16[288,2048]{1,0:T(8,128)(2,1)S(1)}, bf16[288,2048]{1,0:T(8,128)(2,1)S(1)}) custom-call(s32[2]{0:T(128)S(1)} %pad_add_fusion.ids, bf16[192,2048]{1,0:T(8,128)(2,1)S(1)} %copy-done.1, bf16[192,2048]{1,0:T(8,128)(2,1)} %collective-permute-done.7.refs_1_, bf16[192,2048]{1,0:T(8,128)(2,1)} %collective-permute-done.8.refs_2_, ...), custom_call_target="tpu_custom_call" | custom-call | flops 5898240 | bytes 5898240 | tf_op jit(solution)/shard_map/factors/pallas_call | solution.py:262
  67.6 0.8 collective-permute-start.22
  68.7 7.1 %collective-permute-start.12 = (bf16[384,512]{1,0:T(8,128)(2,1)S(1)}, bf16[384,512]{1,0:T(8,128)(2,1)S(1)}, u32[]{:S(2)}, u32[]{:S(2)}) collective-permute-start(bf16[384,512]{1,0:T(8,128)(2,1)S(1)} %get-tuple-element.73), channel_id=1, source_target_pairs={{0,8},{24,16},{1,9},{25,17},{2,10},{26,18},{3,11},{27,19},{4,12},{... | collective-permute-start | bytes 1179656 | tf_op jit(solution)/shard_map/ppermute | solution.py:482
  76.0 1.3 collective-permute-start.17
  78.1 3.6 %collective-permute-done.12 = bf16[384,512]{1,0:T(8,128)(2,1)S(1)} collective-permute-done((bf16[384,512]{1,0:T(8,128)(2,1)S(1)}, bf16[384,512]{1,0:T(8,128)(2,1)S(1)}, u32[]{:S(2)}, u32[]{:S(2)}) %collective-permute-start.12) | collective-permute-done | bytes 393248 | tf_op jit(solution)/shard_map/ppermute | solution.py:482
  82.6 1.8 %collective-permute-done.19.refs_1_ = bf16[192,2048]{1,0:T(8,128)(2,1)S(1)} collective-permute-done((bf16[192,2048]{1,0:T(8,128)(2,1)S(1)}, bf16[192,2048]{1,0:T(8,128)(2,1)S(1)}, u32[]{:S(2)}, u32[]{:S(2)}) %collective-permute-start.19) | collective-permute-done | bytes 786464 | tf_op jit(solution)/shard_map/ppermute | solution.py:69
  84.4 1.3 collective-permute-start.23
  85.7 1.3 factors.3
  87.2 1.3 collective-permute-start.21
  88.5 4.4 %collective-permute-done.17.refs_1_ = bf16[384,512]{1,0:T(8,128)(2,1)S(1)} collective-permute-done((bf16[384,512]{1,0:T(8,128)(2,1)S(1)}, bf16[384,512]{1,0:T(8,128)(2,1)S(1)}, u32[]{:S(2)}, u32[]{:S(2)}) %collective-permute-start.17) | collective-permute-done | bytes 393248 | tf_op jit(solution)/shard_map/ppermute | solution.py:69
  92.9 3.1 %deltas_and_input_grad.4 = (bf16[384,512]{1,0:T(8,128)(2,1)S(1)}, bf16[384,512]{1,0:T(8,128)(2,1)S(1)}, f32[384,1536]{1,0:T(8,128)S(1)}) custom-call(s32[2]{0:T(128)S(1)} %pad_add_fusion.ids, bf16[384,512]{1,0:T(8,128)(2,1)S(1)} %add_convert_fusion.6.refs_0_, bf16[384,512]{1,0:T(8,128)(2,1)S(1)} %collective-permute-done.17.refs_1_, ...), custom_call_target="tpu_custom_call" | custom-call | tf_op jit(solution)/shard_map/deltas_and_input_grad/pallas_call | solution.py:377
  96.0 3.1 %gate_and_up_grad.4 = (bf16[1536,2048]{1,0:T(8,128)(2,1)}, bf16[1536,2048]{1,0:T(8,128)(2,1)}) custom-call(bf16[1536,384]{1,0:T(8,128)(2,1)S(1)} %inputs_transposed.1.inputs, bf16[384,512]{1,0:T(8,128)(2,1)S(1)} %get-tuple-element.85.gate_delta, bf16[384,512]{1,0:T(8,128)(2,1)S(1)} %get-tuple-element.86.up_delta), custom_call_target="tpu_custom_call" | custom-call | tf_op jit(solution)/shard_map/gate_and_up_grad/pallas_call | solution.py:412
  99.2 1.5 %collective-permute-start.20 = (bf16[384,512]{1,0:T(8,128)(2,1)S(1)}, bf16[384,512]{1,0:T(8,128)(2,1)S(1)}, u32[]{:S(2)}, u32[]{:S(2)}) collective-permute-start(bf16[384,512]{1,0:T(8,128)(2,1)S(1)} %add_convert_fusion.3.refs_0_), channel_id=1, source_target_pairs={{8,0},{16,24},{9,1},{17,25},{10,2},{18,26},{11,3},{19,27},{12,4},{... | collective-permute-start | bytes 1179656 | tf_op jit(solution)/shard_map/ppermute | solution.py:69
  101.3 3.3 %deltas_and_input_grad.5 = (bf16[384,512]{1,0:T(8,128)(2,1)S(1)}, bf16[384,512]{1,0:T(8,128)(2,1)S(1)}, f32[384,1536]{1,0:T(8,128)S(1)}) custom-call(s32[2]{0:T(128)S(1)} %pad_add_fusion.ids, bf16[384,512]{1,0:T(8,128)(2,1)S(1)} %add_convert_fusion.1.refs_0_, bf16[384,512]{1,0:T(8,128)(2,1)S(1)} %collective-permute-done.23.refs_1_, ...), custom_call_target="tpu_custom_call" | custom-call | tf_op jit(solution)/shard_map/deltas_and_input_grad/pallas_call | solution.py:377
  104.6 3.1 %gate_and_up_grad.5 = (bf16[1536,2048]{1,0:T(8,128)(2,1)}, bf16[1536,2048]{1,0:T(8,128)(2,1)}) custom-call(bf16[1536,384]{1,0:T(8,128)(2,1)S(1)} %inputs_transposed.1.inputs, bf16[384,512]{1,0:T(8,128)(2,1)S(1)} %get-tuple-element.96.gate_delta, bf16[384,512]{1,0:T(8,128)(2,1)S(1)} %get-tuple-element.97.up_delta, ...), custom_call_target="tpu_custom_call", output_to_operand_aliasing={{0}: (3, {}), {1}: (4, {})} | custom-call | tf_op jit(solution)/shard_map/gate_and_up_grad/pallas_call | solution.py:412
  107.6 6.1 %down_grad.1 = bf16[2048,1536]{1,0:T(8,128)(2,1)} custom-call(s32[2]{0:T(128)S(1)} %pad_add_fusion.ids, bf16[288,2048]{1,0:T(8,128)(2,1)S(1)} %get-tuple-element.77.early, bf16[96,2048]{1,0:T(8,128)(2,1)S(1)} %get-tuple-element.103.late, bf16[384,1536]{1,0:T(8,128)(2,1)S(1)} %get-tuple-element.66.refs_0_.cotangent), custom_call_target="tpu_custom_call" | custom-call | flops 2415919104 | bytes 9043968 | tf_op jit(solution)/shard_map/down_grad/pallas_call | solution.py:295
  113.7 3.3 %deltas_and_input_grad.6 = (bf16[384,512]{1,0:T(8,128)(2,1)S(1)}, bf16[384,512]{1,0:T(8,128)(2,1)S(1)}, f32[384,1536]{1,0:T(8,128)S(1)}) custom-call(s32[2]{0:T(128)S(1)} %pad_add_fusion.ids, bf16[384,512]{1,0:T(8,128)(2,1)S(1)} %add_convert_fusion.4.refs_0_, bf16[384,512]{1,0:T(8,128)(2,1)S(1)} %collective-permute-done.21.refs_1_, ...), custom_call_target="tpu_custom_call" | custom-call | tf_op jit(solution)/shard_map/deltas_and_input_grad/pallas_call | solution.py:377
  117.0 3.1 %gate_and_up_grad.6 = (bf16[1536,2048]{1,0:T(8,128)(2,1)}, bf16[1536,2048]{1,0:T(8,128)(2,1)}) custom-call(bf16[1536,384]{1,0:T(8,128)(2,1)S(1)} %inputs_transposed.1.inputs, bf16[384,512]{1,0:T(8,128)(2,1)S(1)} %get-tuple-element.106.gate_delta, bf16[384,512]{1,0:T(8,128)(2,1)S(1)} %get-tuple-element.107.up_delta, ...), custom_call_target="tpu_custom_call", output_to_operand_aliasing={{0}: (3, {}), {1}: (4, {})} | custom-call | tf_op jit(solution)/shard_map/gate_and_up_grad/pallas_call | solution.py:412
  120.1 3.3 %deltas_and_input_grad.7 = (bf16[384,512]{1,0:T(8,128)(2,1)S(1)}, bf16[384,512]{1,0:T(8,128)(2,1)S(1)}, bf16[4,48,1536]{2,1,0:T(8,128)(2,1)S(1)}, bf16[4,48,1536]{2,1,0:T(8,128)(2,1)S(1)}) custom-call(s32[2]{0:T(128)S(1)} %pad_add_fusion.ids, bf16[384,512]{1,0:T(8,128)(2,1)S(1)} %add_convert_fusion.3.refs_0_, ...), custom_call_target="tpu_custom_call" | custom-call | tf_op jit(solution)/shard_map/deltas_and_input_grad/pallas_call | solution.py:377
  123.5 2.0 %collective-permute-done.24 = bf16[4,48,1536]{2,1,0:T(8,128)(2,1)S(1)} collective-permute-done((bf16[4,48,1536]{2,1,0:T(8,128)(2,1)S(1)}, bf16[4,48,1536]{2,1,0:T(8,128)(2,1)S(1)}, u32[]{:S(2)}, u32[]{:S(2)}) %collective-permute-start.24) | collective-permute-done | bytes 589856 | tf_op jit(solution)/shard_map/ppermute | solution.py:507
  125.7 1.5 %collective-permute-start.25 = (bf16[48,1536]{1,0:T(8,128)(2,1)S(1)}, bf16[48,1536]{1,0:T(8,128)(2,1)S(1)}, u32[]{:S(2)}, u32[]{:S(2)}) collective-permute-start(bf16[48,1536]{1,0:T(8,128)(2,1)S(1)} %get-tuple-element.122), channel_id=1, source_target_pairs={{0,2},{1,3},{2,0},{3,1},{4,6},{5,7},{6,4},{7,5},{8,10},{9,11},{10,... | collective-permute-start | bytes 442376 | tf_op jit(solution)/shard_map/ppermute | solution.py:511
  127.2 1.3 collective-permute-start.27
  128.5 0.7 collective-permute-start.26
  129.2 3.1 %gate_and_up_grad.7 = (bf16[1536,2048]{1,0:T(8,128)(2,1)}, bf16[1536,2048]{1,0:T(8,128)(2,1)}) custom-call(bf16[1536,384]{1,0:T(8,128)(2,1)S(1)} %inputs_transposed.1.inputs, bf16[384,512]{1,0:T(8,128)(2,1)S(1)} %get-tuple-element.115.gate_delta, bf16[384,512]{1,0:T(8,128)(2,1)S(1)} %get-tuple-element.116.up_delta, ...), custom_call_target="tpu_custom_call", output_to_operand_aliasing={{0}: (3, {}), {1}: (4, {})} | custom-call | flops 1207959552 | bytes 5111808 | tf_op jit(solution)/shard_map/gate_and_up_grad/pallas_call | solution.py:412
  132.4 3.2 %collective-permute-done.27 = bf16[48,1536]{1,0:T(8,128)(2,1)S(1)} collective-permute-done((bf16[48,1536]{1,0:T(8,128)(2,1)S(1)}, bf16[48,1536]{1,0:T(8,128)(2,1)S(1)}, u32[]{:S(2)}, u32[]{:S(2)}) %collective-permute-start.27) | collective-permute-done | bytes 147488 | tf_op jit(solution)/shard_map/ppermute | solution.py:511
  135.6 1.4 collective-permute-done.26
  137.0 0.7 fusion.2
  (49 shorter events, 4.2 us)
Async XLA Ops:
  1.9 23.2 %collective-permute-start.8 = (bf16[192,2048]{1,0:T(8,128)(2,1)S(1)}, bf16[192,2048]{1,0:T(8,128)(2,1)}, u32[]{:S(2)}, u32[]{:S(2)}) collective-permute-start(bf16[192,2048]{1,0:T(8,128)(2,1)S(1)} %get-tuple-element.65.refs_0_), channel_id=1, source_target_pairs={{8,16},{16,8},{9,17},{17,9},{10,18},{18,10},{11,19},{19,11},{12,20... | collective-permute-start | bytes 2359304 | tf_op jit(solution)/shard_map/ppermute | solution.py:444
  3.4 22.9 %collective-permute-start.7 = (bf16[192,2048]{1,0:T(8,128)(2,1)S(1)}, bf16[192,2048]{1,0:T(8,128)(2,1)}, u32[]{:S(2)}, u32[]{:S(2)}) collective-permute-start(bf16[192,2048]{1,0:T(8,128)(2,1)S(1)} %get-tuple-element.65.refs_0_), channel_id=1, source_target_pairs={{0,8},{24,16},{8,0},{16,24},{1,9},{25,17},{9,1},{17,25},{2,10},{26... | collective-permute-start | bytes 2359304 | tf_op jit(solution)/shard_map/ppermute | solution.py:55
  8.4 0.9 copy-start
  9.3 8.2 %collective-permute-start.3 = (bf16[96,1536]{1,0:T(8,128)(2,1)S(1)}, bf16[96,1536]{1,0:T(8,128)(2,1)S(1)}, u32[]{:S(2)}, u32[]{:S(2)}) collective-permute-start(bf16[96,1536]{1,0:T(8,128)(2,1)S(1)} %get-tuple-element.63.refs_0_), channel_id=1, source_target_pairs={{0,4},{1,5},{2,6},{3,7},{4,0},{5,1},{6,2},{7,3},{8,12},{9,13},{10,... | collective-permute-start | bytes 884744 | tf_op jit(solution)/shard_map/ppermute | solution.py:86
  10.8 8.2 %collective-permute-start.1 = (bf16[96,1536]{1,0:T(8,128)(2,1)S(1)}, bf16[96,1536]{1,0:T(8,128)(2,1)S(1)}, u32[]{:S(2)}, u32[]{:S(2)}) collective-permute-start(bf16[96,1536]{1,0:T(8,128)(2,1)S(1)} %get-tuple-element.63.refs_0_), channel_id=1, source_target_pairs={{0,2},{1,3},{2,0},{3,1},{4,6},{5,7},{6,4},{7,5},{8,10},{9,11},{10,... | collective-permute-start | bytes 884744 | tf_op jit(solution)/shard_map/ppermute | solution.py:86
  12.3 6.7 %collective-permute-start = (bf16[96,1536]{1,0:T(8,128)(2,1)S(1)}, bf16[96,1536]{1,0:T(8,128)(2,1)S(1)}, u32[]{:S(2)}, u32[]{:S(2)}) collective-permute-start(bf16[96,1536]{1,0:T(8,128)(2,1)S(1)} %get-tuple-element.63.refs_0_), channel_id=1, source_target_pairs={{0,1},{1,0},{2,3},{3,2},{4,5},{5,4},{6,7},{7,6},{8,9},{9,8},{10,11... | collective-permute-start | bytes 884744 | tf_op jit(solution)/shard_map/ppermute | solution.py:86
  17.5 7.6 %collective-permute-start.5 = (bf16[96,1536]{1,0:T(8,128)(2,1)S(1)}, bf16[96,1536]{1,0:T(8,128)(2,1)S(1)}, u32[]{:S(2)}, u32[]{:S(2)}) collective-permute-start(bf16[96,1536]{1,0:T(8,128)(2,1)S(1)} %collective-permute-done.3.refs_4_), channel_id=1, source_target_pairs={{0,2},{1,3},{2,0},{3,1},{4,6},{5,7},{6,4},{7,5},{8,10},{9,11},{10,... | collective-permute-start | bytes 884744 | tf_op jit(solution)/shard_map/ppermute | solution.py:86
  19.0 8.2 %collective-permute-start.4 = (bf16[96,1536]{1,0:T(8,128)(2,1)S(1)}, bf16[96,1536]{1,0:T(8,128)(2,1)S(1)}, u32[]{:S(2)}, u32[]{:S(2)}) collective-permute-start(bf16[96,1536]{1,0:T(8,128)(2,1)S(1)} %collective-permute-done.3.refs_4_), channel_id=1, source_target_pairs={{0,1},{1,0},{2,3},{3,2},{4,5},{5,4},{6,7},{7,6},{8,9},{9,8},{10,11... | collective-permute-start | bytes 884744 | tf_op jit(solution)/shard_map/ppermute | solution.py:86
  19.0 8.2 %collective-permute-start.2 = (bf16[96,1536]{1,0:T(8,128)(2,1)S(1)}, bf16[96,1536]{1,0:T(8,128)(2,1)S(1)}, u32[]{:S(2)}, u32[]{:S(2)}) collective-permute-start(bf16[96,1536]{1,0:T(8,128)(2,1)S(1)} %collective-permute-done.1.refs_2_), channel_id=1, source_target_pairs={{0,1},{1,0},{2,3},{3,2},{4,5},{5,4},{6,7},{7,6},{8,9},{9,8},{10,11... | collective-permute-start | bytes 884744 | tf_op jit(solution)/shard_map/ppermute | solution.py:86
  25.1 2.1 %collective-permute-start.6 = (bf16[96,1536]{1,0:T(8,128)(2,1)S(1)}, bf16[96,1536]{1,0:T(8,128)(2,1)S(1)}, u32[]{:S(2)}, u32[]{:S(2)}) collective-permute-start(bf16[96,1536]{1,0:T(8,128)(2,1)S(1)} %collective-permute-done.5.refs_6_), channel_id=1, source_target_pairs={{0,1},{1,0},{2,3},{3,2},{4,5},{5,4},{6,7},{7,6},{8,9},{9,8},{10,11... | collective-permute-start | bytes 884744 | tf_op jit(solution)/shard_map/ppermute | solution.py:86
  25.1 26.0 %collective-permute-start.15 = (bf16[192,2048]{1,0:T(8,128)(2,1)}, bf16[192,2048]{1,0:T(8,128)(2,1)}, u32[]{:S(2)}, u32[]{:S(2)}) collective-permute-start(bf16[192,2048]{1,0:T(8,128)(2,1)} %collective-permute-done.8.refs_2_), channel_id=1, source_target_pairs={{8,0},{16,24},{9,1},{17,25},{10,2},{18,26},{11,3},{19,27},{12,4},{... | collective-permute-start | bytes 2359304 | tf_op jit(solution)/shard_map/ppermute | solution.py:69
  26.4 24.7 %collective-permute-start.14 = (bf16[192,2048]{1,0:T(8,128)(2,1)}, bf16[192,2048]{1,0:T(8,128)(2,1)S(1)}, u32[]{:S(2)}, u32[]{:S(2)}) collective-permute-start(bf16[192,2048]{1,0:T(8,128)(2,1)} %collective-permute-done.7.refs_1_), channel_id=1, source_target_pairs={{8,16},{16,8},{9,17},{17,9},{10,18},{18,10},{11,19},{19,11},{12,20... | collective-permute-start | bytes 2359304 | tf_op jit(solution)/shard_map/ppermute | solution.py:444
  30.0 33.4 %copy-start.1 = (bf16[192,2048]{1,0:T(8,128)(2,1)S(1)}, bf16[192,2048]{1,0:T(8,128)(2,1)}, u32[]{:S(2)}) copy-start(bf16[192,2048]{1,0:T(8,128)(2,1)} %copy-done) | copy-start | bytes 2359300
  30.0 15.7 %collective-permute-start.9 = (bf16[384,512]{1,0:T(8,128)(2,1)S(1)}, bf16[384,512]{1,0:T(8,128)(2,1)S(1)}, u32[]{:S(2)}, u32[]{:S(2)}) collective-permute-start(bf16[384,512]{1,0:T(8,128)(2,1)S(1)} %get-tuple-element.70), channel_id=1, source_target_pairs={{0,8},{24,16},{1,9},{25,17},{2,10},{26,18},{3,11},{27,19},{4,12},{... | collective-permute-start | bytes 1179656 | tf_op jit(solution)/shard_map/ppermute | solution.py:482
  37.2 55.6 %slice-start.2 = ((s8[6291456]{0:T(1024)(128)(4,1)}), s8[4194304]{0:T(1024)(128)(4,1)S(1)}, s32[]{:S(2)}) async-start(s8[6291456]{0:T(1024)(128)(4,1)} %bitcast.15), calls=%async_computation.2 | async-start | bytes 8388608
  45.7 12.0 %collective-permute-start.10 = (bf16[384,512]{1,0:T(8,128)(2,1)S(1)}, bf16[384,512]{1,0:T(8,128)(2,1)S(1)}, u32[]{:S(2)}, u32[]{:S(2)}) collective-permute-start(bf16[384,512]{1,0:T(8,128)(2,1)S(1)} %get-tuple-element.71), channel_id=1, source_target_pairs={{0,8},{24,16},{1,9},{25,17},{2,10},{26,18},{3,11},{27,19},{4,12},{... | collective-permute-start | bytes 1179656 | tf_op jit(solution)/shard_map/ppermute | solution.py:482
  50.1 42.8 %slice-start = ((s8[6291456]{0:T(1024)(128)(4,1)}), s8[4194304]{0:T(1024)(128)(4,1)S(1)}, s32[]{:S(2)}) async-start(s8[6291456]{0:T(1024)(128)(4,1)} %bitcast.13), calls=%async_computation | async-start | bytes 8388608
  51.1 41.8 %slice-start.3 = ((s8[6291456]{0:T(1024)(128)(4,1)}), s8[2097152]{0:T(1024)(128)(4,1)S(1)}, s32[]{:S(2)}) async-start(s8[6291456]{0:T(1024)(128)(4,1)} %bitcast.15), calls=%async_computation.3 | async-start | bytes 4194304
  51.2 17.2 %collective-permute-start.16 = (bf16[384,512]{1,0:T(8,128)(2,1)S(1)}, bf16[384,512]{1,0:T(8,128)(2,1)S(1)}, u32[]{:S(2)}, u32[]{:S(2)}) collective-permute-start(bf16[384,512]{1,0:T(8,128)(2,1)S(1)} %add_convert_fusion.7), channel_id=1, source_target_pairs={{8,16},{16,8},{9,17},{17,9},{10,18},{18,10},{11,19},{19,11},{12,20... | collective-permute-start | bytes 1179656 | tf_op jit(solution)/shard_map/ppermute | solution.py:486
  57.7 11.1 %collective-permute-start.11 = (bf16[384,512]{1,0:T(8,128)(2,1)S(1)}, bf16[384,512]{1,0:T(8,128)(2,1)S(1)}, u32[]{:S(2)}, u32[]{:S(2)}) collective-permute-start(bf16[384,512]{1,0:T(8,128)(2,1)S(1)} %get-tuple-element.72), channel_id=1, source_target_pairs={{0,8},{24,16},{1,9},{25,17},{2,10},{26,18},{3,11},{27,19},{4,12},{... | collective-permute-start | bytes 1179656 | tf_op jit(solution)/shard_map/ppermute | solution.py:482
  62.1 22.4 %collective-permute-start.19 = (bf16[192,2048]{1,0:T(8,128)(2,1)S(1)}, bf16[192,2048]{1,0:T(8,128)(2,1)S(1)}, u32[]{:S(2)}, u32[]{:S(2)}) collective-permute-start(bf16[192,2048]{1,0:T(8,128)(2,1)S(1)} %collective-permute-done.14.refs_0_), channel_id=1, source_target_pairs={{8,0},{16,24},{9,1},{17,25},{10,2},{18,26},{11,3},{19,27},{12,4},{... | collective-permute-start | bytes 2359304 | tf_op jit(solution)/shard_map/ppermute | solution.py:69
  67.5 25.4 %slice-start.1 = ((s8[6291456]{0:T(1024)(128)(4,1)}), s8[2097152]{0:T(1024)(128)(4,1)S(1)}, s32[]{:S(2)}) async-start(s8[6291456]{0:T(1024)(128)(4,1)} %bitcast.13), calls=%async_computation.1 | async-start | bytes 4194304
  67.6 14.9 %collective-permute-start.22 = (bf16[384,512]{1,0:T(8,128)(2,1)S(1)}, bf16[384,512]{1,0:T(8,128)(2,1)S(1)}, u32[]{:S(2)}, u32[]{:S(2)}) collective-permute-start(bf16[384,512]{1,0:T(8,128)(2,1)S(1)} %add_convert_fusion.2), channel_id=1, source_target_pairs={{8,16},{16,8},{9,17},{17,9},{10,18},{18,10},{11,19},{19,11},{12,20... | collective-permute-start | bytes 1179656 | tf_op jit(solution)/shard_map/ppermute | solution.py:486
  68.7 13.0 %collective-permute-start.12 = (bf16[384,512]{1,0:T(8,128)(2,1)S(1)}, bf16[384,512]{1,0:T(8,128)(2,1)S(1)}, u32[]{:S(2)}, u32[]{:S(2)}) collective-permute-start(bf16[384,512]{1,0:T(8,128)(2,1)S(1)} %get-tuple-element.73), channel_id=1, source_target_pairs={{0,8},{24,16},{1,9},{25,17},{2,10},{26,18},{3,11},{27,19},{4,12},{... | collective-permute-start | bytes 1179656 | tf_op jit(solution)/shard_map/ppermute | solution.py:482
  76.0 16.9 %collective-permute-start.17 = (bf16[384,512]{1,0:T(8,128)(2,1)S(1)}, bf16[384,512]{1,0:T(8,128)(2,1)S(1)}, u32[]{:S(2)}, u32[]{:S(2)}) collective-permute-start(bf16[384,512]{1,0:T(8,128)(2,1)S(1)} %add_convert_fusion.6.refs_0_), channel_id=1, source_target_pairs={{8,0},{16,24},{9,1},{17,25},{10,2},{18,26},{11,3},{19,27},{12,4},{... | collective-permute-start | bytes 1179656 | tf_op jit(solution)/shard_map/ppermute | solution.py:69
  77.4 9.7 %collective-permute-start.18 = (bf16[384,512]{1,0:T(8,128)(2,1)S(1)}, bf16[384,512]{1,0:T(8,128)(2,1)S(1)}, u32[]{:S(2)}, u32[]{:S(2)}) collective-permute-start(bf16[384,512]{1,0:T(8,128)(2,1)S(1)} %add_convert_fusion.5), channel_id=1, source_target_pairs={{8,16},{16,8},{9,17},{17,9},{10,18},{18,10},{11,19},{19,11},{12,20... | collective-permute-start | bytes 1179656 | tf_op jit(solution)/shard_map/ppermute | solution.py:486
  81.8 17.3 %collective-permute-start.13 = (bf16[384,512]{1,0:T(8,128)(2,1)S(1)}, bf16[384,512]{1,0:T(8,128)(2,1)S(1)}, u32[]{:S(2)}, u32[]{:S(2)}) collective-permute-start(bf16[384,512]{1,0:T(8,128)(2,1)S(1)} %add_convert_fusion.8), channel_id=1, source_target_pairs={{8,16},{16,8},{9,17},{17,9},{10,18},{18,10},{11,19},{19,11},{12,20... | collective-permute-start | bytes 1179656 | tf_op jit(solution)/shard_map/ppermute | solution.py:486
  84.4 16.9 %collective-permute-start.23 = (bf16[384,512]{1,0:T(8,128)(2,1)S(1)}, bf16[384,512]{1,0:T(8,128)(2,1)S(1)}, u32[]{:S(2)}, u32[]{:S(2)}) collective-permute-start(bf16[384,512]{1,0:T(8,128)(2,1)S(1)} %add_convert_fusion.1.refs_0_), channel_id=1, source_target_pairs={{8,0},{16,24},{9,1},{17,25},{10,2},{18,26},{11,3},{19,27},{12,4},{... | collective-permute-start | bytes 1179656 | tf_op jit(solution)/shard_map/ppermute | solution.py:69
  87.2 26.6 %collective-permute-start.21 = (bf16[384,512]{1,0:T(8,128)(2,1)S(1)}, bf16[384,512]{1,0:T(8,128)(2,1)S(1)}, u32[]{:S(2)}, u32[]{:S(2)}) collective-permute-start(bf16[384,512]{1,0:T(8,128)(2,1)S(1)} %add_convert_fusion.4.refs_0_), channel_id=1, source_target_pairs={{8,0},{16,24},{9,1},{17,25},{10,2},{18,26},{11,3},{19,27},{12,4},{... | collective-permute-start | bytes 1179656 | tf_op jit(solution)/shard_map/ppermute | solution.py:69
  99.2 20.9 %collective-permute-start.20 = (bf16[384,512]{1,0:T(8,128)(2,1)S(1)}, bf16[384,512]{1,0:T(8,128)(2,1)S(1)}, u32[]{:S(2)}, u32[]{:S(2)}) collective-permute-start(bf16[384,512]{1,0:T(8,128)(2,1)S(1)} %add_convert_fusion.3.refs_0_), channel_id=1, source_target_pairs={{8,0},{16,24},{9,1},{17,25},{10,2},{18,26},{11,3},{19,27},{12,4},{... | collective-permute-start | bytes 1179656 | tf_op jit(solution)/shard_map/ppermute | solution.py:69
  123.4 2.1 %collective-permute-start.24 = (bf16[4,48,1536]{2,1,0:T(8,128)(2,1)S(1)}, bf16[4,48,1536]{2,1,0:T(8,128)(2,1)S(1)}, u32[]{:S(2)}, u32[]{:S(2)}) collective-permute-start(bf16[4,48,1536]{2,1,0:T(8,128)(2,1)S(1)} %get-tuple-element.114), channel_id=1, source_target_pairs={{0,1},{1,0},{2,3},{3,2},{4,5},{5,4},{6,7},{7,6},{8,9},{9,8},{10,11... | collective-permute-start | bytes 1769480 | tf_op jit(solution)/shard_map/ppermute | solution.py:507
  125.7 6.8 %collective-permute-start.25 = (bf16[48,1536]{1,0:T(8,128)(2,1)S(1)}, bf16[48,1536]{1,0:T(8,128)(2,1)S(1)}, u32[]{:S(2)}, u32[]{:S(2)}) collective-permute-start(bf16[48,1536]{1,0:T(8,128)(2,1)S(1)} %get-tuple-element.122), channel_id=1, source_target_pairs={{0,2},{1,3},{2,0},{3,1},{4,6},{5,7},{6,4},{7,5},{8,10},{9,11},{10,... | collective-permute-start | bytes 442376 | tf_op jit(solution)/shard_map/ppermute | solution.py:511
  127.2 8.4 %collective-permute-start.27 = (bf16[48,1536]{1,0:T(8,128)(2,1)S(1)}, bf16[48,1536]{1,0:T(8,128)(2,1)S(1)}, u32[]{:S(2)}, u32[]{:S(2)}) collective-permute-start(bf16[48,1536]{1,0:T(8,128)(2,1)S(1)} %get-tuple-element.123), channel_id=1, source_target_pairs={{0,6},{1,7},{2,4},{3,5},{4,2},{5,3},{6,0},{7,1},{8,14},{9,15},{10,... | collective-permute-start | bytes 442376 | tf_op jit(solution)/shard_map/ppermute | solution.py:511
  128.5 8.5 %collective-permute-start.26 = (bf16[48,1536]{1,0:T(8,128)(2,1)S(1)}, bf16[48,1536]{1,0:T(8,128)(2,1)S(1)}, u32[]{:S(2)}, u32[]{:S(2)}) collective-permute-start(bf16[48,1536]{1,0:T(8,128)(2,1)S(1)} %get-tuple-element.124), channel_id=1, source_target_pairs={{0,4},{1,5},{2,6},{3,7},{4,0},{5,1},{6,2},{7,3},{8,12},{9,13},{10,... | collective-permute-start | bytes 442376 | tf_op jit(solution)/shard_map/ppermute | solution.py:511

commit v2 on v1

--- a/solution.py
+++ b/solution.py
@@ -272,7 +272,7 @@
         compiler_params=pltpu.CompilerParams(vmem_limit_bytes=16 * MIB),
         cost_estimate=pl.CostEstimate(
             flops=10 * rows * width,
-            bytes_accessed=4 * rows * width + 6 * rows * width,
+            bytes_accessed=10 * rows * width * (8 if len(sources) == 1 else 1),
             transcendentals=rows * width,
         ),
         name="factors",
@@ -320,7 +320,11 @@
     middle, got, *factors, gate_weight, up_weight = refs[:8]
     refs = list(refs[8:])
     before = None if first else refs.pop(0)
-    gate_out, up_out = refs[:2]
+    if last:
+        gate_out, up_out = refs[:2]
+    else:
+        inputs = refs.pop(0)
+        running, gate_grad, up_grad, gate_out, up_out = refs[-5:]
 
     @pl.when(pl.program_id(0) == 0)
     def _():
@@ -341,7 +345,9 @@
     if not first:
         term += before[...]
     if not last:
-        refs[2][...] = term
+        running[...] = term
+        gate_grad[...] = contract(inputs[...], gate_out[...], 1, 0).astype(BF16)
+        up_grad[...] = contract(inputs[...], up_out[...], 1, 0).astype(BF16)
         return
     keep, send, result = refs[2:]
     result[...] = term
@@ -352,25 +358,36 @@
         out[slot // 2] = result[rows_at(start, rows), :].astype(BF16)
 
 
-def deltas(ids, grads, factors, weights, n, n_col, chunk, before):
+def deltas(ids, grads, factors, weights, inputs_t, n, n_col, chunk, before, weight_out):
     total, units = grads[0].shape
-    depth = weights[0].shape[0]
+    depth, width = weights[0].shape
     rows = total // n_col
     tile = tile_of(depth, 512)
     tall = whole((total, units))
     wide = pl.BlockSpec((tile, units), lambda j, *_: (j, chunk))
     running = pl.BlockSpec((total, tile), lambda j, *_: (0, j))
-    delta_shape = jax.ShapeDtypeStruct((total, units), BF16)
+    delta_shape = (total, units)
     last = chunk == CHUNKS - 1
+    more = [] if before is None else [before]
+    more_specs = [running] * len(more)
+    aliases = {}
     if last:
         half = pl.BlockSpec((n_col // 2, rows, tile), lambda j, *_: (0, 0, j))
-        out_specs = [half, half]
-        out_shape = [jax.ShapeDtypeStruct((n_col // 2, rows, depth), BF16)] * 2
+        out_specs = [tall, tall, half, half]
+        out_shape = [jax.ShapeDtypeStruct(delta_shape, BF16)] * 2
+        out_shape += [jax.ShapeDtypeStruct((n_col // 2, rows, depth), BF16)] * 2
         scratch = [pltpu.VMEM((total, tile), F32)]
     else:
-        out_specs, scratch = [running], []
+        more.append(inputs_t)
+        more_specs.append(pl.BlockSpec((tile, total), lambda j, *_: (j, 0)))
+        held, held_specs = filled(weight_out)
+        aliases = {9 + len(more) + number: 1 + number for number in range(len(held))}
+        more += held
+        more_specs += held_specs
+        out_specs = [running, wide, wide]
         out_shape = [jax.ShapeDtypeStruct((total, depth), F32)]
-    more = [] if before is None else [before]
+        out_shape += [jax.ShapeDtypeStruct((depth, width), BF16)] * 2
+        scratch = [pltpu.VMEM(delta_shape, BF16)] * 2
     factor_specs = [
         pl.BlockSpec((factor.shape[0], units), lambda j, *_: (0, chunk)) for factor in factors
     ]
@@ -379,14 +396,15 @@
         grid_spec=pltpu.PrefetchScalarGridSpec(
             num_scalar_prefetch=1,
             grid=(depth // tile,),
-            in_specs=[tall] * 2 + factor_specs + [wide] * 2 + [running] * len(more),
-            out_specs=[tall, tall] + out_specs,
+            in_specs=[tall] * 2 + factor_specs + [wide] * 2 + more_specs,
+            out_specs=out_specs,
             scratch_shapes=scratch,
         ),
-        out_shape=[delta_shape, delta_shape] + out_shape,
+        out_shape=out_shape,
+        input_output_aliases=aliases,
         compiler_params=pltpu.CompilerParams(vmem_limit_bytes=28 * MIB),
         cost_estimate=NO_COST,
-        name="deltas_and_input_grad",
+        name="chunk",
     )(ids, *grads, *factors, *weights, *more)
 
 
@@ -454,36 +472,41 @@
     early = factors_of(ids, sources[:-1], n_row)
     late = factors_of(ids, sources[-1:], n_row)
     factors = [*early[:2], *late[:2]]
-    before = {0: early, 2: late}
+    before = {0: [*early, *late]}
     running = weight_out = met = None
     sent = []
 
     def work_on(chunk, running, weight_out):
-        gate_delta, up_delta, *running = deltas(
+        made = deltas(
             ids,
             sent[chunk],
             factors,
             (gate_weight, up_weight),
+            inputs_t,
             n_row,
             n_col,
             chunk,
             running,
+            weight_out,
         )
-        weight_out = weight_grads(inputs_t, gate_delta, up_delta, chunk, weight_out)
-        if chunk == CHUNKS - 1:
+        if chunk < CHUNKS - 1:
+            running, *weight_out = lax.optimization_barrier(tuple(made))
             return running, weight_out
-        running, *weight_out = lax.optimization_barrier((running[0], *weight_out))
-        return running, weight_out
+        gate_delta, up_delta, *running = made
+        return running, weight_grads(inputs_t, gate_delta, up_delta, chunk, weight_out)
 
     for chunk, held in enumerate(terms):
         for step in range(half - 1):
             if met is not None:
                 held = after(held, met)
-            got = met = lax.ppermute(held, "row", inward([step], n_row))
+            got = lax.ppermute(held, "row", inward([step], n_row))
+            met = got
             if chunk == 0:
                 got = after(got, terms[-1], far[-1], away[0][1], inputs_t)
             held = add(held, got)
-        got = lax.ppermute(held, "row", across(n_row))
+        if chunk == 1:
+            held = after(held, crossed)
+        got = crossed = lax.ppermute(held, "row", across(n_row))
         if chunk == CHUNKS - 1:
             sent[0] = (sent[0][0], after(sent[0][1], sent[2][0]))
             running, weight_out = work_on(0, None, None)
@@ -491,18 +514,13 @@
         elif chunk in before:
             got = after(got, *before[chunk])
         held = add(held, got)
-        if chunk == 1:
-            held = after(held, away[-1][1])
         sent.append(sent_out(held, place, n_row))
 
     for chunk in range(1, CHUNKS):
-        if chunk == CHUNKS - 2:
-            hidden = after(late[2], running)
-            down_grad = down_grads(ids, early[2], hidden, tokens, n_row)
-            running, down_grad = lax.optimization_barrier((running, down_grad))
         running, weight_out = work_on(chunk, running, weight_out)
     gate_grad, up_grad = weight_out
     keep, send = running
+    down_grad = down_grads(ids, early[2], after(late[2], send), tokens, n_row)
 
     keep = add(keep, lax.ppermute(send, "col", [(i, i ^ 1) for i in range(n_col)]))
     input_grad = keep[0].astype(F32)

time: 138 us -> 130 us (0.942)
  starting transfers between devices: 50 us -> 45.9 us
  waiting for transfers between devices: 37 us -> 34.6 us
    pallas_call x4 -> x1, Pallas kernels: 12.3 us -> 3.05 us  [weight_grads(): pl.pallas_call(weight_grad_kernel, grid=(depth // tile,), in_specs=[pl.Bl...]
    pallas_call x4, Pallas kernels: 12.9 us -> 20.8 us  [deltas(): pl.pallas_call(functools.partial(delta_kernel, n, n_col, before is None,...]
    ppermute x3, waiting for transfers between devices: 4.71 us -> 0.01 us  [on_device(): input_grad += lax.ppermute(keep[number], 'col', pairs).astype(F32)]
    ppermute x8, starting transfers between devices: 26.1 us -> 23.7 us  [the longest x4 20.8 us: on_device(): got = lax.ppermute(held, 'row', inward([step], n_row))]
    ppermute x6, waiting for transfers between devices: 6.89 us -> 9.16 us  [sent_out(): got = lax.ppermute(block, 'row', outward([step], n))]
    ppermute x1, starting transfers between devices: 5.01 us -> 3.09 us  [own_half(): met = lax.ppermute(block, 'row', inward([0], n) + outward([0], n))]
  transfers between devices with their start and end apart: 28 -> 28, of which waited for: 13 -> 10; matrix products, arithmetic and copies ran while one was open for 1% -> 1% of each run, Pallas kernels for 31% -> 32%
where the time goes in v2:
time: 130 us
  starting transfers between devices  45.9 us (35%)
  Pallas kernels  45.7 us (35%)
  waiting for transfers between devices  34.6 us (27%)
  other arithmetic  1.77 us (1%)
    ppermute x4, starting transfers between devices, on_device(): got = lax.ppermute(held, 'row', inward([step], n_row))  20.8 us
    pallas_call x4, Pallas kernels, deltas(): pl.pallas_call(functools.partial(delta_kernel, n, n_col, before is None,...  20.8 us
    ppermute x4, waiting for transfers between devices, on_device(): got = lax.ppermute(held, 'row', inward([step], n_row))  12.3 us
    ppermute x7, waiting for transfers between devices, cube_gather(): pieces[slot | bit] = lax.ppermute(pieces[slot], 'col', pairs)  11.1 us
    ppermute x6, waiting for transfers between devices, sent_out(): got = lax.ppermute(block, 'row', outward([step], n))  9.16 us
    ppermute x6, starting transfers between devices, sent_out(): got = lax.ppermute(block, 'row', outward([step], n))  8.2 us
    pallas_call x2, Pallas kernels, partials(): pl.pallas_call(functools.partial(partial_kernel, len(pieces)), grid_spec=...  8.13 us
    pallas_call x1, Pallas kernels, down_grads(): pl.pallas_call(functools.partial(down_kernel, n), grid_spec=pltpu.Prefetc...  6.08 us
  transfers between devices with their start and end apart: 28, of which 10 were waited for; matrix products, arithmetic and copies ran while one was open for 1% of the time, Pallas kernels for 32%

profile of v2, /device:TPU:0, one launch (start us, length us, event | category | flops | bytes accessed | tf_op | source)
XLA Modules:
  0.0 129.9 jit_solution(16083925260860100741)
XLA Ops:
  0.6 1.2 join.1
  1.9 3.1 %collective-permute-start.7 = (bf16[192,2048]{1,0:T(8,128)(2,1)S(1)}, bf16[192,2048]{1,0:T(8,128)(2,1)}, u32[]{:S(2)}, u32[]{:S(2)}) collective-permute-start(bf16[192,2048]{1,0:T(8,128)(2,1)S(1)} %get-tuple-element.47.refs_0_), channel_id=1, source_target_pairs={{0,8},{24,16},{8,0},{16,24},{1,9},{25,17},{9,1},{17,25},{2,10},{26... | collective-permute-start | bytes 2359304 | tf_op jit(solution)/shard_map/ppermute | solution.py:55
  5.0 1.6 %collective-permute-start.8 = (bf16[192,2048]{1,0:T(8,128)(2,1)S(1)}, bf16[192,2048]{1,0:T(8,128)(2,1)}, u32[]{:S(2)}, u32[]{:S(2)}) collective-permute-start(bf16[192,2048]{1,0:T(8,128)(2,1)S(1)} %get-tuple-element.47.refs_0_), channel_id=1, source_target_pairs={{8,16},{16,8},{9,17},{17,9},{10,18},{18,10},{11,19},{19,11},{12,20... | collective-permute-start | bytes 2359304 | tf_op jit(solution)/shard_map/ppermute | solution.py:462
  6.5 0.9 copy-done
  7.4 1.5 %collective-permute-start.3 = (bf16[96,1536]{1,0:T(8,128)(2,1)S(1)}, bf16[96,1536]{1,0:T(8,128)(2,1)S(1)}, u32[]{:S(2)}, u32[]{:S(2)}) collective-permute-start(bf16[96,1536]{1,0:T(8,128)(2,1)S(1)} %get-tuple-element.45.refs_0_), channel_id=1, source_target_pairs={{0,4},{1,5},{2,6},{3,7},{4,0},{5,1},{6,2},{7,3},{8,12},{9,13},{10,... | collective-permute-start | bytes 884744 | tf_op jit(solution)/shard_map/ppermute | solution.py:86
  8.9 1.5 %collective-permute-start.1 = (bf16[96,1536]{1,0:T(8,128)(2,1)S(1)}, bf16[96,1536]{1,0:T(8,128)(2,1)S(1)}, u32[]{:S(2)}, u32[]{:S(2)}) collective-permute-start(bf16[96,1536]{1,0:T(8,128)(2,1)S(1)} %get-tuple-element.45.refs_0_), channel_id=1, source_target_pairs={{0,2},{1,3},{2,0},{3,1},{4,6},{5,7},{6,4},{7,5},{8,10},{9,11},{10,... | collective-permute-start | bytes 884744 | tf_op jit(solution)/shard_map/ppermute | solution.py:86
  10.4 5.5 %collective-permute-done.3.refs_4_ = bf16[96,1536]{1,0:T(8,128)(2,1)S(1)} collective-permute-done((bf16[96,1536]{1,0:T(8,128)(2,1)S(1)}, bf16[96,1536]{1,0:T(8,128)(2,1)S(1)}, u32[]{:S(2)}, u32[]{:S(2)}) %collective-permute-start.3) | collective-permute-done | bytes 294944 | tf_op jit(solution)/shard_map/ppermute | solution.py:86
  15.9 1.5 %collective-permute-start.5 = (bf16[96,1536]{1,0:T(8,128)(2,1)S(1)}, bf16[96,1536]{1,0:T(8,128)(2,1)S(1)}, u32[]{:S(2)}, u32[]{:S(2)}) collective-permute-start(bf16[96,1536]{1,0:T(8,128)(2,1)S(1)} %collective-permute-done.3.refs_4_), channel_id=1, source_target_pairs={{0,2},{1,3},{2,0},{3,1},{4,6},{5,7},{6,4},{7,5},{8,10},{9,11},{10,... | collective-permute-start | bytes 884744 | tf_op jit(solution)/shard_map/ppermute | solution.py:86
  17.4 0.5 collective-permute-start.2
  17.9 5.7 %collective-permute-done.5.refs_6_ = bf16[96,1536]{1,0:T(8,128)(2,1)S(1)} collective-permute-done((bf16[96,1536]{1,0:T(8,128)(2,1)S(1)}, bf16[96,1536]{1,0:T(8,128)(2,1)S(1)}, u32[]{:S(2)}, u32[]{:S(2)}) %collective-permute-start.5) | collective-permute-done | bytes 294944 | tf_op jit(solution)/shard_map/ppermute | solution.py:86
  23.5 0.7 collective-permute-start.14
  24.3 1.3 collective-permute-start.15
  25.6 2.8 %hidden_grad_partials.2 = (bf16[384,512]{1,0:T(8,128)(2,1)S(1)}, bf16[384,1536]{1,0:T(8,128)(2,1)S(1)}) custom-call(s32[2]{0:T(128)S(1)} %pad_add_fusion.ids, bf16[96,1536]{1,0:T(8,128)(2,1)S(1)} %get-tuple-element.45.refs_0_, bf16[96,1536]{1,0:T(8,128)(2,1)S(1)} %collective-permute-done.refs_1_, bf16[96,1536]{1,0:T(8,128)(2,1)S(1)} %collective-permute-done.1.refs_2_, ...), custom_call_target="tpu_custom_call" | custom-call | flops 603979776 | bytes 3145728 | tf_op jit(solution)/shard_map/hidden_grad_partials/pallas_call | solution.py:193
  28.4 7.7 %collective-permute-start.9 = (bf16[384,512]{1,0:T(8,128)(2,1)S(1)}, bf16[384,512]{1,0:T(8,128)(2,1)S(1)}, u32[]{:S(2)}, u32[]{:S(2)}) collective-permute-start(bf16[384,512]{1,0:T(8,128)(2,1)S(1)} %get-tuple-element.52), channel_id=1, source_target_pairs={{0,8},{24,16},{1,9},{25,17},{2,10},{26,18},{3,11},{27,19},{4,12},{... | collective-permute-start | bytes 1179656 | tf_op jit(solution)/shard_map/ppermute | solution.py:502
  36.1 5.3 %hidden_grad_partials.3 = (bf16[384,512]{1,0:T(8,128)(2,1)S(1)}, bf16[384,512]{1,0:T(8,128)(2,1)S(1)}, bf16[384,512]{1,0:T(8,128)(2,1)S(1)}) custom-call(s32[2]{0:T(128)S(1)} %pad_add_fusion.ids, bf16[384,1536]{1,0:T(8,128)(2,1)S(1)} %get-tuple-element.48.refs_0_.cotangent, bf16[2048,1536]{1,0:T(8,128)(2,1)} %refs_1_.3), custom_call_target="tpu_custom_call" | custom-call | flops 1811939328 | bytes 7077888 | tf_op jit(solution)/shard_map/hidden_grad_partials/pallas_call | solution.py:193
  41.5 3.4 %collective-permute-done.9 = bf16[384,512]{1,0:T(8,128)(2,1)S(1)} collective-permute-done((bf16[384,512]{1,0:T(8,128)(2,1)S(1)}, bf16[384,512]{1,0:T(8,128)(2,1)S(1)}, u32[]{:S(2)}, u32[]{:S(2)}) %collective-permute-start.9) | collective-permute-done | bytes 393248 | tf_op jit(solution)/shard_map/ppermute | solution.py:502
  44.8 4.4 %collective-permute-start.10 = (bf16[384,512]{1,0:T(8,128)(2,1)S(1)}, bf16[384,512]{1,0:T(8,128)(2,1)S(1)}, u32[]{:S(2)}, u32[]{:S(2)}) collective-permute-start(bf16[384,512]{1,0:T(8,128)(2,1)S(1)} %get-tuple-element.53), channel_id=1, source_target_pairs={{0,8},{24,16},{1,9},{25,17},{2,10},{26,18},{3,11},{27,19},{4,12},{... | collective-permute-start | bytes 1179656 | tf_op jit(solution)/shard_map/ppermute | solution.py:502
  49.3 1.0 inputs_transposed.1.refs_8_.refs_9_.inputs
  50.3 1.6 %collective-permute-start.17 = (bf16[192,2048]{1,0:T(8,128)(2,1)S(1)}, bf16[192,2048]{1,0:T(8,128)(2,1)S(1)}, u32[]{:S(2)}, u32[]{:S(2)}) collective-permute-start(bf16[192,2048]{1,0:T(8,128)(2,1)S(1)} %collective-permute-done.14.refs_0_), channel_id=1, source_target_pairs={{8,0},{16,24},{9,1},{17,25},{10,2},{18,26},{11,3},{19,27},{12,4},{... | collective-permute-start | bytes 2359304 | tf_op jit(solution)/shard_map/ppermute | solution.py:69
  51.9 0.7 collective-permute-start.16
  52.6 4.5 %collective-permute-done.10 = bf16[384,512]{1,0:T(8,128)(2,1)S(1)} collective-permute-done((bf16[384,512]{1,0:T(8,128)(2,1)S(1)}, bf16[384,512]{1,0:T(8,128)(2,1)S(1)}, u32[]{:S(2)}, u32[]{:S(2)}) %collective-permute-start.10) | collective-permute-done | bytes 393248 | tf_op jit(solution)/shard_map/ppermute | solution.py:502
  57.1 4.4 %collective-permute-start.11 = (bf16[384,512]{1,0:T(8,128)(2,1)S(1)}, bf16[384,512]{1,0:T(8,128)(2,1)S(1)}, u32[]{:S(2)}, u32[]{:S(2)}) collective-permute-start(bf16[384,512]{1,0:T(8,128)(2,1)S(1)} %get-tuple-element.54), channel_id=1, source_target_pairs={{0,8},{24,16},{1,9},{25,17},{2,10},{26,18},{3,11},{27,19},{4,12},{... | collective-permute-start | bytes 1179656 | tf_op jit(solution)/shard_map/ppermute | solution.py:502
  61.6 4.1 %factors.2 = (bf16[288,2048]{1,0:T(8,128)(2,1)S(1)}, bf16[288,2048]{1,0:T(8,128)(2,1)S(1)}, bf16[288,2048]{1,0:T(8,128)(2,1)S(1)}) custom-call(s32[2]{0:T(128)S(1)} %pad_add_fusion.ids, bf16[192,2048]{1,0:T(8,128)(2,1)S(1)} %copy-done.1, bf16[192,2048]{1,0:T(8,128)(2,1)} %collective-permute-done.7.refs_1_, bf16[192,2048]{1,0:T(8,128)(2,1)} %collective-permute-done.8.refs_2_, ...), custom_call_target="tpu_custom_call" | custom-call | flops 5898240 | bytes 5898240 | tf_op jit(solution)/shard_map/factors/pallas_call | solution.py:262
  65.8 0.8 collective-permute-start.22
  66.6 1.9 %collective-permute-done.11 = bf16[384,512]{1,0:T(8,128)(2,1)S(1)} collective-permute-done((bf16[384,512]{1,0:T(8,128)(2,1)S(1)}, bf16[384,512]{1,0:T(8,128)(2,1)S(1)}, u32[]{:S(2)}, u32[]{:S(2)}) %collective-permute-start.11) | collective-permute-done | bytes 393248 | tf_op jit(solution)/shard_map/ppermute | solution.py:502
  68.5 4.4 %collective-permute-start.12 = (bf16[384,512]{1,0:T(8,128)(2,1)S(1)}, bf16[384,512]{1,0:T(8,128)(2,1)S(1)}, u32[]{:S(2)}, u32[]{:S(2)}) collective-permute-start(bf16[384,512]{1,0:T(8,128)(2,1)S(1)} %get-tuple-element.55), channel_id=1, source_target_pairs={{0,8},{24,16},{1,9},{25,17},{2,10},{26,18},{3,11},{27,19},{4,12},{... | collective-permute-start | bytes 1179656 | tf_op jit(solution)/shard_map/ppermute | solution.py:502
  73.0 0.7 collective-permute-start.19
  73.7 1.3 %factors.3 = (bf16[96,2048]{1,0:T(8,128)(2,1)S(1)}, bf16[96,2048]{1,0:T(8,128)(2,1)S(1)}, bf16[96,2048]{1,0:T(8,128)(2,1)S(1)}) custom-call(s32[2]{0:T(128)S(1)} %pad_add_fusion.ids, bf16[192,2048]{1,0:T(8,128)(2,1)S(1)} %collective-permute-done.14.refs_0_, bf16[192,2048]{1,0:T(8,128)(2,1)S(1)} %collective-permute-done.17.refs_1_), custom_call_target="tpu_custom_call" | custom-call | flops 1966080 | bytes 15728640 | tf_op jit(solution)/shard_map/factors/pallas_call | solution.py:262
  75.2 1.3 collective-permute-start.18
  76.5 2.5 %collective-permute-done.12 = bf16[384,512]{1,0:T(8,128)(2,1)S(1)} collective-permute-done((bf16[384,512]{1,0:T(8,128)(2,1)S(1)}, bf16[384,512]{1,0:T(8,128)(2,1)S(1)}, u32[]{:S(2)}, u32[]{:S(2)}) %collective-permute-start.12) | collective-permute-done | bytes 393248 | tf_op jit(solution)/shard_map/ppermute | solution.py:502
  79.1 0.7 collective-permute-start.13
  79.9 1.3 collective-permute-start.23
  81.3 1.3 collective-permute-start.21
  82.6 4.3 %collective-permute-done.18.refs_1_ = bf16[384,512]{1,0:T(8,128)(2,1)S(1)} collective-permute-done((bf16[384,512]{1,0:T(8,128)(2,1)S(1)}, bf16[384,512]{1,0:T(8,128)(2,1)S(1)}, u32[]{:S(2)}, u32[]{:S(2)}) %collective-permute-start.18) | collective-permute-done | bytes 393248 | tf_op jit(solution)/shard_map/ppermute | solution.py:69
  87.0 5.7 %chunk.4 = (f32[384,1536]{1,0:T(8,128)S(1)}, bf16[1536,2048]{1,0:T(8,128)(2,1)}, bf16[1536,2048]{1,0:T(8,128)(2,1)}) custom-call(s32[2]{0:T(128)S(1)} %pad_add_fusion.ids, bf16[384,512]{1,0:T(8,128)(2,1)S(1)} %add_convert_fusion.6.refs_0_, bf16[384,512]{1,0:T(8,128)(2,1)S(1)} %collective-permute-done.18.refs_1_, ...), custom_call_target="tpu_custom_call" | custom-call | tf_op jit(solution)/shard_map/chunk/pallas_call | solution.py:394
  92.8 1.5 %collective-permute-start.20 = (bf16[384,512]{1,0:T(8,128)(2,1)S(1)}, bf16[384,512]{1,0:T(8,128)(2,1)S(1)}, u32[]{:S(2)}, u32[]{:S(2)}) collective-permute-start(bf16[384,512]{1,0:T(8,128)(2,1)S(1)} %add_convert_fusion.3.refs_0_), channel_id=1, source_target_pairs={{8,0},{16,24},{9,1},{17,25},{10,2},{18,26},{11,3},{19,27},{12,4},{... | collective-permute-start | bytes 1179656 | tf_op jit(solution)/shard_map/ppermute | solution.py:69
  94.2 2.3 %collective-permute-done.23.refs_1_ = bf16[384,512]{1,0:T(8,128)(2,1)S(1)} collective-permute-done((bf16[384,512]{1,0:T(8,128)(2,1)S(1)}, bf16[384,512]{1,0:T(8,128)(2,1)S(1)}, u32[]{:S(2)}, u32[]{:S(2)}) %collective-permute-start.23) | collective-permute-done | bytes 393248 | tf_op jit(solution)/shard_map/ppermute | solution.py:69
  96.6 5.9 %chunk.5 = (f32[384,1536]{1,0:T(8,128)S(1)}, bf16[1536,2048]{1,0:T(8,128)(2,1)}, bf16[1536,2048]{1,0:T(8,128)(2,1)}) custom-call(s32[2]{0:T(128)S(1)} %pad_add_fusion.ids, bf16[384,512]{1,0:T(8,128)(2,1)S(1)} %add_convert_fusion.1.refs_0_, bf16[384,512]{1,0:T(8,128)(2,1)S(1)} %collective-permute-done.23.refs_1_, ...), custom_call_target="tpu_custom_call", output_to_operand_aliasing={{1}: (11, {}), {2}: (12, {})} | custom-call | tf_op jit(solution)/shard_map/chunk/pallas_call | solution.py:394
  102.4 2.5 %collective-permute-done.21.refs_1_ = bf16[384,512]{1,0:T(8,128)(2,1)S(1)} collective-permute-done((bf16[384,512]{1,0:T(8,128)(2,1)S(1)}, bf16[384,512]{1,0:T(8,128)(2,1)S(1)}, u32[]{:S(2)}, u32[]{:S(2)}) %collective-permute-start.21) | collective-permute-done | bytes 393248 | tf_op jit(solution)/shard_map/ppermute | solution.py:69
  105.0 5.9 %chunk.6 = (f32[384,1536]{1,0:T(8,128)S(1)}, bf16[1536,2048]{1,0:T(8,128)(2,1)}, bf16[1536,2048]{1,0:T(8,128)(2,1)}) custom-call(s32[2]{0:T(128)S(1)} %pad_add_fusion.ids, bf16[384,512]{1,0:T(8,128)(2,1)S(1)} %add_convert_fusion.4.refs_0_, bf16[384,512]{1,0:T(8,128)(2,1)S(1)} %collective-permute-done.21.refs_1_, ...), custom_call_target="tpu_custom_call", output_to_operand_aliasing={{1}: (11, {}), {2}: (12, {})} | custom-call | tf_op jit(solution)/shard_map/chunk/pallas_call | solution.py:394
  110.9 3.3 %chunk.7 = (bf16[384,512]{1,0:T(8,128)(2,1)S(1)}, bf16[384,512]{1,0:T(8,128)(2,1)S(1)}, bf16[4,48,1536]{2,1,0:T(8,128)(2,1)S(1)}, bf16[4,48,1536]{2,1,0:T(8,128)(2,1)S(1)}) custom-call(s32[2]{0:T(128)S(1)} %pad_add_fusion.ids, bf16[384,512]{1,0:T(8,128)(2,1)S(1)} %add_convert_fusion.3.refs_0_, bf16[384,512]{1,0:T(8,128)(2,1)S(1)} %collective-permute-done.20.refs_1_, ...), custom_call_target="tpu_custom_call" | custom-call | tf_op jit(solution)/shard_map/chunk/pallas_call | solution.py:394
  114.3 2.0 %collective-permute-done.24 = bf16[4,48,1536]{2,1,0:T(8,128)(2,1)S(1)} collective-permute-done((bf16[4,48,1536]{2,1,0:T(8,128)(2,1)S(1)}, bf16[4,48,1536]{2,1,0:T(8,128)(2,1)S(1)}, u32[]{:S(2)}, u32[]{:S(2)}) %collective-permute-start.24) | collective-permute-done | bytes 589856 | tf_op jit(solution)/shard_map/ppermute | solution.py:525
  116.5 1.6 %collective-permute-start.25 = (bf16[48,1536]{1,0:T(8,128)(2,1)S(1)}, bf16[48,1536]{1,0:T(8,128)(2,1)S(1)}, u32[]{:S(2)}, u32[]{:S(2)}) collective-permute-start(bf16[48,1536]{1,0:T(8,128)(2,1)S(1)} %get-tuple-element.86), channel_id=1, source_target_pairs={{0,2},{1,3},{2,0},{3,1},{4,6},{5,7},{6,4},{7,5},{8,10},{9,11},{10,... | collective-permute-start | bytes 442376 | tf_op jit(solution)/shard_map/ppermute | solution.py:529
  118.0 1.3 %collective-permute-start.26 = (bf16[48,1536]{1,0:T(8,128)(2,1)S(1)}, bf16[48,1536]{1,0:T(8,128)(2,1)S(1)}, u32[]{:S(2)}, u32[]{:S(2)}) collective-permute-start(bf16[48,1536]{1,0:T(8,128)(2,1)S(1)} %get-tuple-element.88), channel_id=1, source_target_pairs={{0,4},{1,5},{2,6},{3,7},{4,0},{5,1},{6,2},{7,3},{8,12},{9,13},{10,... | collective-permute-start | bytes 442376 | tf_op jit(solution)/shard_map/ppermute | solution.py:529
  119.3 0.7 collective-permute-start.27
  120.0 6.1 %down_grad.1 = bf16[2048,1536]{1,0:T(8,128)(2,1)} custom-call(s32[2]{0:T(128)S(1)} %pad_add_fusion.ids, bf16[288,2048]{1,0:T(8,128)(2,1)S(1)} %get-tuple-element.59.early, bf16[96,2048]{1,0:T(8,128)(2,1)S(1)} %get-tuple-element.85.late, bf16[384,1536]{1,0:T(8,128)(2,1)S(1)} %get-tuple-element.48.refs_0_.cotangent), custom_call_target="tpu_custom_call" | custom-call | flops 2415919104 | bytes 9043968 | tf_op jit(solution)/shard_map/down_grad/pallas_call | solution.py:295
  126.1 3.0 %gate_and_up_grad.1 = (bf16[1536,2048]{1,0:T(8,128)(2,1)}, bf16[1536,2048]{1,0:T(8,128)(2,1)}) custom-call(bf16[1536,384]{1,0:T(8,128)(2,1)S(1)} %inputs_transposed.1.refs_8_.refs_9_.inputs, bf16[384,512]{1,0:T(8,128)(2,1)S(1)} %get-tuple-element.79.gate_delta, ...), custom_call_target="tpu_custom_call", output_to_operand_aliasing={{0}: (3, {}), {1}: (4, {})} | custom-call | flops 1207959552 | bytes 5111808 | tf_op jit(solution)/shard_map/gate_and_up_grad/pallas_call | solution.py:430
  129.2 0.7 fusion.2
  (46 shorter events, 1.2 us)
Async XLA Ops:
  1.9 21.7 %collective-permute-start.7 = (bf16[192,2048]{1,0:T(8,128)(2,1)S(1)}, bf16[192,2048]{1,0:T(8,128)(2,1)}, u32[]{:S(2)}, u32[]{:S(2)}) collective-permute-start(bf16[192,2048]{1,0:T(8,128)(2,1)S(1)} %get-tuple-element.47.refs_0_), channel_id=1, source_target_pairs={{0,8},{24,16},{8,0},{16,24},{1,9},{25,17},{9,1},{17,25},{2,10},{26... | collective-permute-start | bytes 2359304 | tf_op jit(solution)/shard_map/ppermute | solution.py:55
  5.0 19.3 %collective-permute-start.8 = (bf16[192,2048]{1,0:T(8,128)(2,1)S(1)}, bf16[192,2048]{1,0:T(8,128)(2,1)}, u32[]{:S(2)}, u32[]{:S(2)}) collective-permute-start(bf16[192,2048]{1,0:T(8,128)(2,1)S(1)} %get-tuple-element.47.refs_0_), channel_id=1, source_target_pairs={{8,16},{16,8},{9,17},{17,9},{10,18},{18,10},{11,19},{19,11},{12,20... | collective-permute-start | bytes 2359304 | tf_op jit(solution)/shard_map/ppermute | solution.py:462
  6.5 0.9 copy-start
  7.4 8.5 %collective-permute-start.3 = (bf16[96,1536]{1,0:T(8,128)(2,1)S(1)}, bf16[96,1536]{1,0:T(8,128)(2,1)S(1)}, u32[]{:S(2)}, u32[]{:S(2)}) collective-permute-start(bf16[96,1536]{1,0:T(8,128)(2,1)S(1)} %get-tuple-element.45.refs_0_), channel_id=1, source_target_pairs={{0,4},{1,5},{2,6},{3,7},{4,0},{5,1},{6,2},{7,3},{8,12},{9,13},{10,... | collective-permute-start | bytes 884744 | tf_op jit(solution)/shard_map/ppermute | solution.py:86
  8.9 8.4 %collective-permute-start.1 = (bf16[96,1536]{1,0:T(8,128)(2,1)S(1)}, bf16[96,1536]{1,0:T(8,128)(2,1)S(1)}, u32[]{:S(2)}, u32[]{:S(2)}) collective-permute-start(bf16[96,1536]{1,0:T(8,128)(2,1)S(1)} %get-tuple-element.45.refs_0_), channel_id=1, source_target_pairs={{0,2},{1,3},{2,0},{3,1},{4,6},{5,7},{6,4},{7,5},{8,10},{9,11},{10,... | collective-permute-start | bytes 884744 | tf_op jit(solution)/shard_map/ppermute | solution.py:86
  10.4 7.0 %collective-permute-start = (bf16[96,1536]{1,0:T(8,128)(2,1)S(1)}, bf16[96,1536]{1,0:T(8,128)(2,1)S(1)}, u32[]{:S(2)}, u32[]{:S(2)}) collective-permute-start(bf16[96,1536]{1,0:T(8,128)(2,1)S(1)} %get-tuple-element.45.refs_0_), channel_id=1, source_target_pairs={{0,1},{1,0},{2,3},{3,2},{4,5},{5,4},{6,7},{7,6},{8,9},{9,8},{10,11... | collective-permute-start | bytes 884744 | tf_op jit(solution)/shard_map/ppermute | solution.py:86
  15.9 7.7 %collective-permute-start.5 = (bf16[96,1536]{1,0:T(8,128)(2,1)S(1)}, bf16[96,1536]{1,0:T(8,128)(2,1)S(1)}, u32[]{:S(2)}, u32[]{:S(2)}) collective-permute-start(bf16[96,1536]{1,0:T(8,128)(2,1)S(1)} %collective-permute-done.3.refs_4_), channel_id=1, source_target_pairs={{0,2},{1,3},{2,0},{3,1},{4,6},{5,7},{6,4},{7,5},{8,10},{9,11},{10,... | collective-permute-start | bytes 884744 | tf_op jit(solution)/shard_map/ppermute | solution.py:86
  17.4 8.3 %collective-permute-start.4 = (bf16[96,1536]{1,0:T(8,128)(2,1)S(1)}, bf16[96,1536]{1,0:T(8,128)(2,1)S(1)}, u32[]{:S(2)}, u32[]{:S(2)}) collective-permute-start(bf16[96,1536]{1,0:T(8,128)(2,1)S(1)} %collective-permute-done.3.refs_4_), channel_id=1, source_target_pairs={{0,1},{1,0},{2,3},{3,2},{4,5},{5,4},{6,7},{7,6},{8,9},{9,8},{10,11... | collective-permute-start | bytes 884744 | tf_op jit(solution)/shard_map/ppermute | solution.py:86
  17.4 8.3 %collective-permute-start.2 = (bf16[96,1536]{1,0:T(8,128)(2,1)S(1)}, bf16[96,1536]{1,0:T(8,128)(2,1)S(1)}, u32[]{:S(2)}, u32[]{:S(2)}) collective-permute-start(bf16[96,1536]{1,0:T(8,128)(2,1)S(1)} %collective-permute-done.1.refs_2_), channel_id=1, source_target_pairs={{0,1},{1,0},{2,3},{3,2},{4,5},{5,4},{6,7},{7,6},{8,9},{9,8},{10,11... | collective-permute-start | bytes 884744 | tf_op jit(solution)/shard_map/ppermute | solution.py:86
  23.5 2.1 %collective-permute-start.6 = (bf16[96,1536]{1,0:T(8,128)(2,1)S(1)}, bf16[96,1536]{1,0:T(8,128)(2,1)S(1)}, u32[]{:S(2)}, u32[]{:S(2)}) collective-permute-start(bf16[96,1536]{1,0:T(8,128)(2,1)S(1)} %collective-permute-done.5.refs_6_), channel_id=1, source_target_pairs={{0,1},{1,0},{2,3},{3,2},{4,5},{5,4},{6,7},{7,6},{8,9},{9,8},{10,11... | collective-permute-start | bytes 884744 | tf_op jit(solution)/shard_map/ppermute | solution.py:86
  23.5 26.7 %collective-permute-start.14 = (bf16[192,2048]{1,0:T(8,128)(2,1)}, bf16[192,2048]{1,0:T(8,128)(2,1)S(1)}, u32[]{:S(2)}, u32[]{:S(2)}) collective-permute-start(bf16[192,2048]{1,0:T(8,128)(2,1)} %collective-permute-done.7.refs_1_), channel_id=1, source_target_pairs={{8,16},{16,8},{9,17},{17,9},{10,18},{18,10},{11,19},{19,11},{12,20... | collective-permute-start | bytes 2359304 | tf_op jit(solution)/shard_map/ppermute | solution.py:462
  24.3 26.0 %collective-permute-start.15 = (bf16[192,2048]{1,0:T(8,128)(2,1)}, bf16[192,2048]{1,0:T(8,128)(2,1)}, u32[]{:S(2)}, u32[]{:S(2)}) collective-permute-start(bf16[192,2048]{1,0:T(8,128)(2,1)} %collective-permute-done.8.refs_2_), channel_id=1, source_target_pairs={{8,0},{16,24},{9,1},{17,25},{10,2},{18,26},{11,3},{19,27},{12,4},{... | collective-permute-start | bytes 2359304 | tf_op jit(solution)/shard_map/ppermute | solution.py:69
  28.4 33.1 %copy-start.1 = (bf16[192,2048]{1,0:T(8,128)(2,1)S(1)}, bf16[192,2048]{1,0:T(8,128)(2,1)}, u32[]{:S(2)}) copy-start(bf16[192,2048]{1,0:T(8,128)(2,1)} %copy-done) | copy-start | bytes 2359300
  28.4 16.4 %collective-permute-start.9 = (bf16[384,512]{1,0:T(8,128)(2,1)S(1)}, bf16[384,512]{1,0:T(8,128)(2,1)S(1)}, u32[]{:S(2)}, u32[]{:S(2)}) collective-permute-start(bf16[384,512]{1,0:T(8,128)(2,1)S(1)} %get-tuple-element.52), channel_id=1, source_target_pairs={{0,8},{24,16},{1,9},{25,17},{2,10},{26,18},{3,11},{27,19},{4,12},{... | collective-permute-start | bytes 1179656 | tf_op jit(solution)/shard_map/ppermute | solution.py:502
  36.1 50.8 %slice-start.2 = ((s8[6291456]{0:T(1024)(128)(4,1)}), s8[4194304]{0:T(1024)(128)(4,1)S(1)}, s32[]{:S(2)}) async-start(s8[6291456]{0:T(1024)(128)(4,1)} %bitcast.15), calls=%async_computation.2 | async-start | bytes 8388608
  44.8 12.3 %collective-permute-start.10 = (bf16[384,512]{1,0:T(8,128)(2,1)S(1)}, bf16[384,512]{1,0:T(8,128)(2,1)S(1)}, u32[]{:S(2)}, u32[]{:S(2)}) collective-permute-start(bf16[384,512]{1,0:T(8,128)(2,1)S(1)} %get-tuple-element.53), channel_id=1, source_target_pairs={{0,8},{24,16},{1,9},{25,17},{2,10},{26,18},{3,11},{27,19},{4,12},{... | collective-permute-start | bytes 1179656 | tf_op jit(solution)/shard_map/ppermute | solution.py:502
  49.2 37.7 %slice-start = ((s8[6291456]{0:T(1024)(128)(4,1)}), s8[4194304]{0:T(1024)(128)(4,1)S(1)}, s32[]{:S(2)}) async-start(s8[6291456]{0:T(1024)(128)(4,1)} %bitcast.13), calls=%async_computation | async-start | bytes 8388608
  50.3 36.7 %slice-start.3 = ((s8[6291456]{0:T(1024)(128)(4,1)}), s8[2097152]{0:T(1024)(128)(4,1)S(1)}, s32[]{:S(2)}) async-start(s8[6291456]{0:T(1024)(128)(4,1)} %bitcast.15), calls=%async_computation.3 | async-start | bytes 4194304
  50.3 23.5 %collective-permute-start.17 = (bf16[192,2048]{1,0:T(8,128)(2,1)S(1)}, bf16[192,2048]{1,0:T(8,128)(2,1)S(1)}, u32[]{:S(2)}, u32[]{:S(2)}) collective-permute-start(bf16[192,2048]{1,0:T(8,128)(2,1)S(1)} %collective-permute-done.14.refs_0_), channel_id=1, source_target_pairs={{8,0},{16,24},{9,1},{17,25},{10,2},{18,26},{11,3},{19,27},{12,4},{... | collective-permute-start | bytes 2359304 | tf_op jit(solution)/shard_map/ppermute | solution.py:69
  51.9 13.8 %collective-permute-start.16 = (bf16[384,512]{1,0:T(8,128)(2,1)S(1)}, bf16[384,512]{1,0:T(8,128)(2,1)S(1)}, u32[]{:S(2)}, u32[]{:S(2)}) collective-permute-start(bf16[384,512]{1,0:T(8,128)(2,1)S(1)} %add_convert_fusion.7), channel_id=1, source_target_pairs={{8,16},{16,8},{9,17},{17,9},{10,18},{18,10},{11,19},{19,11},{12,20... | collective-permute-start | bytes 1179656 | tf_op jit(solution)/shard_map/ppermute | solution.py:509
  57.1 11.4 %collective-permute-start.11 = (bf16[384,512]{1,0:T(8,128)(2,1)S(1)}, bf16[384,512]{1,0:T(8,128)(2,1)S(1)}, u32[]{:S(2)}, u32[]{:S(2)}) collective-permute-start(bf16[384,512]{1,0:T(8,128)(2,1)S(1)} %get-tuple-element.54), channel_id=1, source_target_pairs={{0,8},{24,16},{1,9},{25,17},{2,10},{26,18},{3,11},{27,19},{4,12},{... | collective-permute-start | bytes 1179656 | tf_op jit(solution)/shard_map/ppermute | solution.py:502
  65.7 21.3 %slice-start.1 = ((s8[6291456]{0:T(1024)(128)(4,1)}), s8[2097152]{0:T(1024)(128)(4,1)S(1)}, s32[]{:S(2)}) async-start(s8[6291456]{0:T(1024)(128)(4,1)} %bitcast.13), calls=%async_computation.1 | async-start | bytes 4194304
  65.8 14.0 %collective-permute-start.22 = (bf16[384,512]{1,0:T(8,128)(2,1)S(1)}, bf16[384,512]{1,0:T(8,128)(2,1)S(1)}, u32[]{:S(2)}, u32[]{:S(2)}) collective-permute-start(bf16[384,512]{1,0:T(8,128)(2,1)S(1)} %add_convert_fusion.2), channel_id=1, source_target_pairs={{8,16},{16,8},{9,17},{17,9},{10,18},{18,10},{11,19},{19,11},{12,20... | collective-permute-start | bytes 1179656 | tf_op jit(solution)/shard_map/ppermute | solution.py:509
  68.5 10.5 %collective-permute-start.12 = (bf16[384,512]{1,0:T(8,128)(2,1)S(1)}, bf16[384,512]{1,0:T(8,128)(2,1)S(1)}, u32[]{:S(2)}, u32[]{:S(2)}) collective-permute-start(bf16[384,512]{1,0:T(8,128)(2,1)S(1)} %get-tuple-element.55), channel_id=1, source_target_pairs={{0,8},{24,16},{1,9},{25,17},{2,10},{26,18},{3,11},{27,19},{4,12},{... | collective-permute-start | bytes 1179656 | tf_op jit(solution)/shard_map/ppermute | solution.py:502
  73.0 8.2 %collective-permute-start.19 = (bf16[384,512]{1,0:T(8,128)(2,1)S(1)}, bf16[384,512]{1,0:T(8,128)(2,1)S(1)}, u32[]{:S(2)}, u32[]{:S(2)}) collective-permute-start(bf16[384,512]{1,0:T(8,128)(2,1)S(1)} %add_convert_fusion.5), channel_id=1, source_target_pairs={{8,16},{16,8},{9,17},{17,9},{10,18},{18,10},{11,19},{19,11},{12,20... | collective-permute-start | bytes 1179656 | tf_op jit(solution)/shard_map/ppermute | solution.py:509
  75.2 11.8 %collective-permute-start.18 = (bf16[384,512]{1,0:T(8,128)(2,1)S(1)}, bf16[384,512]{1,0:T(8,128)(2,1)S(1)}, u32[]{:S(2)}, u32[]{:S(2)}) collective-permute-start(bf16[384,512]{1,0:T(8,128)(2,1)S(1)} %add_convert_fusion.6.refs_0_), channel_id=1, source_target_pairs={{8,0},{16,24},{9,1},{17,25},{10,2},{18,26},{11,3},{19,27},{12,4},{... | collective-permute-start | bytes 1179656 | tf_op jit(solution)/shard_map/ppermute | solution.py:69
  79.1 13.6 %collective-permute-start.13 = (bf16[384,512]{1,0:T(8,128)(2,1)S(1)}, bf16[384,512]{1,0:T(8,128)(2,1)S(1)}, u32[]{:S(2)}, u32[]{:S(2)}) collective-permute-start(bf16[384,512]{1,0:T(8,128)(2,1)S(1)} %add_convert_fusion.8), channel_id=1, source_target_pairs={{8,16},{16,8},{9,17},{17,9},{10,18},{18,10},{11,19},{19,11},{12,20... | collective-permute-start | bytes 1179656 | tf_op jit(solution)/shard_map/ppermute | solution.py:509
  79.9 16.6 %collective-permute-start.23 = (bf16[384,512]{1,0:T(8,128)(2,1)S(1)}, bf16[384,512]{1,0:T(8,128)(2,1)S(1)}, u32[]{:S(2)}, u32[]{:S(2)}) collective-permute-start(bf16[384,512]{1,0:T(8,128)(2,1)S(1)} %add_convert_fusion.1.refs_0_), channel_id=1, source_target_pairs={{8,0},{16,24},{9,1},{17,25},{10,2},{18,26},{11,3},{19,27},{12,4},{... | collective-permute-start | bytes 1179656 | tf_op jit(solution)/shard_map/ppermute | solution.py:69
  81.3 23.6 %collective-permute-start.21 = (bf16[384,512]{1,0:T(8,128)(2,1)S(1)}, bf16[384,512]{1,0:T(8,128)(2,1)S(1)}, u32[]{:S(2)}, u32[]{:S(2)}) collective-permute-start(bf16[384,512]{1,0:T(8,128)(2,1)S(1)} %add_convert_fusion.4.refs_0_), channel_id=1, source_target_pairs={{8,0},{16,24},{9,1},{17,25},{10,2},{18,26},{11,3},{19,27},{12,4},{... | collective-permute-start | bytes 1179656 | tf_op jit(solution)/shard_map/ppermute | solution.py:69
  92.8 18.1 %collective-permute-start.20 = (bf16[384,512]{1,0:T(8,128)(2,1)S(1)}, bf16[384,512]{1,0:T(8,128)(2,1)S(1)}, u32[]{:S(2)}, u32[]{:S(2)}) collective-permute-start(bf16[384,512]{1,0:T(8,128)(2,1)S(1)} %add_convert_fusion.3.refs_0_), channel_id=1, source_target_pairs={{8,0},{16,24},{9,1},{17,25},{10,2},{18,26},{11,3},{19,27},{12,4},{... | collective-permute-start | bytes 1179656 | tf_op jit(solution)/shard_map/ppermute | solution.py:69
  114.2 2.1 %collective-permute-start.24 = (bf16[4,48,1536]{2,1,0:T(8,128)(2,1)S(1)}, bf16[4,48,1536]{2,1,0:T(8,128)(2,1)S(1)}, u32[]{:S(2)}, u32[]{:S(2)}) collective-permute-start(bf16[4,48,1536]{2,1,0:T(8,128)(2,1)S(1)} %get-tuple-element.78), channel_id=1, source_target_pairs={{0,1},{1,0},{2,3},{3,2},{4,5},{5,4},{6,7},{7,6},{8,9},{9,8},{10,11... | collective-permute-start | bytes 1769480 | tf_op jit(solution)/shard_map/ppermute | solution.py:525
  116.5 12.7 %collective-permute-start.25 = (bf16[48,1536]{1,0:T(8,128)(2,1)S(1)}, bf16[48,1536]{1,0:T(8,128)(2,1)S(1)}, u32[]{:S(2)}, u32[]{:S(2)}) collective-permute-start(bf16[48,1536]{1,0:T(8,128)(2,1)S(1)} %get-tuple-element.86), channel_id=1, source_target_pairs={{0,2},{1,3},{2,0},{3,1},{4,6},{5,7},{6,4},{7,5},{8,10},{9,11},{10,... | collective-permute-start | bytes 442376 | tf_op jit(solution)/shard_map/ppermute | solution.py:529
  118.0 11.1 %collective-permute-start.26 = (bf16[48,1536]{1,0:T(8,128)(2,1)S(1)}, bf16[48,1536]{1,0:T(8,128)(2,1)S(1)}, u32[]{:S(2)}, u32[]{:S(2)}) collective-permute-start(bf16[48,1536]{1,0:T(8,128)(2,1)S(1)} %get-tuple-element.88), channel_id=1, source_target_pairs={{0,4},{1,5},{2,6},{3,7},{4,0},{5,1},{6,2},{7,3},{8,12},{9,13},{10,... | collective-permute-start | bytes 442376 | tf_op jit(solution)/shard_map/ppermute | solution.py:529
  119.3 9.8 %collective-permute-start.27 = (bf16[48,1536]{1,0:T(8,128)(2,1)S(1)}, bf16[48,1536]{1,0:T(8,128)(2,1)S(1)}, u32[]{:S(2)}, u32[]{:S(2)}) collective-permute-start(bf16[48,1536]{1,0:T(8,128)(2,1)S(1)} %get-tuple-element.87), channel_id=1, source_target_pairs={{0,6},{1,7},{2,4},{3,5},{4,2},{5,3},{6,0},{7,1},{8,14},{9,15},{10,... | collective-permute-start | bytes 442376 | tf_op jit(solution)/shard_map/ppermute | solution.py:529

commit v3 on v2

--- a/solution.py
+++ b/solution.py
@@ -279,7 +279,8 @@
     )(ids, *operands)
 
 
-def down_kernel(n, ids, early, late, cotangent, out, hidden):
+def down_kernel(n, ids, early, late, cotangent, *refs):
+    out, hidden = refs[-2:]
     rows = late.shape[0]
     for number, block in enumerate(row_blocks(ids[0], n)):
         source = late if number == n - 1 else early
@@ -288,32 +289,36 @@
     out[...] = contract(hidden[...], cotangent[...], 0, 0).astype(BF16)
 
 
-def down_grads(ids, early, late, cotangent, n):
+def down_grads(ids, early, late, cotangent, n, part, parts, before):
     total, depth = cotangent.shape
     width = late.shape[1]
-    tile = tile_of(width, 512)
+    tile = tile_of(width // parts, 512)
+    tiles = width // parts // tile
+    more, more_specs = filled(before)
     return pl.pallas_call(
         functools.partial(down_kernel, n),
         grid_spec=pltpu.PrefetchScalarGridSpec(
             num_scalar_prefetch=1,
-            grid=(width // tile,),
+            grid=(tiles,),
             in_specs=[
-                pl.BlockSpec((early.shape[0], tile), lambda j, *_: (0, j)),
-                pl.BlockSpec((late.shape[0], tile), lambda j, *_: (0, j)),
+                pl.BlockSpec((early.shape[0], tile), lambda j, *_: (0, part * tiles + j)),
+                pl.BlockSpec((late.shape[0], tile), lambda j, *_: (0, part * tiles + j)),
                 whole((total, depth)),
-            ],
-            out_specs=pl.BlockSpec((tile, depth), lambda j, *_: (j, 0)),
+            ]
+            + more_specs,
+            out_specs=pl.BlockSpec((tile, depth), lambda j, *_: (part * tiles + j, 0)),
             scratch_shapes=[pltpu.VMEM((total, tile), BF16)],
         ),
         out_shape=jax.ShapeDtypeStruct((width, depth), BF16),
+        input_output_aliases={4: 0} if more else {},
         compiler_params=pltpu.CompilerParams(vmem_limit_bytes=20 * MIB),
         cost_estimate=pl.CostEstimate(
-            flops=2 * total * depth * width,
-            bytes_accessed=2 * (width * depth + total * depth + total * width),
+            flops=2 * total * depth * width // parts,
+            bytes_accessed=2 * (width * depth // parts + total * depth + total * width // parts),
             transcendentals=0,
         ),
         name="down_grad",
-    )(ids, early, late, cotangent)
+    )(ids, early, late, cotangent, *more)
 
 
 def delta_kernel(n, n_col, first, last, ids, *refs):
@@ -498,7 +503,7 @@
     for chunk, held in enumerate(terms):
         for step in range(half - 1):
             if met is not None:
-                held = after(held, met)
+                held = after(held, met, *([inputs_t] if chunk == 1 else []))
             got = lax.ppermute(held, "row", inward([step], n_row))
             met = got
             if chunk == 0:
@@ -508,7 +513,10 @@
             held = after(held, crossed)
         got = crossed = lax.ppermute(held, "row", across(n_row))
         if chunk == CHUNKS - 1:
-            sent[0] = (sent[0][0], after(sent[0][1], sent[2][0]))
+            hidden = after(late[2], sent[2][0])
+            down_grad = down_grads(ids, early[2], hidden, tokens, n_row, 0, 2, None)
+            got_0, down_grad = lax.optimization_barrier((sent[0][1], down_grad))
+            sent[0] = (sent[0][0], got_0)
             running, weight_out = work_on(0, None, None)
             got, running, *weight_out = lax.optimization_barrier((got, running, *weight_out))
         elif chunk in before:
@@ -520,7 +528,8 @@
         running, weight_out = work_on(chunk, running, weight_out)
     gate_grad, up_grad = weight_out
     keep, send = running
-    down_grad = down_grads(ids, early[2], after(late[2], send), tokens, n_row)
+    hidden = after(late[2], send)
+    down_grad = down_grads(ids, early[2], hidden, tokens, n_row, 1, 2, [down_grad])
 
     keep = add(keep, lax.ppermute(send, "col", [(i, i ^ 1) for i in range(n_col)]))
     input_grad = keep[0].astype(F32)

time: 130 us -> 129 us (level)
  waiting for transfers between devices: 34.6 us -> 30.9 us
  Pallas kernels: 45.7 us -> 47.3 us
    ppermute x6, waiting for transfers between devices: 9.16 us -> 5.48 us  [sent_out(): got = lax.ppermute(block, 'row', outward([step], n))]
    pallas_call x1 -> x2, Pallas kernels: 6.08 us -> 7.74 us  [down_grads(): pl.pallas_call(functools.partial(down_kernel, n), grid_spec=pltpu.Prefetc...]
  transfers between devices with their start and end apart: 28 -> 28, of which waited for: 10 -> 11; matrix products, arithmetic and copies ran while one was open for 1% -> 1% of each run, Pallas kernels for 32% -> 33%
where the time goes in v3:
time: 129 us; the launch traced here: 128 us
  Pallas kernels  47.3 us (37%)
  starting transfers between devices  46 us (36%)
  waiting for transfers between devices  30.9 us (24%)
  other arithmetic  1.77 us (1%)
    ppermute x4, starting transfers between devices, on_device(): got = lax.ppermute(held, 'row', inward([step], n_row))  20.8 us
    pallas_call x4, Pallas kernels, deltas(): pl.pallas_call(functools.partial(delta_kernel, n, n_col, before is None,...  20.8 us
    ppermute x4, waiting for transfers between devices, on_device(): got = lax.ppermute(held, 'row', inward([step], n_row))  12.3 us
    ppermute x7, waiting for transfers between devices, cube_gather(): pieces[slot | bit] = lax.ppermute(pieces[slot], 'col', pairs)  11.1 us
    ppermute x6, starting transfers between devices, sent_out(): got = lax.ppermute(block, 'row', outward([step], n))  8.33 us
    pallas_call x2, Pallas kernels, partials(): pl.pallas_call(functools.partial(partial_kernel, len(pieces)), grid_spec=...  8.14 us
    pallas_call x2, Pallas kernels, down_grads(): pl.pallas_call(functools.partial(down_kernel, n), grid_spec=pltpu.Prefetc...  7.74 us
    ppermute x6, waiting for transfers between devices, sent_out(): got = lax.ppermute(block, 'row', outward([step], n))  5.48 us
  transfers between devices with their start and end apart: 28, of which 11 were waited for; matrix products, arithmetic and copies ran while one was open for 1% of the time, Pallas kernels for 33%

profile of v3, /device:TPU:0, one launch (start us, length us, event | category | flops | bytes accessed | tf_op | source)
XLA Modules:
  0.0 128.0 jit_solution(4799449369302228643)
XLA Ops:
  0.6 1.2 join.1
  1.9 3.1 %collective-permute-start.7 = (bf16[192,2048]{1,0:T(8,128)(2,1)S(1)}, bf16[192,2048]{1,0:T(8,128)(2,1)}, u32[]{:S(2)}, u32[]{:S(2)}) collective-permute-start(bf16[192,2048]{1,0:T(8,128)(2,1)S(1)} %get-tuple-element.49.refs_0_), channel_id=1, source_target_pairs={{0,8},{24,16},{8,0},{16,24},{1,9},{25,17},{9,1},{17,25},{2,10},{26... | collective-permute-start | bytes 2359304 | tf_op jit(solution)/shard_map/ppermute | solution.py:55
  5.0 1.6 %collective-permute-start.8 = (bf16[192,2048]{1,0:T(8,128)(2,1)S(1)}, bf16[192,2048]{1,0:T(8,128)(2,1)}, u32[]{:S(2)}, u32[]{:S(2)}) collective-permute-start(bf16[192,2048]{1,0:T(8,128)(2,1)S(1)} %get-tuple-element.49.refs_0_), channel_id=1, source_target_pairs={{8,16},{16,8},{9,17},{17,9},{10,18},{18,10},{11,19},{19,11},{12,20... | collective-permute-start | bytes 2359304 | tf_op jit(solution)/shard_map/ppermute | solution.py:467
  6.5 0.9 copy-done
  7.4 1.5 %collective-permute-start.3 = (bf16[96,1536]{1,0:T(8,128)(2,1)S(1)}, bf16[96,1536]{1,0:T(8,128)(2,1)S(1)}, u32[]{:S(2)}, u32[]{:S(2)}) collective-permute-start(bf16[96,1536]{1,0:T(8,128)(2,1)S(1)} %get-tuple-element.47.refs_0_), channel_id=1, source_target_pairs={{0,4},{1,5},{2,6},{3,7},{4,0},{5,1},{6,2},{7,3},{8,12},{9,13},{10,... | collective-permute-start | bytes 884744 | tf_op jit(solution)/shard_map/ppermute | solution.py:86
  8.9 1.5 %collective-permute-start.1 = (bf16[96,1536]{1,0:T(8,128)(2,1)S(1)}, bf16[96,1536]{1,0:T(8,128)(2,1)S(1)}, u32[]{:S(2)}, u32[]{:S(2)}) collective-permute-start(bf16[96,1536]{1,0:T(8,128)(2,1)S(1)} %get-tuple-element.47.refs_0_), channel_id=1, source_target_pairs={{0,2},{1,3},{2,0},{3,1},{4,6},{5,7},{6,4},{7,5},{8,10},{9,11},{10,... | collective-permute-start | bytes 884744 | tf_op jit(solution)/shard_map/ppermute | solution.py:86
  10.4 5.5 %collective-permute-done.3.refs_4_ = bf16[96,1536]{1,0:T(8,128)(2,1)S(1)} collective-permute-done((bf16[96,1536]{1,0:T(8,128)(2,1)S(1)}, bf16[96,1536]{1,0:T(8,128)(2,1)S(1)}, u32[]{:S(2)}, u32[]{:S(2)}) %collective-permute-start.3) | collective-permute-done | bytes 294944 | tf_op jit(solution)/shard_map/ppermute | solution.py:86
  15.9 1.5 %collective-permute-start.5 = (bf16[96,1536]{1,0:T(8,128)(2,1)S(1)}, bf16[96,1536]{1,0:T(8,128)(2,1)S(1)}, u32[]{:S(2)}, u32[]{:S(2)}) collective-permute-start(bf16[96,1536]{1,0:T(8,128)(2,1)S(1)} %collective-permute-done.3.refs_4_), channel_id=1, source_target_pairs={{0,2},{1,3},{2,0},{3,1},{4,6},{5,7},{6,4},{7,5},{8,10},{9,11},{10,... | collective-permute-start | bytes 884744 | tf_op jit(solution)/shard_map/ppermute | solution.py:86
  17.9 5.7 %collective-permute-done.5.refs_6_ = bf16[96,1536]{1,0:T(8,128)(2,1)S(1)} collective-permute-done((bf16[96,1536]{1,0:T(8,128)(2,1)S(1)}, bf16[96,1536]{1,0:T(8,128)(2,1)S(1)}, u32[]{:S(2)}, u32[]{:S(2)}) %collective-permute-start.5) | collective-permute-done | bytes 294944 | tf_op jit(solution)/shard_map/ppermute | solution.py:86
  23.5 0.7 collective-permute-start.14
  24.3 1.3 %collective-permute-start.15 = (bf16[192,2048]{1,0:T(8,128)(2,1)}, bf16[192,2048]{1,0:T(8,128)(2,1)}, u32[]{:S(2)}, u32[]{:S(2)}) collective-permute-start(bf16[192,2048]{1,0:T(8,128)(2,1)} %collective-permute-done.8.refs_2_), channel_id=1, source_target_pairs={{8,0},{16,24},{9,1},{17,25},{10,2},{18,26},{11,3},{19,27},{12,4},{... | collective-permute-start | bytes 2359304 | tf_op jit(solution)/shard_map/ppermute | solution.py:69
  25.6 2.8 %hidden_grad_partials.2 = (bf16[384,512]{1,0:T(8,128)(2,1)S(1)}, bf16[384,1536]{1,0:T(8,128)(2,1)S(1)}) custom-call(s32[2]{0:T(128)S(1)} %pad_add_fusion.ids, bf16[96,1536]{1,0:T(8,128)(2,1)S(1)} %get-tuple-element.47.refs_0_, bf16[96,1536]{1,0:T(8,128)(2,1)S(1)} %collective-permute-done.refs_1_, bf16[96,1536]{1,0:T(8,128)(2,1)S(1)} %collective-permute-done.1.refs_2_, ...), custom_call_target="tpu_custom_call" | custom-call | flops 603979776 | bytes 3145728 | tf_op jit(solution)/shard_map/hidden_grad_partials/pallas_call | solution.py:193
  28.4 7.7 %collective-permute-start.9 = (bf16[384,512]{1,0:T(8,128)(2,1)S(1)}, bf16[384,512]{1,0:T(8,128)(2,1)S(1)}, u32[]{:S(2)}, u32[]{:S(2)}) collective-permute-start(bf16[384,512]{1,0:T(8,128)(2,1)S(1)} %get-tuple-element.54), channel_id=1, source_target_pairs={{0,8},{24,16},{1,9},{25,17},{2,10},{26,18},{3,11},{27,19},{4,12},{... | collective-permute-start | bytes 1179656 | tf_op jit(solution)/shard_map/ppermute | solution.py:507
  36.1 1.0 inputs_transposed.1.refs_8_.refs_9_.inputs
  37.1 5.4 %hidden_grad_partials.3 = (bf16[384,512]{1,0:T(8,128)(2,1)S(1)}, bf16[384,512]{1,0:T(8,128)(2,1)S(1)}, bf16[384,512]{1,0:T(8,128)(2,1)S(1)}) custom-call(s32[2]{0:T(128)S(1)} %pad_add_fusion.ids, bf16[384,1536]{1,0:T(8,128)(2,1)S(1)} %get-tuple-element.50.refs_0_.cotangent, bf16[2048,1536]{1,0:T(8,128)(2,1)} %refs_1_.3), custom_call_target="tpu_custom_call" | custom-call | flops 1811939328 | bytes 7077888 | tf_op jit(solution)/shard_map/hidden_grad_partials/pallas_call | solution.py:193
  42.5 2.4 %collective-permute-done.9 = bf16[384,512]{1,0:T(8,128)(2,1)S(1)} collective-permute-done((bf16[384,512]{1,0:T(8,128)(2,1)S(1)}, bf16[384,512]{1,0:T(8,128)(2,1)S(1)}, u32[]{:S(2)}, u32[]{:S(2)}) %collective-permute-start.9) | collective-permute-done | bytes 393248 | tf_op jit(solution)/shard_map/ppermute | solution.py:507
  44.8 4.4 %collective-permute-start.10 = (bf16[384,512]{1,0:T(8,128)(2,1)S(1)}, bf16[384,512]{1,0:T(8,128)(2,1)S(1)}, u32[]{:S(2)}, u32[]{:S(2)}) collective-permute-start(bf16[384,512]{1,0:T(8,128)(2,1)S(1)} %get-tuple-element.55), channel_id=1, source_target_pairs={{0,8},{24,16},{1,9},{25,17},{2,10},{26,18},{3,11},{27,19},{4,12},{... | collective-permute-start | bytes 1179656 | tf_op jit(solution)/shard_map/ppermute | solution.py:507
  49.3 1.3 %collective-permute-start.17 = (bf16[192,2048]{1,0:T(8,128)(2,1)S(1)}, bf16[192,2048]{1,0:T(8,128)(2,1)S(1)}, u32[]{:S(2)}, u32[]{:S(2)}) collective-permute-start(bf16[192,2048]{1,0:T(8,128)(2,1)S(1)} %collective-permute-done.14.refs_0_), channel_id=1, source_target_pairs={{8,0},{16,24},{9,1},{17,25},{10,2},{18,26},{11,3},{19,27},{12,4},{... | collective-permute-start | bytes 2359304 | tf_op jit(solution)/shard_map/ppermute | solution.py:69
  50.7 0.7 collective-permute-start.16
  51.4 5.8 %collective-permute-done.10 = bf16[384,512]{1,0:T(8,128)(2,1)S(1)} collective-permute-done((bf16[384,512]{1,0:T(8,128)(2,1)S(1)}, bf16[384,512]{1,0:T(8,128)(2,1)S(1)}, u32[]{:S(2)}, u32[]{:S(2)}) %collective-permute-start.10) | collective-permute-done | bytes 393248 | tf_op jit(solution)/shard_map/ppermute | solution.py:507
  57.1 4.4 %collective-permute-start.11 = (bf16[384,512]{1,0:T(8,128)(2,1)S(1)}, bf16[384,512]{1,0:T(8,128)(2,1)S(1)}, u32[]{:S(2)}, u32[]{:S(2)}) collective-permute-start(bf16[384,512]{1,0:T(8,128)(2,1)S(1)} %get-tuple-element.56), channel_id=1, source_target_pairs={{0,8},{24,16},{1,9},{25,17},{2,10},{26,18},{3,11},{27,19},{4,12},{... | collective-permute-start | bytes 1179656 | tf_op jit(solution)/shard_map/ppermute | solution.py:507
  61.6 4.1 %factors.2 = (bf16[288,2048]{1,0:T(8,128)(2,1)S(1)}, bf16[288,2048]{1,0:T(8,128)(2,1)S(1)}, bf16[288,2048]{1,0:T(8,128)(2,1)S(1)}) custom-call(s32[2]{0:T(128)S(1)} %pad_add_fusion.ids, bf16[192,2048]{1,0:T(8,128)(2,1)S(1)} %copy-done.1, bf16[192,2048]{1,0:T(8,128)(2,1)} %collective-permute-done.7.refs_1_, bf16[192,2048]{1,0:T(8,128)(2,1)} %collective-permute-done.8.refs_2_, ...), custom_call_target="tpu_custom_call" | custom-call | flops 5898240 | bytes 5898240 | tf_op jit(solution)/shard_map/factors/pallas_call | solution.py:262
  65.8 0.7 collective-permute-start.22
  66.5 2.1 %collective-permute-done.11 = bf16[384,512]{1,0:T(8,128)(2,1)S(1)} collective-permute-done((bf16[384,512]{1,0:T(8,128)(2,1)S(1)}, bf16[384,512]{1,0:T(8,128)(2,1)S(1)}, u32[]{:S(2)}, u32[]{:S(2)}) %collective-permute-start.11) | collective-permute-done | bytes 393248 | tf_op jit(solution)/shard_map/ppermute | solution.py:507
  68.5 4.4 %collective-permute-start.12 = (bf16[384,512]{1,0:T(8,128)(2,1)S(1)}, bf16[384,512]{1,0:T(8,128)(2,1)S(1)}, u32[]{:S(2)}, u32[]{:S(2)}) collective-permute-start(bf16[384,512]{1,0:T(8,128)(2,1)S(1)} %get-tuple-element.57), channel_id=1, source_target_pairs={{0,8},{24,16},{1,9},{25,17},{2,10},{26,18},{3,11},{27,19},{4,12},{... | collective-permute-start | bytes 1179656 | tf_op jit(solution)/shard_map/ppermute | solution.py:507
  73.1 0.8 collective-permute-start.19
  73.9 1.3 %factors.3 = (bf16[96,2048]{1,0:T(8,128)(2,1)S(1)}, bf16[96,2048]{1,0:T(8,128)(2,1)S(1)}, bf16[96,2048]{1,0:T(8,128)(2,1)S(1)}) custom-call(s32[2]{0:T(128)S(1)} %pad_add_fusion.ids, bf16[192,2048]{1,0:T(8,128)(2,1)S(1)} %collective-permute-done.14.refs_0_, bf16[192,2048]{1,0:T(8,128)(2,1)S(1)} %collective-permute-done.17.refs_1_), custom_call_target="tpu_custom_call" | custom-call | flops 1966080 | bytes 15728640 | tf_op jit(solution)/shard_map/factors/pallas_call | solution.py:262
  75.3 1.6 %collective-permute-start.18 = (bf16[384,512]{1,0:T(8,128)(2,1)S(1)}, bf16[384,512]{1,0:T(8,128)(2,1)S(1)}, u32[]{:S(2)}, u32[]{:S(2)}) collective-permute-start(bf16[384,512]{1,0:T(8,128)(2,1)S(1)} %add_convert_fusion.6.refs_0_), channel_id=1, source_target_pairs={{8,0},{16,24},{9,1},{17,25},{10,2},{18,26},{11,3},{19,27},{12,4},{... | collective-permute-start | bytes 1179656 | tf_op jit(solution)/shard_map/ppermute | solution.py:69
  76.9 2.1 %collective-permute-done.12 = bf16[384,512]{1,0:T(8,128)(2,1)S(1)} collective-permute-done((bf16[384,512]{1,0:T(8,128)(2,1)S(1)}, bf16[384,512]{1,0:T(8,128)(2,1)S(1)}, u32[]{:S(2)}, u32[]{:S(2)}) %collective-permute-start.12) | collective-permute-done | bytes 393248 | tf_op jit(solution)/shard_map/ppermute | solution.py:507
  79.1 0.7 collective-permute-start.13
  79.9 1.3 %collective-permute-start.23 = (bf16[384,512]{1,0:T(8,128)(2,1)S(1)}, bf16[384,512]{1,0:T(8,128)(2,1)S(1)}, u32[]{:S(2)}, u32[]{:S(2)}) collective-permute-start(bf16[384,512]{1,0:T(8,128)(2,1)S(1)} %add_convert_fusion.1.refs_0_), channel_id=1, source_target_pairs={{8,0},{16,24},{9,1},{17,25},{10,2},{18,26},{11,3},{19,27},{12,4},{... | collective-permute-start | bytes 1179656 | tf_op jit(solution)/shard_map/ppermute | solution.py:69
  81.3 1.4 %collective-permute-start.21 = (bf16[384,512]{1,0:T(8,128)(2,1)S(1)}, bf16[384,512]{1,0:T(8,128)(2,1)S(1)}, u32[]{:S(2)}, u32[]{:S(2)}) collective-permute-start(bf16[384,512]{1,0:T(8,128)(2,1)S(1)} %add_convert_fusion.4.refs_0_), channel_id=1, source_target_pairs={{8,0},{16,24},{9,1},{17,25},{10,2},{18,26},{11,3},{19,27},{12,4},{... | collective-permute-start | bytes 1179656 | tf_op jit(solution)/shard_map/ppermute | solution.py:69
  82.8 3.9 %down_grad.2.refs_0_ = bf16[2048,1536]{1,0:T(8,128)(2,1)} custom-call(s32[2]{0:T(128)S(1)} %pad_add_fusion.ids, bf16[288,2048]{1,0:T(8,128)(2,1)S(1)} %get-tuple-element.61.early, bf16[96,2048]{1,0:T(8,128)(2,1)S(1)} %get-tuple-element.88.late, bf16[384,1536]{1,0:T(8,128)(2,1)S(1)} %get-tuple-element.50.refs_0_.cotangent), custom_call_target="tpu_custom_call" | custom-call | flops 1207959552 | bytes 5111808 | tf_op jit(solution)/shard_map/down_grad/pallas_call | solution.py:298
  86.6 1.4 %collective-permute-done.18.refs_1_ = bf16[384,512]{1,0:T(8,128)(2,1)S(1)} collective-permute-done((bf16[384,512]{1,0:T(8,128)(2,1)S(1)}, bf16[384,512]{1,0:T(8,128)(2,1)S(1)}, u32[]{:S(2)}, u32[]{:S(2)}) %collective-permute-start.18) | collective-permute-done | bytes 393248 | tf_op jit(solution)/shard_map/ppermute | solution.py:69
  88.1 5.7 %chunk.4 = (f32[384,1536]{1,0:T(8,128)S(1)}, bf16[1536,2048]{1,0:T(8,128)(2,1)}, bf16[1536,2048]{1,0:T(8,128)(2,1)}) custom-call(s32[2]{0:T(128)S(1)} %pad_add_fusion.ids, bf16[384,512]{1,0:T(8,128)(2,1)S(1)} %add_convert_fusion.6.refs_0_, bf16[384,512]{1,0:T(8,128)(2,1)S(1)} %collective-permute-done.18.refs_1_, ...), custom_call_target="tpu_custom_call" | custom-call | tf_op jit(solution)/shard_map/chunk/pallas_call | solution.py:399
  93.9 1.5 %collective-permute-start.20 = (bf16[384,512]{1,0:T(8,128)(2,1)S(1)}, bf16[384,512]{1,0:T(8,128)(2,1)S(1)}, u32[]{:S(2)}, u32[]{:S(2)}) collective-permute-start(bf16[384,512]{1,0:T(8,128)(2,1)S(1)} %add_convert_fusion.3.refs_0_), channel_id=1, source_target_pairs={{8,0},{16,24},{9,1},{17,25},{10,2},{18,26},{11,3},{19,27},{12,4},{... | collective-permute-start | bytes 1179656 | tf_op jit(solution)/shard_map/ppermute | solution.py:69
  95.4 1.2 collective-permute-done.23.refs_1_
  96.6 5.9 %chunk.5 = (f32[384,1536]{1,0:T(8,128)S(1)}, bf16[1536,2048]{1,0:T(8,128)(2,1)}, bf16[1536,2048]{1,0:T(8,128)(2,1)}) custom-call(s32[2]{0:T(128)S(1)} %pad_add_fusion.ids, bf16[384,512]{1,0:T(8,128)(2,1)S(1)} %add_convert_fusion.1.refs_0_, bf16[384,512]{1,0:T(8,128)(2,1)S(1)} %collective-permute-done.23.refs_1_, ...), custom_call_target="tpu_custom_call", output_to_operand_aliasing={{1}: (11, {}), {2}: (12, {})} | custom-call | tf_op jit(solution)/shard_map/chunk/pallas_call | solution.py:399
  102.4 2.5 %collective-permute-done.21.refs_1_ = bf16[384,512]{1,0:T(8,128)(2,1)S(1)} collective-permute-done((bf16[384,512]{1,0:T(8,128)(2,1)S(1)}, bf16[384,512]{1,0:T(8,128)(2,1)S(1)}, u32[]{:S(2)}, u32[]{:S(2)}) %collective-permute-start.21) | collective-permute-done | bytes 393248 | tf_op jit(solution)/shard_map/ppermute | solution.py:69
  105.0 5.9 %chunk.6 = (f32[384,1536]{1,0:T(8,128)S(1)}, bf16[1536,2048]{1,0:T(8,128)(2,1)}, bf16[1536,2048]{1,0:T(8,128)(2,1)}) custom-call(s32[2]{0:T(128)S(1)} %pad_add_fusion.ids, bf16[384,512]{1,0:T(8,128)(2,1)S(1)} %add_convert_fusion.4.refs_0_, bf16[384,512]{1,0:T(8,128)(2,1)S(1)} %collective-permute-done.21.refs_1_, ...), custom_call_target="tpu_custom_call", output_to_operand_aliasing={{1}: (11, {}), {2}: (12, {})} | custom-call | tf_op jit(solution)/shard_map/chunk/pallas_call | solution.py:399
  111.2 3.3 %chunk.7 = (bf16[384,512]{1,0:T(8,128)(2,1)S(1)}, bf16[384,512]{1,0:T(8,128)(2,1)S(1)}, bf16[4,48,1536]{2,1,0:T(8,128)(2,1)S(1)}, bf16[4,48,1536]{2,1,0:T(8,128)(2,1)S(1)}) custom-call(s32[2]{0:T(128)S(1)} %pad_add_fusion.ids, bf16[384,512]{1,0:T(8,128)(2,1)S(1)} %add_convert_fusion.3.refs_0_, bf16[384,512]{1,0:T(8,128)(2,1)S(1)} %collective-permute-done.20.refs_1_, ...), custom_call_target="tpu_custom_call" | custom-call | tf_op jit(solution)/shard_map/chunk/pallas_call | solution.py:399
  114.6 2.0 %collective-permute-done.24 = bf16[4,48,1536]{2,1,0:T(8,128)(2,1)S(1)} collective-permute-done((bf16[4,48,1536]{2,1,0:T(8,128)(2,1)S(1)}, bf16[4,48,1536]{2,1,0:T(8,128)(2,1)S(1)}, u32[]{:S(2)}, u32[]{:S(2)}) %collective-permute-start.24) | collective-permute-done | bytes 589856 | tf_op jit(solution)/shard_map/ppermute | solution.py:534
  116.8 1.6 %collective-permute-start.25 = (bf16[48,1536]{1,0:T(8,128)(2,1)S(1)}, bf16[48,1536]{1,0:T(8,128)(2,1)S(1)}, u32[]{:S(2)}, u32[]{:S(2)}) collective-permute-start(bf16[48,1536]{1,0:T(8,128)(2,1)S(1)} %get-tuple-element.90), channel_id=1, source_target_pairs={{0,2},{1,3},{2,0},{3,1},{4,6},{5,7},{6,4},{7,5},{8,10},{9,11},{10,... | collective-permute-start | bytes 442376 | tf_op jit(solution)/shard_map/ppermute | solution.py:538
  118.3 1.4 %collective-permute-start.26 = (bf16[48,1536]{1,0:T(8,128)(2,1)S(1)}, bf16[48,1536]{1,0:T(8,128)(2,1)S(1)}, u32[]{:S(2)}, u32[]{:S(2)}) collective-permute-start(bf16[48,1536]{1,0:T(8,128)(2,1)S(1)} %get-tuple-element.92), channel_id=1, source_target_pairs={{0,4},{1,5},{2,6},{3,7},{4,0},{5,1},{6,2},{7,3},{8,12},{9,13},{10,... | collective-permute-start | bytes 442376 | tf_op jit(solution)/shard_map/ppermute | solution.py:538
  119.8 0.6 collective-permute-start.27
  120.3 3.9 %down_grad.3 = bf16[2048,1536]{1,0:T(8,128)(2,1)} custom-call(s32[2]{0:T(128)S(1)} %pad_add_fusion.ids, bf16[288,2048]{1,0:T(8,128)(2,1)S(1)} %get-tuple-element.61.early, bf16[96,2048]{1,0:T(8,128)(2,1)S(1)} %get-tuple-element.88.late, bf16[384,1536]{1,0:T(8,128)(2,1)S(1)} %get-tuple-element.50.refs_0_.cotangent, ...), custom_call_target="tpu_custom_call", output_to_operand_aliasing={{}: (4, {})} | custom-call | flops 1207959552 | bytes 5111808 | tf_op jit(solution)/shard_map/down_grad/pallas_call | solution.py:298
  124.2 3.1 %gate_and_up_grad.1 = (bf16[1536,2048]{1,0:T(8,128)(2,1)}, bf16[1536,2048]{1,0:T(8,128)(2,1)}) custom-call(bf16[1536,384]{1,0:T(8,128)(2,1)S(1)} %inputs_transposed.1.refs_8_.refs_9_.inputs, bf16[384,512]{1,0:T(8,128)(2,1)S(1)} %get-tuple-element.82.gate_delta, ...), custom_call_target="tpu_custom_call", output_to_operand_aliasing={{0}: (3, {}), {1}: (4, {})} | custom-call | flops 1207959552 | bytes 5111808 | tf_op jit(solution)/shard_map/gate_and_up_grad/pallas_call | solution.py:435
  127.3 0.7 fusion.2
  (47 shorter events, 2.1 us)
Async XLA Ops:
  1.9 21.7 %collective-permute-start.7 = (bf16[192,2048]{1,0:T(8,128)(2,1)S(1)}, bf16[192,2048]{1,0:T(8,128)(2,1)}, u32[]{:S(2)}, u32[]{:S(2)}) collective-permute-start(bf16[192,2048]{1,0:T(8,128)(2,1)S(1)} %get-tuple-element.49.refs_0_), channel_id=1, source_target_pairs={{0,8},{24,16},{8,0},{16,24},{1,9},{25,17},{9,1},{17,25},{2,10},{26... | collective-permute-start | bytes 2359304 | tf_op jit(solution)/shard_map/ppermute | solution.py:55
  5.0 19.3 %collective-permute-start.8 = (bf16[192,2048]{1,0:T(8,128)(2,1)S(1)}, bf16[192,2048]{1,0:T(8,128)(2,1)}, u32[]{:S(2)}, u32[]{:S(2)}) collective-permute-start(bf16[192,2048]{1,0:T(8,128)(2,1)S(1)} %get-tuple-element.49.refs_0_), channel_id=1, source_target_pairs={{8,16},{16,8},{9,17},{17,9},{10,18},{18,10},{11,19},{19,11},{12,20... | collective-permute-start | bytes 2359304 | tf_op jit(solution)/shard_map/ppermute | solution.py:467
  6.5 0.9 copy-start
  7.4 8.5 %collective-permute-start.3 = (bf16[96,1536]{1,0:T(8,128)(2,1)S(1)}, bf16[96,1536]{1,0:T(8,128)(2,1)S(1)}, u32[]{:S(2)}, u32[]{:S(2)}) collective-permute-start(bf16[96,1536]{1,0:T(8,128)(2,1)S(1)} %get-tuple-element.47.refs_0_), channel_id=1, source_target_pairs={{0,4},{1,5},{2,6},{3,7},{4,0},{5,1},{6,2},{7,3},{8,12},{9,13},{10,... | collective-permute-start | bytes 884744 | tf_op jit(solution)/shard_map/ppermute | solution.py:86
  8.9 8.4 %collective-permute-start.1 = (bf16[96,1536]{1,0:T(8,128)(2,1)S(1)}, bf16[96,1536]{1,0:T(8,128)(2,1)S(1)}, u32[]{:S(2)}, u32[]{:S(2)}) collective-permute-start(bf16[96,1536]{1,0:T(8,128)(2,1)S(1)} %get-tuple-element.47.refs_0_), channel_id=1, source_target_pairs={{0,2},{1,3},{2,0},{3,1},{4,6},{5,7},{6,4},{7,5},{8,10},{9,11},{10,... | collective-permute-start | bytes 884744 | tf_op jit(solution)/shard_map/ppermute | solution.py:86
  10.4 7.0 %collective-permute-start = (bf16[96,1536]{1,0:T(8,128)(2,1)S(1)}, bf16[96,1536]{1,0:T(8,128)(2,1)S(1)}, u32[]{:S(2)}, u32[]{:S(2)}) collective-permute-start(bf16[96,1536]{1,0:T(8,128)(2,1)S(1)} %get-tuple-element.47.refs_0_), channel_id=1, source_target_pairs={{0,1},{1,0},{2,3},{3,2},{4,5},{5,4},{6,7},{7,6},{8,9},{9,8},{10,11... | collective-permute-start | bytes 884744 | tf_op jit(solution)/shard_map/ppermute | solution.py:86
  15.9 7.7 %collective-permute-start.5 = (bf16[96,1536]{1,0:T(8,128)(2,1)S(1)}, bf16[96,1536]{1,0:T(8,128)(2,1)S(1)}, u32[]{:S(2)}, u32[]{:S(2)}) collective-permute-start(bf16[96,1536]{1,0:T(8,128)(2,1)S(1)} %collective-permute-done.3.refs_4_), channel_id=1, source_target_pairs={{0,2},{1,3},{2,0},{3,1},{4,6},{5,7},{6,4},{7,5},{8,10},{9,11},{10,... | collective-permute-start | bytes 884744 | tf_op jit(solution)/shard_map/ppermute | solution.py:86
  17.4 8.3 %collective-permute-start.4 = (bf16[96,1536]{1,0:T(8,128)(2,1)S(1)}, bf16[96,1536]{1,0:T(8,128)(2,1)S(1)}, u32[]{:S(2)}, u32[]{:S(2)}) collective-permute-start(bf16[96,1536]{1,0:T(8,128)(2,1)S(1)} %collective-permute-done.3.refs_4_), channel_id=1, source_target_pairs={{0,1},{1,0},{2,3},{3,2},{4,5},{5,4},{6,7},{7,6},{8,9},{9,8},{10,11... | collective-permute-start | bytes 884744 | tf_op jit(solution)/shard_map/ppermute | solution.py:86
  17.4 8.3 %collective-permute-start.2 = (bf16[96,1536]{1,0:T(8,128)(2,1)S(1)}, bf16[96,1536]{1,0:T(8,128)(2,1)S(1)}, u32[]{:S(2)}, u32[]{:S(2)}) collective-permute-start(bf16[96,1536]{1,0:T(8,128)(2,1)S(1)} %collective-permute-done.1.refs_2_), channel_id=1, source_target_pairs={{0,1},{1,0},{2,3},{3,2},{4,5},{5,4},{6,7},{7,6},{8,9},{9,8},{10,11... | collective-permute-start | bytes 884744 | tf_op jit(solution)/shard_map/ppermute | solution.py:86
  23.5 2.1 %collective-permute-start.6 = (bf16[96,1536]{1,0:T(8,128)(2,1)S(1)}, bf16[96,1536]{1,0:T(8,128)(2,1)S(1)}, u32[]{:S(2)}, u32[]{:S(2)}) collective-permute-start(bf16[96,1536]{1,0:T(8,128)(2,1)S(1)} %collective-permute-done.5.refs_6_), channel_id=1, source_target_pairs={{0,1},{1,0},{2,3},{3,2},{4,5},{5,4},{6,7},{7,6},{8,9},{9,8},{10,11... | collective-permute-start | bytes 884744 | tf_op jit(solution)/shard_map/ppermute | solution.py:86
  23.5 25.7 %collective-permute-start.14 = (bf16[192,2048]{1,0:T(8,128)(2,1)}, bf16[192,2048]{1,0:T(8,128)(2,1)S(1)}, u32[]{:S(2)}, u32[]{:S(2)}) collective-permute-start(bf16[192,2048]{1,0:T(8,128)(2,1)} %collective-permute-done.7.refs_1_), channel_id=1, source_target_pairs={{8,16},{16,8},{9,17},{17,9},{10,18},{18,10},{11,19},{19,11},{12,20... | collective-permute-start | bytes 2359304 | tf_op jit(solution)/shard_map/ppermute | solution.py:467
  24.3 25.0 %collective-permute-start.15 = (bf16[192,2048]{1,0:T(8,128)(2,1)}, bf16[192,2048]{1,0:T(8,128)(2,1)}, u32[]{:S(2)}, u32[]{:S(2)}) collective-permute-start(bf16[192,2048]{1,0:T(8,128)(2,1)} %collective-permute-done.8.refs_2_), channel_id=1, source_target_pairs={{8,0},{16,24},{9,1},{17,25},{10,2},{18,26},{11,3},{19,27},{12,4},{... | collective-permute-start | bytes 2359304 | tf_op jit(solution)/shard_map/ppermute | solution.py:69
  28.4 33.1 %copy-start.1 = (bf16[192,2048]{1,0:T(8,128)(2,1)S(1)}, bf16[192,2048]{1,0:T(8,128)(2,1)}, u32[]{:S(2)}) copy-start(bf16[192,2048]{1,0:T(8,128)(2,1)} %copy-done) | copy-start | bytes 2359300
  28.4 16.4 %collective-permute-start.9 = (bf16[384,512]{1,0:T(8,128)(2,1)S(1)}, bf16[384,512]{1,0:T(8,128)(2,1)S(1)}, u32[]{:S(2)}, u32[]{:S(2)}) collective-permute-start(bf16[384,512]{1,0:T(8,128)(2,1)S(1)} %get-tuple-element.54), channel_id=1, source_target_pairs={{0,8},{24,16},{1,9},{25,17},{2,10},{26,18},{3,11},{27,19},{4,12},{... | collective-permute-start | bytes 1179656 | tf_op jit(solution)/shard_map/ppermute | solution.py:507
  37.1 50.9 %slice-start.2 = ((s8[6291456]{0:T(1024)(128)(4,1)}), s8[4194304]{0:T(1024)(128)(4,1)S(1)}, s32[]{:S(2)}) async-start(s8[6291456]{0:T(1024)(128)(4,1)} %bitcast.15), calls=%async_computation.2 | async-start | bytes 8388608
  44.8 12.3 %collective-permute-start.10 = (bf16[384,512]{1,0:T(8,128)(2,1)S(1)}, bf16[384,512]{1,0:T(8,128)(2,1)S(1)}, u32[]{:S(2)}, u32[]{:S(2)}) collective-permute-start(bf16[384,512]{1,0:T(8,128)(2,1)S(1)} %get-tuple-element.55), channel_id=1, source_target_pairs={{0,8},{24,16},{1,9},{25,17},{2,10},{26,18},{3,11},{27,19},{4,12},{... | collective-permute-start | bytes 1179656 | tf_op jit(solution)/shard_map/ppermute | solution.py:507
  49.3 24.6 %collective-permute-start.17 = (bf16[192,2048]{1,0:T(8,128)(2,1)S(1)}, bf16[192,2048]{1,0:T(8,128)(2,1)S(1)}, u32[]{:S(2)}, u32[]{:S(2)}) collective-permute-start(bf16[192,2048]{1,0:T(8,128)(2,1)S(1)} %collective-permute-done.14.refs_0_), channel_id=1, source_target_pairs={{8,0},{16,24},{9,1},{17,25},{10,2},{18,26},{11,3},{19,27},{12,4},{... | collective-permute-start | bytes 2359304 | tf_op jit(solution)/shard_map/ppermute | solution.py:69
  50.7 15.1 %collective-permute-start.16 = (bf16[384,512]{1,0:T(8,128)(2,1)S(1)}, bf16[384,512]{1,0:T(8,128)(2,1)S(1)}, u32[]{:S(2)}, u32[]{:S(2)}) collective-permute-start(bf16[384,512]{1,0:T(8,128)(2,1)S(1)} %add_convert_fusion.7), channel_id=1, source_target_pairs={{8,16},{16,8},{9,17},{17,9},{10,18},{18,10},{11,19},{19,11},{12,20... | collective-permute-start | bytes 1179656 | tf_op jit(solution)/shard_map/ppermute | solution.py:514
  57.1 11.4 %collective-permute-start.11 = (bf16[384,512]{1,0:T(8,128)(2,1)S(1)}, bf16[384,512]{1,0:T(8,128)(2,1)S(1)}, u32[]{:S(2)}, u32[]{:S(2)}) collective-permute-start(bf16[384,512]{1,0:T(8,128)(2,1)S(1)} %get-tuple-element.56), channel_id=1, source_target_pairs={{0,8},{24,16},{1,9},{25,17},{2,10},{26,18},{3,11},{27,19},{4,12},{... | collective-permute-start | bytes 1179656 | tf_op jit(solution)/shard_map/ppermute | solution.py:507
  65.8 14.0 %collective-permute-start.22 = (bf16[384,512]{1,0:T(8,128)(2,1)S(1)}, bf16[384,512]{1,0:T(8,128)(2,1)S(1)}, u32[]{:S(2)}, u32[]{:S(2)}) collective-permute-start(bf16[384,512]{1,0:T(8,128)(2,1)S(1)} %add_convert_fusion.2), channel_id=1, source_target_pairs={{8,16},{16,8},{9,17},{17,9},{10,18},{18,10},{11,19},{19,11},{12,20... | collective-permute-start | bytes 1179656 | tf_op jit(solution)/shard_map/ppermute | solution.py:514
  68.5 10.5 %collective-permute-start.12 = (bf16[384,512]{1,0:T(8,128)(2,1)S(1)}, bf16[384,512]{1,0:T(8,128)(2,1)S(1)}, u32[]{:S(2)}, u32[]{:S(2)}) collective-permute-start(bf16[384,512]{1,0:T(8,128)(2,1)S(1)} %get-tuple-element.57), channel_id=1, source_target_pairs={{0,8},{24,16},{1,9},{25,17},{2,10},{26,18},{3,11},{27,19},{4,12},{... | collective-permute-start | bytes 1179656 | tf_op jit(solution)/shard_map/ppermute | solution.py:507
  73.0 15.0 %slice-start.3 = ((s8[6291456]{0:T(1024)(128)(4,1)}), s8[2097152]{0:T(1024)(128)(4,1)S(1)}, s32[]{:S(2)}) async-start(s8[6291456]{0:T(1024)(128)(4,1)} %bitcast.15), calls=%async_computation.3 | async-start | bytes 4194304
  73.1 8.2 %collective-permute-start.19 = (bf16[384,512]{1,0:T(8,128)(2,1)S(1)}, bf16[384,512]{1,0:T(8,128)(2,1)S(1)}, u32[]{:S(2)}, u32[]{:S(2)}) collective-permute-start(bf16[384,512]{1,0:T(8,128)(2,1)S(1)} %add_convert_fusion.5), channel_id=1, source_target_pairs={{8,16},{16,8},{9,17},{17,9},{10,18},{18,10},{11,19},{19,11},{12,20... | collective-permute-start | bytes 1179656 | tf_op jit(solution)/shard_map/ppermute | solution.py:514
  75.3 12.7 %slice-start = ((s8[6291456]{0:T(1024)(128)(4,1)}), s8[4194304]{0:T(1024)(128)(4,1)S(1)}, s32[]{:S(2)}) async-start(s8[6291456]{0:T(1024)(128)(4,1)} %bitcast.13), calls=%async_computation | async-start | bytes 8388608
  75.3 12.7 %collective-permute-start.18 = (bf16[384,512]{1,0:T(8,128)(2,1)S(1)}, bf16[384,512]{1,0:T(8,128)(2,1)S(1)}, u32[]{:S(2)}, u32[]{:S(2)}) collective-permute-start(bf16[384,512]{1,0:T(8,128)(2,1)S(1)} %add_convert_fusion.6.refs_0_), channel_id=1, source_target_pairs={{8,0},{16,24},{9,1},{17,25},{10,2},{18,26},{11,3},{19,27},{12,4},{... | collective-permute-start | bytes 1179656 | tf_op jit(solution)/shard_map/ppermute | solution.py:69
  79.1 14.7 %collective-permute-start.13 = (bf16[384,512]{1,0:T(8,128)(2,1)S(1)}, bf16[384,512]{1,0:T(8,128)(2,1)S(1)}, u32[]{:S(2)}, u32[]{:S(2)}) collective-permute-start(bf16[384,512]{1,0:T(8,128)(2,1)S(1)} %add_convert_fusion.8), channel_id=1, source_target_pairs={{8,16},{16,8},{9,17},{17,9},{10,18},{18,10},{11,19},{19,11},{12,20... | collective-permute-start | bytes 1179656 | tf_op jit(solution)/shard_map/ppermute | solution.py:514
  79.9 16.6 %collective-permute-start.23 = (bf16[384,512]{1,0:T(8,128)(2,1)S(1)}, bf16[384,512]{1,0:T(8,128)(2,1)S(1)}, u32[]{:S(2)}, u32[]{:S(2)}) collective-permute-start(bf16[384,512]{1,0:T(8,128)(2,1)S(1)} %add_convert_fusion.1.refs_0_), channel_id=1, source_target_pairs={{8,0},{16,24},{9,1},{17,25},{10,2},{18,26},{11,3},{19,27},{12,4},{... | collective-permute-start | bytes 1179656 | tf_op jit(solution)/shard_map/ppermute | solution.py:69
  81.3 6.7 %slice-start.1 = ((s8[6291456]{0:T(1024)(128)(4,1)}), s8[2097152]{0:T(1024)(128)(4,1)S(1)}, s32[]{:S(2)}) async-start(s8[6291456]{0:T(1024)(128)(4,1)} %bitcast.13), calls=%async_computation.1 | async-start | bytes 4194304
  81.3 23.6 %collective-permute-start.21 = (bf16[384,512]{1,0:T(8,128)(2,1)S(1)}, bf16[384,512]{1,0:T(8,128)(2,1)S(1)}, u32[]{:S(2)}, u32[]{:S(2)}) collective-permute-start(bf16[384,512]{1,0:T(8,128)(2,1)S(1)} %add_convert_fusion.4.refs_0_), channel_id=1, source_target_pairs={{8,0},{16,24},{9,1},{17,25},{10,2},{18,26},{11,3},{19,27},{12,4},{... | collective-permute-start | bytes 1179656 | tf_op jit(solution)/shard_map/ppermute | solution.py:69
  93.9 17.3 %collective-permute-start.20 = (bf16[384,512]{1,0:T(8,128)(2,1)S(1)}, bf16[384,512]{1,0:T(8,128)(2,1)S(1)}, u32[]{:S(2)}, u32[]{:S(2)}) collective-permute-start(bf16[384,512]{1,0:T(8,128)(2,1)S(1)} %add_convert_fusion.3.refs_0_), channel_id=1, source_target_pairs={{8,0},{16,24},{9,1},{17,25},{10,2},{18,26},{11,3},{19,27},{12,4},{... | collective-permute-start | bytes 1179656 | tf_op jit(solution)/shard_map/ppermute | solution.py:69
  114.5 2.1 %collective-permute-start.24 = (bf16[4,48,1536]{2,1,0:T(8,128)(2,1)S(1)}, bf16[4,48,1536]{2,1,0:T(8,128)(2,1)S(1)}, u32[]{:S(2)}, u32[]{:S(2)}) collective-permute-start(bf16[4,48,1536]{2,1,0:T(8,128)(2,1)S(1)} %get-tuple-element.81), channel_id=1, source_target_pairs={{0,1},{1,0},{2,3},{3,2},{4,5},{5,4},{6,7},{7,6},{8,9},{9,8},{10,11... | collective-permute-start | bytes 1769480 | tf_op jit(solution)/shard_map/ppermute | solution.py:534
  116.8 10.5 %collective-permute-start.25 = (bf16[48,1536]{1,0:T(8,128)(2,1)S(1)}, bf16[48,1536]{1,0:T(8,128)(2,1)S(1)}, u32[]{:S(2)}, u32[]{:S(2)}) collective-permute-start(bf16[48,1536]{1,0:T(8,128)(2,1)S(1)} %get-tuple-element.90), channel_id=1, source_target_pairs={{0,2},{1,3},{2,0},{3,1},{4,6},{5,7},{6,4},{7,5},{8,10},{9,11},{10,... | collective-permute-start | bytes 442376 | tf_op jit(solution)/shard_map/ppermute | solution.py:538
  118.3 8.9 %collective-permute-start.26 = (bf16[48,1536]{1,0:T(8,128)(2,1)S(1)}, bf16[48,1536]{1,0:T(8,128)(2,1)S(1)}, u32[]{:S(2)}, u32[]{:S(2)}) collective-permute-start(bf16[48,1536]{1,0:T(8,128)(2,1)S(1)} %get-tuple-element.92), channel_id=1, source_target_pairs={{0,4},{1,5},{2,6},{3,7},{4,0},{5,1},{6,2},{7,3},{8,12},{9,13},{10,... | collective-permute-start | bytes 442376 | tf_op jit(solution)/shard_map/ppermute | solution.py:538
  119.8 7.5 %collective-permute-start.27 = (bf16[48,1536]{1,0:T(8,128)(2,1)S(1)}, bf16[48,1536]{1,0:T(8,128)(2,1)S(1)}, u32[]{:S(2)}, u32[]{:S(2)}) collective-permute-start(bf16[48,1536]{1,0:T(8,128)(2,1)S(1)} %get-tuple-element.91), channel_id=1, source_target_pairs={{0,6},{1,7},{2,4},{3,5},{4,2},{5,3},{6,0},{7,1},{8,14},{9,15},{10,... | collective-permute-start | bytes 442376 | tf_op jit(solution)/shard_map/ppermute | solution.py:538

commit v4 on v3

--- a/solution.py
+++ b/solution.py
@@ -367,7 +367,7 @@
     total, units = grads[0].shape
     depth, width = weights[0].shape
     rows = total // n_col
-    tile = tile_of(depth, 512)
+    tile = tile_of(depth, 768)
     tall = whole((total, units))
     wide = pl.BlockSpec((tile, units), lambda j, *_: (j, chunk))
     running = pl.BlockSpec((total, tile), lambda j, *_: (0, j))
@@ -422,7 +422,7 @@
 def weight_grads(inputs_t, gate_delta, up_delta, chunk, before):
     depth, total = inputs_t.shape
     units = gate_delta.shape[1]
-    tile = tile_of(depth, 512)
+    tile = tile_of(depth, 768)
     more, more_specs = filled(before)
     out = pl.BlockSpec((tile, units), lambda j: (j, chunk))
     cost = NO_COST

time: 129 us -> 128 us (level)
  no operation moved by 1% of the time
where the time goes in v4:
time: 128 us
  Pallas kernels  47 us (37%)
  starting transfers between devices  46 us (36%)
  waiting for transfers between devices  31 us (24%)
  other arithmetic  1.77 us (1%)
    ppermute x4, starting transfers between devices, on_device(): got = lax.ppermute(held, 'row', inward([step], n_row))  20.8 us
    pallas_call x4, Pallas kernels, deltas(): pl.pallas_call(functools.partial(delta_kernel, n, n_col, before is None,...  20.5 us
    ppermute x4, waiting for transfers between devices, on_device(): got = lax.ppermute(held, 'row', inward([step], n_row))  12.3 us
    ppermute x7, waiting for transfers between devices, cube_gather(): pieces[slot | bit] = lax.ppermute(pieces[slot], 'col', pairs)  11.1 us
    ppermute x6, starting transfers between devices, sent_out(): got = lax.ppermute(block, 'row', outward([step], n))  8.33 us
    pallas_call x2, Pallas kernels, partials(): pl.pallas_call(functools.partial(partial_kernel, len(pieces)), grid_spec=...  8.14 us
    pallas_call x2, Pallas kernels, down_grads(): pl.pallas_call(functools.partial(down_kernel, n), grid_spec=pltpu.Prefetc...  7.74 us
    ppermute x6, waiting for transfers between devices, sent_out(): got = lax.ppermute(block, 'row', outward([step], n))  5.56 us
  transfers between devices with their start and end apart: 28, of which 11 were waited for; matrix products, arithmetic and copies ran while one was open for 1% of the time, Pallas kernels for 33%

profile of v4, /device:TPU:0, one launch (start us, length us, event | category | flops | bytes accessed | tf_op | source)
XLA Modules:
  0.0 127.7 jit_solution(4431785621954045072)
XLA Ops:
  0.6 1.2 join.1
  1.9 3.1 %collective-permute-start.7 = (bf16[192,2048]{1,0:T(8,128)(2,1)S(1)}, bf16[192,2048]{1,0:T(8,128)(2,1)}, u32[]{:S(2)}, u32[]{:S(2)}) collective-permute-start(bf16[192,2048]{1,0:T(8,128)(2,1)S(1)} %get-tuple-element.49.refs_0_), channel_id=1, source_target_pairs={{0,8},{24,16},{8,0},{16,24},{1,9},{25,17},{9,1},{17,25},{2,10},{26... | collective-permute-start | bytes 2359304 | tf_op jit(solution)/shard_map/ppermute | solution.py:55
  5.0 1.6 %collective-permute-start.8 = (bf16[192,2048]{1,0:T(8,128)(2,1)S(1)}, bf16[192,2048]{1,0:T(8,128)(2,1)}, u32[]{:S(2)}, u32[]{:S(2)}) collective-permute-start(bf16[192,2048]{1,0:T(8,128)(2,1)S(1)} %get-tuple-element.49.refs_0_), channel_id=1, source_target_pairs={{8,16},{16,8},{9,17},{17,9},{10,18},{18,10},{11,19},{19,11},{12,20... | collective-permute-start | bytes 2359304 | tf_op jit(solution)/shard_map/ppermute | solution.py:467
  6.5 0.9 copy-done
  7.4 1.5 %collective-permute-start.3 = (bf16[96,1536]{1,0:T(8,128)(2,1)S(1)}, bf16[96,1536]{1,0:T(8,128)(2,1)S(1)}, u32[]{:S(2)}, u32[]{:S(2)}) collective-permute-start(bf16[96,1536]{1,0:T(8,128)(2,1)S(1)} %get-tuple-element.47.refs_0_), channel_id=1, source_target_pairs={{0,4},{1,5},{2,6},{3,7},{4,0},{5,1},{6,2},{7,3},{8,12},{9,13},{10,... | collective-permute-start | bytes 884744 | tf_op jit(solution)/shard_map/ppermute | solution.py:86
  8.9 1.5 %collective-permute-start.1 = (bf16[96,1536]{1,0:T(8,128)(2,1)S(1)}, bf16[96,1536]{1,0:T(8,128)(2,1)S(1)}, u32[]{:S(2)}, u32[]{:S(2)}) collective-permute-start(bf16[96,1536]{1,0:T(8,128)(2,1)S(1)} %get-tuple-element.47.refs_0_), channel_id=1, source_target_pairs={{0,2},{1,3},{2,0},{3,1},{4,6},{5,7},{6,4},{7,5},{8,10},{9,11},{10,... | collective-permute-start | bytes 884744 | tf_op jit(solution)/shard_map/ppermute | solution.py:86
  10.4 5.5 %collective-permute-done.3.refs_4_ = bf16[96,1536]{1,0:T(8,128)(2,1)S(1)} collective-permute-done((bf16[96,1536]{1,0:T(8,128)(2,1)S(1)}, bf16[96,1536]{1,0:T(8,128)(2,1)S(1)}, u32[]{:S(2)}, u32[]{:S(2)}) %collective-permute-start.3) | collective-permute-done | bytes 294944 | tf_op jit(solution)/shard_map/ppermute | solution.py:86
  15.9 1.5 %collective-permute-start.5 = (bf16[96,1536]{1,0:T(8,128)(2,1)S(1)}, bf16[96,1536]{1,0:T(8,128)(2,1)S(1)}, u32[]{:S(2)}, u32[]{:S(2)}) collective-permute-start(bf16[96,1536]{1,0:T(8,128)(2,1)S(1)} %collective-permute-done.3.refs_4_), channel_id=1, source_target_pairs={{0,2},{1,3},{2,0},{3,1},{4,6},{5,7},{6,4},{7,5},{8,10},{9,11},{10,... | collective-permute-start | bytes 884744 | tf_op jit(solution)/shard_map/ppermute | solution.py:86
  17.9 5.7 %collective-permute-done.5.refs_6_ = bf16[96,1536]{1,0:T(8,128)(2,1)S(1)} collective-permute-done((bf16[96,1536]{1,0:T(8,128)(2,1)S(1)}, bf16[96,1536]{1,0:T(8,128)(2,1)S(1)}, u32[]{:S(2)}, u32[]{:S(2)}) %collective-permute-start.5) | collective-permute-done | bytes 294944 | tf_op jit(solution)/shard_map/ppermute | solution.py:86
  23.5 0.7 collective-permute-start.14
  24.3 1.3 %collective-permute-start.15 = (bf16[192,2048]{1,0:T(8,128)(2,1)}, bf16[192,2048]{1,0:T(8,128)(2,1)}, u32[]{:S(2)}, u32[]{:S(2)}) collective-permute-start(bf16[192,2048]{1,0:T(8,128)(2,1)} %collective-permute-done.8.refs_2_), channel_id=1, source_target_pairs={{8,0},{16,24},{9,1},{17,25},{10,2},{18,26},{11,3},{19,27},{12,4},{... | collective-permute-start | bytes 2359304 | tf_op jit(solution)/shard_map/ppermute | solution.py:69
  25.6 2.8 %hidden_grad_partials.2 = (bf16[384,512]{1,0:T(8,128)(2,1)S(1)}, bf16[384,1536]{1,0:T(8,128)(2,1)S(1)}) custom-call(s32[2]{0:T(128)S(1)} %pad_add_fusion.ids, bf16[96,1536]{1,0:T(8,128)(2,1)S(1)} %get-tuple-element.47.refs_0_, bf16[96,1536]{1,0:T(8,128)(2,1)S(1)} %collective-permute-done.refs_1_, bf16[96,1536]{1,0:T(8,128)(2,1)S(1)} %collective-permute-done.1.refs_2_, ...), custom_call_target="tpu_custom_call" | custom-call | flops 603979776 | bytes 3145728 | tf_op jit(solution)/shard_map/hidden_grad_partials/pallas_call | solution.py:193
  28.4 7.7 %collective-permute-start.9 = (bf16[384,512]{1,0:T(8,128)(2,1)S(1)}, bf16[384,512]{1,0:T(8,128)(2,1)S(1)}, u32[]{:S(2)}, u32[]{:S(2)}) collective-permute-start(bf16[384,512]{1,0:T(8,128)(2,1)S(1)} %get-tuple-element.54), channel_id=1, source_target_pairs={{0,8},{24,16},{1,9},{25,17},{2,10},{26,18},{3,11},{27,19},{4,12},{... | collective-permute-start | bytes 1179656 | tf_op jit(solution)/shard_map/ppermute | solution.py:507
  36.1 1.0 inputs_transposed.1.refs_8_.refs_9_.inputs
  37.1 5.4 %hidden_grad_partials.3 = (bf16[384,512]{1,0:T(8,128)(2,1)S(1)}, bf16[384,512]{1,0:T(8,128)(2,1)S(1)}, bf16[384,512]{1,0:T(8,128)(2,1)S(1)}) custom-call(s32[2]{0:T(128)S(1)} %pad_add_fusion.ids, bf16[384,1536]{1,0:T(8,128)(2,1)S(1)} %get-tuple-element.50.refs_0_.cotangent, bf16[2048,1536]{1,0:T(8,128)(2,1)} %refs_1_.3), custom_call_target="tpu_custom_call" | custom-call | flops 1811939328 | bytes 7077888 | tf_op jit(solution)/shard_map/hidden_grad_partials/pallas_call | solution.py:193
  42.5 2.4 %collective-permute-done.9 = bf16[384,512]{1,0:T(8,128)(2,1)S(1)} collective-permute-done((bf16[384,512]{1,0:T(8,128)(2,1)S(1)}, bf16[384,512]{1,0:T(8,128)(2,1)S(1)}, u32[]{:S(2)}, u32[]{:S(2)}) %collective-permute-start.9) | collective-permute-done | bytes 393248 | tf_op jit(solution)/shard_map/ppermute | solution.py:507
  44.8 4.4 %collective-permute-start.10 = (bf16[384,512]{1,0:T(8,128)(2,1)S(1)}, bf16[384,512]{1,0:T(8,128)(2,1)S(1)}, u32[]{:S(2)}, u32[]{:S(2)}) collective-permute-start(bf16[384,512]{1,0:T(8,128)(2,1)S(1)} %get-tuple-element.55), channel_id=1, source_target_pairs={{0,8},{24,16},{1,9},{25,17},{2,10},{26,18},{3,11},{27,19},{4,12},{... | collective-permute-start | bytes 1179656 | tf_op jit(solution)/shard_map/ppermute | solution.py:507
  49.3 1.3 %collective-permute-start.17 = (bf16[192,2048]{1,0:T(8,128)(2,1)S(1)}, bf16[192,2048]{1,0:T(8,128)(2,1)S(1)}, u32[]{:S(2)}, u32[]{:S(2)}) collective-permute-start(bf16[192,2048]{1,0:T(8,128)(2,1)S(1)} %collective-permute-done.14.refs_0_), channel_id=1, source_target_pairs={{8,0},{16,24},{9,1},{17,25},{10,2},{18,26},{11,3},{19,27},{12,4},{... | collective-permute-start | bytes 2359304 | tf_op jit(solution)/shard_map/ppermute | solution.py:69
  50.7 0.7 collective-permute-start.16
  51.4 5.8 %collective-permute-done.10 = bf16[384,512]{1,0:T(8,128)(2,1)S(1)} collective-permute-done((bf16[384,512]{1,0:T(8,128)(2,1)S(1)}, bf16[384,512]{1,0:T(8,128)(2,1)S(1)}, u32[]{:S(2)}, u32[]{:S(2)}) %collective-permute-start.10) | collective-permute-done | bytes 393248 | tf_op jit(solution)/shard_map/ppermute | solution.py:507
  57.1 4.4 %collective-permute-start.11 = (bf16[384,512]{1,0:T(8,128)(2,1)S(1)}, bf16[384,512]{1,0:T(8,128)(2,1)S(1)}, u32[]{:S(2)}, u32[]{:S(2)}) collective-permute-start(bf16[384,512]{1,0:T(8,128)(2,1)S(1)} %get-tuple-element.56), channel_id=1, source_target_pairs={{0,8},{24,16},{1,9},{25,17},{2,10},{26,18},{3,11},{27,19},{4,12},{... | collective-permute-start | bytes 1179656 | tf_op jit(solution)/shard_map/ppermute | solution.py:507
  61.6 4.1 %factors.2 = (bf16[288,2048]{1,0:T(8,128)(2,1)S(1)}, bf16[288,2048]{1,0:T(8,128)(2,1)S(1)}, bf16[288,2048]{1,0:T(8,128)(2,1)S(1)}) custom-call(s32[2]{0:T(128)S(1)} %pad_add_fusion.ids, bf16[192,2048]{1,0:T(8,128)(2,1)S(1)} %copy-done.1, bf16[192,2048]{1,0:T(8,128)(2,1)} %collective-permute-done.7.refs_1_, bf16[192,2048]{1,0:T(8,128)(2,1)} %collective-permute-done.8.refs_2_, ...), custom_call_target="tpu_custom_call" | custom-call | flops 5898240 | bytes 5898240 | tf_op jit(solution)/shard_map/factors/pallas_call | solution.py:262
  65.8 0.7 collective-permute-start.22
  66.5 2.1 %collective-permute-done.11 = bf16[384,512]{1,0:T(8,128)(2,1)S(1)} collective-permute-done((bf16[384,512]{1,0:T(8,128)(2,1)S(1)}, bf16[384,512]{1,0:T(8,128)(2,1)S(1)}, u32[]{:S(2)}, u32[]{:S(2)}) %collective-permute-start.11) | collective-permute-done | bytes 393248 | tf_op jit(solution)/shard_map/ppermute | solution.py:507
  68.5 4.4 %collective-permute-start.12 = (bf16[384,512]{1,0:T(8,128)(2,1)S(1)}, bf16[384,512]{1,0:T(8,128)(2,1)S(1)}, u32[]{:S(2)}, u32[]{:S(2)}) collective-permute-start(bf16[384,512]{1,0:T(8,128)(2,1)S(1)} %get-tuple-element.57), channel_id=1, source_target_pairs={{0,8},{24,16},{1,9},{25,17},{2,10},{26,18},{3,11},{27,19},{4,12},{... | collective-permute-start | bytes 1179656 | tf_op jit(solution)/shard_map/ppermute | solution.py:507
  73.1 0.8 collective-permute-start.19
  73.9 1.3 %factors.3 = (bf16[96,2048]{1,0:T(8,128)(2,1)S(1)}, bf16[96,2048]{1,0:T(8,128)(2,1)S(1)}, bf16[96,2048]{1,0:T(8,128)(2,1)S(1)}) custom-call(s32[2]{0:T(128)S(1)} %pad_add_fusion.ids, bf16[192,2048]{1,0:T(8,128)(2,1)S(1)} %collective-permute-done.14.refs_0_, bf16[192,2048]{1,0:T(8,128)(2,1)S(1)} %collective-permute-done.17.refs_1_), custom_call_target="tpu_custom_call" | custom-call | flops 1966080 | bytes 15728640 | tf_op jit(solution)/shard_map/factors/pallas_call | solution.py:262
  75.3 1.6 %collective-permute-start.18 = (bf16[384,512]{1,0:T(8,128)(2,1)S(1)}, bf16[384,512]{1,0:T(8,128)(2,1)S(1)}, u32[]{:S(2)}, u32[]{:S(2)}) collective-permute-start(bf16[384,512]{1,0:T(8,128)(2,1)S(1)} %add_convert_fusion.6.refs_0_), channel_id=1, source_target_pairs={{8,0},{16,24},{9,1},{17,25},{10,2},{18,26},{11,3},{19,27},{12,4},{... | collective-permute-start | bytes 1179656 | tf_op jit(solution)/shard_map/ppermute | solution.py:69
  76.9 2.1 %collective-permute-done.12 = bf16[384,512]{1,0:T(8,128)(2,1)S(1)} collective-permute-done((bf16[384,512]{1,0:T(8,128)(2,1)S(1)}, bf16[384,512]{1,0:T(8,128)(2,1)S(1)}, u32[]{:S(2)}, u32[]{:S(2)}) %collective-permute-start.12) | collective-permute-done | bytes 393248 | tf_op jit(solution)/shard_map/ppermute | solution.py:507
  79.1 0.7 collective-permute-start.13
  79.9 1.3 %collective-permute-start.23 = (bf16[384,512]{1,0:T(8,128)(2,1)S(1)}, bf16[384,512]{1,0:T(8,128)(2,1)S(1)}, u32[]{:S(2)}, u32[]{:S(2)}) collective-permute-start(bf16[384,512]{1,0:T(8,128)(2,1)S(1)} %add_convert_fusion.1.refs_0_), channel_id=1, source_target_pairs={{8,0},{16,24},{9,1},{17,25},{10,2},{18,26},{11,3},{19,27},{12,4},{... | collective-permute-start | bytes 1179656 | tf_op jit(solution)/shard_map/ppermute | solution.py:69
  81.3 1.4 %collective-permute-start.21 = (bf16[384,512]{1,0:T(8,128)(2,1)S(1)}, bf16[384,512]{1,0:T(8,128)(2,1)S(1)}, u32[]{:S(2)}, u32[]{:S(2)}) collective-permute-start(bf16[384,512]{1,0:T(8,128)(2,1)S(1)} %add_convert_fusion.4.refs_0_), channel_id=1, source_target_pairs={{8,0},{16,24},{9,1},{17,25},{10,2},{18,26},{11,3},{19,27},{12,4},{... | collective-permute-start | bytes 1179656 | tf_op jit(solution)/shard_map/ppermute | solution.py:69
  82.8 3.9 %down_grad.2.refs_0_ = bf16[2048,1536]{1,0:T(8,128)(2,1)} custom-call(s32[2]{0:T(128)S(1)} %pad_add_fusion.ids, bf16[288,2048]{1,0:T(8,128)(2,1)S(1)} %get-tuple-element.61.early, bf16[96,2048]{1,0:T(8,128)(2,1)S(1)} %get-tuple-element.88.late, bf16[384,1536]{1,0:T(8,128)(2,1)S(1)} %get-tuple-element.50.refs_0_.cotangent), custom_call_target="tpu_custom_call" | custom-call | flops 1207959552 | bytes 5111808 | tf_op jit(solution)/shard_map/down_grad/pallas_call | solution.py:298
  86.6 1.4 %collective-permute-done.18.refs_1_ = bf16[384,512]{1,0:T(8,128)(2,1)S(1)} collective-permute-done((bf16[384,512]{1,0:T(8,128)(2,1)S(1)}, bf16[384,512]{1,0:T(8,128)(2,1)S(1)}, u32[]{:S(2)}, u32[]{:S(2)}) %collective-permute-start.18) | collective-permute-done | bytes 393248 | tf_op jit(solution)/shard_map/ppermute | solution.py:69
  88.1 5.7 %chunk.4 = (f32[384,1536]{1,0:T(8,128)S(1)}, bf16[1536,2048]{1,0:T(8,128)(2,1)}, bf16[1536,2048]{1,0:T(8,128)(2,1)}) custom-call(s32[2]{0:T(128)S(1)} %pad_add_fusion.ids, bf16[384,512]{1,0:T(8,128)(2,1)S(1)} %add_convert_fusion.6.refs_0_, bf16[384,512]{1,0:T(8,128)(2,1)S(1)} %collective-permute-done.18.refs_1_, ...), custom_call_target="tpu_custom_call" | custom-call | tf_op jit(solution)/shard_map/chunk/pallas_call | solution.py:399
  93.9 1.5 %collective-permute-start.20 = (bf16[384,512]{1,0:T(8,128)(2,1)S(1)}, bf16[384,512]{1,0:T(8,128)(2,1)S(1)}, u32[]{:S(2)}, u32[]{:S(2)}) collective-permute-start(bf16[384,512]{1,0:T(8,128)(2,1)S(1)} %add_convert_fusion.3.refs_0_), channel_id=1, source_target_pairs={{8,0},{16,24},{9,1},{17,25},{10,2},{18,26},{11,3},{19,27},{12,4},{... | collective-permute-start | bytes 1179656 | tf_op jit(solution)/shard_map/ppermute | solution.py:69
  95.3 1.2 collective-permute-done.23.refs_1_
  96.6 5.8 %chunk.5 = (f32[384,1536]{1,0:T(8,128)S(1)}, bf16[1536,2048]{1,0:T(8,128)(2,1)}, bf16[1536,2048]{1,0:T(8,128)(2,1)}) custom-call(s32[2]{0:T(128)S(1)} %pad_add_fusion.ids, bf16[384,512]{1,0:T(8,128)(2,1)S(1)} %add_convert_fusion.1.refs_0_, bf16[384,512]{1,0:T(8,128)(2,1)S(1)} %collective-permute-done.23.refs_1_, ...), custom_call_target="tpu_custom_call", output_to_operand_aliasing={{1}: (11, {}), {2}: (12, {})} | custom-call | tf_op jit(solution)/shard_map/chunk/pallas_call | solution.py:399
  102.4 2.6 %collective-permute-done.21.refs_1_ = bf16[384,512]{1,0:T(8,128)(2,1)S(1)} collective-permute-done((bf16[384,512]{1,0:T(8,128)(2,1)S(1)}, bf16[384,512]{1,0:T(8,128)(2,1)S(1)}, u32[]{:S(2)}, u32[]{:S(2)}) %collective-permute-start.21) | collective-permute-done | bytes 393248 | tf_op jit(solution)/shard_map/ppermute | solution.py:69
  105.0 5.8 %chunk.6 = (f32[384,1536]{1,0:T(8,128)S(1)}, bf16[1536,2048]{1,0:T(8,128)(2,1)}, bf16[1536,2048]{1,0:T(8,128)(2,1)}) custom-call(s32[2]{0:T(128)S(1)} %pad_add_fusion.ids, bf16[384,512]{1,0:T(8,128)(2,1)S(1)} %add_convert_fusion.4.refs_0_, bf16[384,512]{1,0:T(8,128)(2,1)S(1)} %collective-permute-done.21.refs_1_, ...), custom_call_target="tpu_custom_call", output_to_operand_aliasing={{1}: (11, {}), {2}: (12, {})} | custom-call | tf_op jit(solution)/shard_map/chunk/pallas_call | solution.py:399
  111.2 3.1 %chunk.7 = (bf16[384,512]{1,0:T(8,128)(2,1)S(1)}, bf16[384,512]{1,0:T(8,128)(2,1)S(1)}, bf16[4,48,1536]{2,1,0:T(8,128)(2,1)S(1)}, bf16[4,48,1536]{2,1,0:T(8,128)(2,1)S(1)}) custom-call(s32[2]{0:T(128)S(1)} %pad_add_fusion.ids, bf16[384,512]{1,0:T(8,128)(2,1)S(1)} %add_convert_fusion.3.refs_0_, bf16[384,512]{1,0:T(8,128)(2,1)S(1)} %collective-permute-done.20.refs_1_, ...), custom_call_target="tpu_custom_call" | custom-call | tf_op jit(solution)/shard_map/chunk/pallas_call | solution.py:399
  114.4 2.0 %collective-permute-done.24 = bf16[4,48,1536]{2,1,0:T(8,128)(2,1)S(1)} collective-permute-done((bf16[4,48,1536]{2,1,0:T(8,128)(2,1)S(1)}, bf16[4,48,1536]{2,1,0:T(8,128)(2,1)S(1)}, u32[]{:S(2)}, u32[]{:S(2)}) %collective-permute-start.24) | collective-permute-done | bytes 589856 | tf_op jit(solution)/shard_map/ppermute | solution.py:534
  116.6 1.6 %collective-permute-start.25 = (bf16[48,1536]{1,0:T(8,128)(2,1)S(1)}, bf16[48,1536]{1,0:T(8,128)(2,1)S(1)}, u32[]{:S(2)}, u32[]{:S(2)}) collective-permute-start(bf16[48,1536]{1,0:T(8,128)(2,1)S(1)} %get-tuple-element.90), channel_id=1, source_target_pairs={{0,2},{1,3},{2,0},{3,1},{4,6},{5,7},{6,4},{7,5},{8,10},{9,11},{10,... | collective-permute-start | bytes 442376 | tf_op jit(solution)/shard_map/ppermute | solution.py:538
  118.2 1.4 %collective-permute-start.26 = (bf16[48,1536]{1,0:T(8,128)(2,1)S(1)}, bf16[48,1536]{1,0:T(8,128)(2,1)S(1)}, u32[]{:S(2)}, u32[]{:S(2)}) collective-permute-start(bf16[48,1536]{1,0:T(8,128)(2,1)S(1)} %get-tuple-element.92), channel_id=1, source_target_pairs={{0,4},{1,5},{2,6},{3,7},{4,0},{5,1},{6,2},{7,3},{8,12},{9,13},{10,... | collective-permute-start | bytes 442376 | tf_op jit(solution)/shard_map/ppermute | solution.py:538
  119.6 0.6 collective-permute-start.27
  120.2 3.9 %down_grad.3 = bf16[2048,1536]{1,0:T(8,128)(2,1)} custom-call(s32[2]{0:T(128)S(1)} %pad_add_fusion.ids, bf16[288,2048]{1,0:T(8,128)(2,1)S(1)} %get-tuple-element.61.early, bf16[96,2048]{1,0:T(8,128)(2,1)S(1)} %get-tuple-element.88.late, bf16[384,1536]{1,0:T(8,128)(2,1)S(1)} %get-tuple-element.50.refs_0_.cotangent, ...), custom_call_target="tpu_custom_call", output_to_operand_aliasing={{}: (4, {})} | custom-call | flops 1207959552 | bytes 5111808 | tf_op jit(solution)/shard_map/down_grad/pallas_call | solution.py:298
  124.0 3.0 %gate_and_up_grad.1 = (bf16[1536,2048]{1,0:T(8,128)(2,1)}, bf16[1536,2048]{1,0:T(8,128)(2,1)}) custom-call(bf16[1536,384]{1,0:T(8,128)(2,1)S(1)} %inputs_transposed.1.refs_8_.refs_9_.inputs, bf16[384,512]{1,0:T(8,128)(2,1)S(1)} %get-tuple-element.82.gate_delta, ...), custom_call_target="tpu_custom_call", output_to_operand_aliasing={{0}: (3, {}), {1}: (4, {})} | custom-call | flops 1207959552 | bytes 5111808 | tf_op jit(solution)/shard_map/gate_and_up_grad/pallas_call | solution.py:435
  127.0 0.7 fusion.2
  (47 shorter events, 2.1 us)
Async XLA Ops:
  1.9 21.7 %collective-permute-start.7 = (bf16[192,2048]{1,0:T(8,128)(2,1)S(1)}, bf16[192,2048]{1,0:T(8,128)(2,1)}, u32[]{:S(2)}, u32[]{:S(2)}) collective-permute-start(bf16[192,2048]{1,0:T(8,128)(2,1)S(1)} %get-tuple-element.49.refs_0_), channel_id=1, source_target_pairs={{0,8},{24,16},{8,0},{16,24},{1,9},{25,17},{9,1},{17,25},{2,10},{26... | collective-permute-start | bytes 2359304 | tf_op jit(solution)/shard_map/ppermute | solution.py:55
  5.0 19.3 %collective-permute-start.8 = (bf16[192,2048]{1,0:T(8,128)(2,1)S(1)}, bf16[192,2048]{1,0:T(8,128)(2,1)}, u32[]{:S(2)}, u32[]{:S(2)}) collective-permute-start(bf16[192,2048]{1,0:T(8,128)(2,1)S(1)} %get-tuple-element.49.refs_0_), channel_id=1, source_target_pairs={{8,16},{16,8},{9,17},{17,9},{10,18},{18,10},{11,19},{19,11},{12,20... | collective-permute-start | bytes 2359304 | tf_op jit(solution)/shard_map/ppermute | solution.py:467
  6.5 0.9 copy-start
  7.4 8.5 %collective-permute-start.3 = (bf16[96,1536]{1,0:T(8,128)(2,1)S(1)}, bf16[96,1536]{1,0:T(8,128)(2,1)S(1)}, u32[]{:S(2)}, u32[]{:S(2)}) collective-permute-start(bf16[96,1536]{1,0:T(8,128)(2,1)S(1)} %get-tuple-element.47.refs_0_), channel_id=1, source_target_pairs={{0,4},{1,5},{2,6},{3,7},{4,0},{5,1},{6,2},{7,3},{8,12},{9,13},{10,... | collective-permute-start | bytes 884744 | tf_op jit(solution)/shard_map/ppermute | solution.py:86
  8.9 8.4 %collective-permute-start.1 = (bf16[96,1536]{1,0:T(8,128)(2,1)S(1)}, bf16[96,1536]{1,0:T(8,128)(2,1)S(1)}, u32[]{:S(2)}, u32[]{:S(2)}) collective-permute-start(bf16[96,1536]{1,0:T(8,128)(2,1)S(1)} %get-tuple-element.47.refs_0_), channel_id=1, source_target_pairs={{0,2},{1,3},{2,0},{3,1},{4,6},{5,7},{6,4},{7,5},{8,10},{9,11},{10,... | collective-permute-start | bytes 884744 | tf_op jit(solution)/shard_map/ppermute | solution.py:86
  10.4 7.0 %collective-permute-start = (bf16[96,1536]{1,0:T(8,128)(2,1)S(1)}, bf16[96,1536]{1,0:T(8,128)(2,1)S(1)}, u32[]{:S(2)}, u32[]{:S(2)}) collective-permute-start(bf16[96,1536]{1,0:T(8,128)(2,1)S(1)} %get-tuple-element.47.refs_0_), channel_id=1, source_target_pairs={{0,1},{1,0},{2,3},{3,2},{4,5},{5,4},{6,7},{7,6},{8,9},{9,8},{10,11... | collective-permute-start | bytes 884744 | tf_op jit(solution)/shard_map/ppermute | solution.py:86
  15.9 7.7 %collective-permute-start.5 = (bf16[96,1536]{1,0:T(8,128)(2,1)S(1)}, bf16[96,1536]{1,0:T(8,128)(2,1)S(1)}, u32[]{:S(2)}, u32[]{:S(2)}) collective-permute-start(bf16[96,1536]{1,0:T(8,128)(2,1)S(1)} %collective-permute-done.3.refs_4_), channel_id=1, source_target_pairs={{0,2},{1,3},{2,0},{3,1},{4,6},{5,7},{6,4},{7,5},{8,10},{9,11},{10,... | collective-permute-start | bytes 884744 | tf_op jit(solution)/shard_map/ppermute | solution.py:86
  17.4 8.3 %collective-permute-start.4 = (bf16[96,1536]{1,0:T(8,128)(2,1)S(1)}, bf16[96,1536]{1,0:T(8,128)(2,1)S(1)}, u32[]{:S(2)}, u32[]{:S(2)}) collective-permute-start(bf16[96,1536]{1,0:T(8,128)(2,1)S(1)} %collective-permute-done.3.refs_4_), channel_id=1, source_target_pairs={{0,1},{1,0},{2,3},{3,2},{4,5},{5,4},{6,7},{7,6},{8,9},{9,8},{10,11... | collective-permute-start | bytes 884744 | tf_op jit(solution)/shard_map/ppermute | solution.py:86
  17.4 8.3 %collective-permute-start.2 = (bf16[96,1536]{1,0:T(8,128)(2,1)S(1)}, bf16[96,1536]{1,0:T(8,128)(2,1)S(1)}, u32[]{:S(2)}, u32[]{:S(2)}) collective-permute-start(bf16[96,1536]{1,0:T(8,128)(2,1)S(1)} %collective-permute-done.1.refs_2_), channel_id=1, source_target_pairs={{0,1},{1,0},{2,3},{3,2},{4,5},{5,4},{6,7},{7,6},{8,9},{9,8},{10,11... | collective-permute-start | bytes 884744 | tf_op jit(solution)/shard_map/ppermute | solution.py:86
  23.5 2.1 %collective-permute-start.6 = (bf16[96,1536]{1,0:T(8,128)(2,1)S(1)}, bf16[96,1536]{1,0:T(8,128)(2,1)S(1)}, u32[]{:S(2)}, u32[]{:S(2)}) collective-permute-start(bf16[96,1536]{1,0:T(8,128)(2,1)S(1)} %collective-permute-done.5.refs_6_), channel_id=1, source_target_pairs={{0,1},{1,0},{2,3},{3,2},{4,5},{5,4},{6,7},{7,6},{8,9},{9,8},{10,11... | collective-permute-start | bytes 884744 | tf_op jit(solution)/shard_map/ppermute | solution.py:86
  23.5 25.7 %collective-permute-start.14 = (bf16[192,2048]{1,0:T(8,128)(2,1)}, bf16[192,2048]{1,0:T(8,128)(2,1)S(1)}, u32[]{:S(2)}, u32[]{:S(2)}) collective-permute-start(bf16[192,2048]{1,0:T(8,128)(2,1)} %collective-permute-done.7.refs_1_), channel_id=1, source_target_pairs={{8,16},{16,8},{9,17},{17,9},{10,18},{18,10},{11,19},{19,11},{12,20... | collective-permute-start | bytes 2359304 | tf_op jit(solution)/shard_map/ppermute | solution.py:467
  24.3 25.0 %collective-permute-start.15 = (bf16[192,2048]{1,0:T(8,128)(2,1)}, bf16[192,2048]{1,0:T(8,128)(2,1)}, u32[]{:S(2)}, u32[]{:S(2)}) collective-permute-start(bf16[192,2048]{1,0:T(8,128)(2,1)} %collective-permute-done.8.refs_2_), channel_id=1, source_target_pairs={{8,0},{16,24},{9,1},{17,25},{10,2},{18,26},{11,3},{19,27},{12,4},{... | collective-permute-start | bytes 2359304 | tf_op jit(solution)/shard_map/ppermute | solution.py:69
  28.4 33.1 %copy-start.1 = (bf16[192,2048]{1,0:T(8,128)(2,1)S(1)}, bf16[192,2048]{1,0:T(8,128)(2,1)}, u32[]{:S(2)}) copy-start(bf16[192,2048]{1,0:T(8,128)(2,1)} %copy-done) | copy-start | bytes 2359300
  28.4 16.4 %collective-permute-start.9 = (bf16[384,512]{1,0:T(8,128)(2,1)S(1)}, bf16[384,512]{1,0:T(8,128)(2,1)S(1)}, u32[]{:S(2)}, u32[]{:S(2)}) collective-permute-start(bf16[384,512]{1,0:T(8,128)(2,1)S(1)} %get-tuple-element.54), channel_id=1, source_target_pairs={{0,8},{24,16},{1,9},{25,17},{2,10},{26,18},{3,11},{27,19},{4,12},{... | collective-permute-start | bytes 1179656 | tf_op jit(solution)/shard_map/ppermute | solution.py:507
  37.1 50.9 %slice-start.2 = ((s8[6291456]{0:T(1024)(128)(4,1)}), s8[4194304]{0:T(1024)(128)(4,1)S(1)}, s32[]{:S(2)}) async-start(s8[6291456]{0:T(1024)(128)(4,1)} %bitcast.15), calls=%async_computation.2 | async-start | bytes 8388608
  44.8 12.3 %collective-permute-start.10 = (bf16[384,512]{1,0:T(8,128)(2,1)S(1)}, bf16[384,512]{1,0:T(8,128)(2,1)S(1)}, u32[]{:S(2)}, u32[]{:S(2)}) collective-permute-start(bf16[384,512]{1,0:T(8,128)(2,1)S(1)} %get-tuple-element.55), channel_id=1, source_target_pairs={{0,8},{24,16},{1,9},{25,17},{2,10},{26,18},{3,11},{27,19},{4,12},{... | collective-permute-start | bytes 1179656 | tf_op jit(solution)/shard_map/ppermute | solution.py:507
  49.3 24.6 %collective-permute-start.17 = (bf16[192,2048]{1,0:T(8,128)(2,1)S(1)}, bf16[192,2048]{1,0:T(8,128)(2,1)S(1)}, u32[]{:S(2)}, u32[]{:S(2)}) collective-permute-start(bf16[192,2048]{1,0:T(8,128)(2,1)S(1)} %collective-permute-done.14.refs_0_), channel_id=1, source_target_pairs={{8,0},{16,24},{9,1},{17,25},{10,2},{18,26},{11,3},{19,27},{12,4},{... | collective-permute-start | bytes 2359304 | tf_op jit(solution)/shard_map/ppermute | solution.py:69
  50.7 15.1 %collective-permute-start.16 = (bf16[384,512]{1,0:T(8,128)(2,1)S(1)}, bf16[384,512]{1,0:T(8,128)(2,1)S(1)}, u32[]{:S(2)}, u32[]{:S(2)}) collective-permute-start(bf16[384,512]{1,0:T(8,128)(2,1)S(1)} %add_convert_fusion.7), channel_id=1, source_target_pairs={{8,16},{16,8},{9,17},{17,9},{10,18},{18,10},{11,19},{19,11},{12,20... | collective-permute-start | bytes 1179656 | tf_op jit(solution)/shard_map/ppermute | solution.py:514
  57.1 11.4 %collective-permute-start.11 = (bf16[384,512]{1,0:T(8,128)(2,1)S(1)}, bf16[384,512]{1,0:T(8,128)(2,1)S(1)}, u32[]{:S(2)}, u32[]{:S(2)}) collective-permute-start(bf16[384,512]{1,0:T(8,128)(2,1)S(1)} %get-tuple-element.56), channel_id=1, source_target_pairs={{0,8},{24,16},{1,9},{25,17},{2,10},{26,18},{3,11},{27,19},{4,12},{... | collective-permute-start | bytes 1179656 | tf_op jit(solution)/shard_map/ppermute | solution.py:507
  65.8 14.0 %collective-permute-start.22 = (bf16[384,512]{1,0:T(8,128)(2,1)S(1)}, bf16[384,512]{1,0:T(8,128)(2,1)S(1)}, u32[]{:S(2)}, u32[]{:S(2)}) collective-permute-start(bf16[384,512]{1,0:T(8,128)(2,1)S(1)} %add_convert_fusion.2), channel_id=1, source_target_pairs={{8,16},{16,8},{9,17},{17,9},{10,18},{18,10},{11,19},{19,11},{12,20... | collective-permute-start | bytes 1179656 | tf_op jit(solution)/shard_map/ppermute | solution.py:514
  68.5 10.5 %collective-permute-start.12 = (bf16[384,512]{1,0:T(8,128)(2,1)S(1)}, bf16[384,512]{1,0:T(8,128)(2,1)S(1)}, u32[]{:S(2)}, u32[]{:S(2)}) collective-permute-start(bf16[384,512]{1,0:T(8,128)(2,1)S(1)} %get-tuple-element.57), channel_id=1, source_target_pairs={{0,8},{24,16},{1,9},{25,17},{2,10},{26,18},{3,11},{27,19},{4,12},{... | collective-permute-start | bytes 1179656 | tf_op jit(solution)/shard_map/ppermute | solution.py:507
  73.0 15.0 %slice-start.3 = ((s8[6291456]{0:T(1024)(128)(4,1)}), s8[2097152]{0:T(1024)(128)(4,1)S(1)}, s32[]{:S(2)}) async-start(s8[6291456]{0:T(1024)(128)(4,1)} %bitcast.15), calls=%async_computation.3 | async-start | bytes 4194304
  73.1 8.2 %collective-permute-start.19 = (bf16[384,512]{1,0:T(8,128)(2,1)S(1)}, bf16[384,512]{1,0:T(8,128)(2,1)S(1)}, u32[]{:S(2)}, u32[]{:S(2)}) collective-permute-start(bf16[384,512]{1,0:T(8,128)(2,1)S(1)} %add_convert_fusion.5), channel_id=1, source_target_pairs={{8,16},{16,8},{9,17},{17,9},{10,18},{18,10},{11,19},{19,11},{12,20... | collective-permute-start | bytes 1179656 | tf_op jit(solution)/shard_map/ppermute | solution.py:514
  75.3 12.7 %slice-start = ((s8[6291456]{0:T(1024)(128)(4,1)}), s8[4194304]{0:T(1024)(128)(4,1)S(1)}, s32[]{:S(2)}) async-start(s8[6291456]{0:T(1024)(128)(4,1)} %bitcast.13), calls=%async_computation | async-start | bytes 8388608
  75.3 12.7 %collective-permute-start.18 = (bf16[384,512]{1,0:T(8,128)(2,1)S(1)}, bf16[384,512]{1,0:T(8,128)(2,1)S(1)}, u32[]{:S(2)}, u32[]{:S(2)}) collective-permute-start(bf16[384,512]{1,0:T(8,128)(2,1)S(1)} %add_convert_fusion.6.refs_0_), channel_id=1, source_target_pairs={{8,0},{16,24},{9,1},{17,25},{10,2},{18,26},{11,3},{19,27},{12,4},{... | collective-permute-start | bytes 1179656 | tf_op jit(solution)/shard_map/ppermute | solution.py:69
  79.1 14.6 %collective-permute-start.13 = (bf16[384,512]{1,0:T(8,128)(2,1)S(1)}, bf16[384,512]{1,0:T(8,128)(2,1)S(1)}, u32[]{:S(2)}, u32[]{:S(2)}) collective-permute-start(bf16[384,512]{1,0:T(8,128)(2,1)S(1)} %add_convert_fusion.8), channel_id=1, source_target_pairs={{8,16},{16,8},{9,17},{17,9},{10,18},{18,10},{11,19},{19,11},{12,20... | collective-permute-start | bytes 1179656 | tf_op jit(solution)/shard_map/ppermute | solution.py:514
  79.9 16.6 %collective-permute-start.23 = (bf16[384,512]{1,0:T(8,128)(2,1)S(1)}, bf16[384,512]{1,0:T(8,128)(2,1)S(1)}, u32[]{:S(2)}, u32[]{:S(2)}) collective-permute-start(bf16[384,512]{1,0:T(8,128)(2,1)S(1)} %add_convert_fusion.1.refs_0_), channel_id=1, source_target_pairs={{8,0},{16,24},{9,1},{17,25},{10,2},{18,26},{11,3},{19,27},{12,4},{... | collective-permute-start | bytes 1179656 | tf_op jit(solution)/shard_map/ppermute | solution.py:69
  81.3 6.7 %slice-start.1 = ((s8[6291456]{0:T(1024)(128)(4,1)}), s8[2097152]{0:T(1024)(128)(4,1)S(1)}, s32[]{:S(2)}) async-start(s8[6291456]{0:T(1024)(128)(4,1)} %bitcast.13), calls=%async_computation.1 | async-start | bytes 4194304
  81.3 23.6 %collective-permute-start.21 = (bf16[384,512]{1,0:T(8,128)(2,1)S(1)}, bf16[384,512]{1,0:T(8,128)(2,1)S(1)}, u32[]{:S(2)}, u32[]{:S(2)}) collective-permute-start(bf16[384,512]{1,0:T(8,128)(2,1)S(1)} %add_convert_fusion.4.refs_0_), channel_id=1, source_target_pairs={{8,0},{16,24},{9,1},{17,25},{10,2},{18,26},{11,3},{19,27},{12,4},{... | collective-permute-start | bytes 1179656 | tf_op jit(solution)/shard_map/ppermute | solution.py:69
  93.9 17.3 %collective-permute-start.20 = (bf16[384,512]{1,0:T(8,128)(2,1)S(1)}, bf16[384,512]{1,0:T(8,128)(2,1)S(1)}, u32[]{:S(2)}, u32[]{:S(2)}) collective-permute-start(bf16[384,512]{1,0:T(8,128)(2,1)S(1)} %add_convert_fusion.3.refs_0_), channel_id=1, source_target_pairs={{8,0},{16,24},{9,1},{17,25},{10,2},{18,26},{11,3},{19,27},{12,4},{... | collective-permute-start | bytes 1179656 | tf_op jit(solution)/shard_map/ppermute | solution.py:69
  114.3 2.1 %collective-permute-start.24 = (bf16[4,48,1536]{2,1,0:T(8,128)(2,1)S(1)}, bf16[4,48,1536]{2,1,0:T(8,128)(2,1)S(1)}, u32[]{:S(2)}, u32[]{:S(2)}) collective-permute-start(bf16[4,48,1536]{2,1,0:T(8,128)(2,1)S(1)} %get-tuple-element.81), channel_id=1, source_target_pairs={{0,1},{1,0},{2,3},{3,2},{4,5},{5,4},{6,7},{7,6},{8,9},{9,8},{10,11... | collective-permute-start | bytes 1769480 | tf_op jit(solution)/shard_map/ppermute | solution.py:534
  116.6 10.4 %collective-permute-start.25 = (bf16[48,1536]{1,0:T(8,128)(2,1)S(1)}, bf16[48,1536]{1,0:T(8,128)(2,1)S(1)}, u32[]{:S(2)}, u32[]{:S(2)}) collective-permute-start(bf16[48,1536]{1,0:T(8,128)(2,1)S(1)} %get-tuple-element.90), channel_id=1, source_target_pairs={{0,2},{1,3},{2,0},{3,1},{4,6},{5,7},{6,4},{7,5},{8,10},{9,11},{10,... | collective-permute-start | bytes 442376 | tf_op jit(solution)/shard_map/ppermute | solution.py:538
  118.2 8.8 %collective-permute-start.26 = (bf16[48,1536]{1,0:T(8,128)(2,1)S(1)}, bf16[48,1536]{1,0:T(8,128)(2,1)S(1)}, u32[]{:S(2)}, u32[]{:S(2)}) collective-permute-start(bf16[48,1536]{1,0:T(8,128)(2,1)S(1)} %get-tuple-element.92), channel_id=1, source_target_pairs={{0,4},{1,5},{2,6},{3,7},{4,0},{5,1},{6,2},{7,3},{8,12},{9,13},{10,... | collective-permute-start | bytes 442376 | tf_op jit(solution)/shard_map/ppermute | solution.py:538
  119.6 7.4 %collective-permute-start.27 = (bf16[48,1536]{1,0:T(8,128)(2,1)S(1)}, bf16[48,1536]{1,0:T(8,128)(2,1)S(1)}, u32[]{:S(2)}, u32[]{:S(2)}) collective-permute-start(bf16[48,1536]{1,0:T(8,128)(2,1)S(1)} %get-tuple-element.91), channel_id=1, source_target_pairs={{0,6},{1,7},{2,4},{3,5},{4,2},{5,3},{6,0},{7,1},{8,14},{9,15},{10,... | collective-permute-start | bytes 442376 | tf_op jit(solution)/shard_map/ppermute | solution.py:538

commit v5 on v4

--- a/solution.py
+++ b/solution.py
@@ -525,11 +525,13 @@
         sent.append(sent_out(held, place, n_row))
 
     for chunk in range(1, CHUNKS):
+        if chunk == CHUNKS - 2:
+            hidden = after(late[2], running)
+            down_grad = down_grads(ids, early[2], hidden, tokens, n_row, 1, 2, [down_grad])
+            running, down_grad = lax.optimization_barrier((running, down_grad))
         running, weight_out = work_on(chunk, running, weight_out)
     gate_grad, up_grad = weight_out
     keep, send = running
-    hidden = after(late[2], send)
-    down_grad = down_grads(ids, early[2], hidden, tokens, n_row, 1, 2, [down_grad])
 
     keep = add(keep, lax.ppermute(send, "col", [(i, i ^ 1) for i in range(n_col)]))
     input_grad = keep[0].astype(F32)

time: 128 us -> 129 us (level)
    ppermute x3, waiting for transfers between devices: 0.01 us -> 3.82 us  [on_device(): input_grad += lax.ppermute(keep[number], 'col', pairs).astype(F32)]
    ppermute x6, waiting for transfers between devices: 5.56 us -> 2.62 us  [sent_out(): got = lax.ppermute(block, 'row', outward([step], n))]
where the time goes in v5:
time: 129 us
  Pallas kernels  46.9 us (36%)
  starting transfers between devices  46 us (36%)
  waiting for transfers between devices  31.9 us (25%)
  other arithmetic  1.77 us (1%)
    ppermute x4, starting transfers between devices, on_device(): got = lax.ppermute(held, 'row', inward([step], n_row))  20.8 us
    pallas_call x4, Pallas kernels, deltas(): pl.pallas_call(functools.partial(delta_kernel, n, n_col, before is None,...  20.5 us
    ppermute x4, waiting for transfers between devices, on_device(): got = lax.ppermute(held, 'row', inward([step], n_row))  12.3 us
    ppermute x7, waiting for transfers between devices, cube_gather(): pieces[slot | bit] = lax.ppermute(pieces[slot], 'col', pairs)  11.1 us
    ppermute x6, starting transfers between devices, sent_out(): got = lax.ppermute(block, 'row', outward([step], n))  8.33 us
    pallas_call x2, Pallas kernels, partials(): pl.pallas_call(functools.partial(partial_kernel, len(pieces)), grid_spec=...  8.14 us
    pallas_call x2, Pallas kernels, down_grads(): pl.pallas_call(functools.partial(down_kernel, n), grid_spec=pltpu.Prefetc...  7.74 us
    pallas_call x2, Pallas kernels, factors_of(): pl.pallas_call(functools.partial(factor_kernel, n, count), grid_spec=pltp...  5.4 us
  transfers between devices with their start and end apart: 28, of which 11 were waited for; matrix products, arithmetic and copies ran while one was open for 1% of the time, Pallas kernels for 33%

profile of v5, /device:TPU:0, one launch (start us, length us, event | category | flops | bytes accessed | tf_op | source)
XLA Modules:
  0.0 128.6 jit_solution(12699974990855734977)
XLA Ops:
  0.6 1.2 join.1
  1.9 3.1 %collective-permute-start.7 = (bf16[192,2048]{1,0:T(8,128)(2,1)S(1)}, bf16[192,2048]{1,0:T(8,128)(2,1)}, u32[]{:S(2)}, u32[]{:S(2)}) collective-permute-start(bf16[192,2048]{1,0:T(8,128)(2,1)S(1)} %get-tuple-element.51.refs_0_), channel_id=1, source_target_pairs={{0,8},{24,16},{8,0},{16,24},{1,9},{25,17},{9,1},{17,25},{2,10},{26... | collective-permute-start | bytes 2359304 | tf_op jit(solution)/shard_map/ppermute | solution.py:55
  5.0 1.6 %collective-permute-start.8 = (bf16[192,2048]{1,0:T(8,128)(2,1)S(1)}, bf16[192,2048]{1,0:T(8,128)(2,1)}, u32[]{:S(2)}, u32[]{:S(2)}) collective-permute-start(bf16[192,2048]{1,0:T(8,128)(2,1)S(1)} %get-tuple-element.51.refs_0_), channel_id=1, source_target_pairs={{8,16},{16,8},{9,17},{17,9},{10,18},{18,10},{11,19},{19,11},{12,20... | collective-permute-start | bytes 2359304 | tf_op jit(solution)/shard_map/ppermute | solution.py:467
  6.5 0.9 copy-done
  7.4 1.5 %collective-permute-start.3 = (bf16[96,1536]{1,0:T(8,128)(2,1)S(1)}, bf16[96,1536]{1,0:T(8,128)(2,1)S(1)}, u32[]{:S(2)}, u32[]{:S(2)}) collective-permute-start(bf16[96,1536]{1,0:T(8,128)(2,1)S(1)} %get-tuple-element.49.refs_0_), channel_id=1, source_target_pairs={{0,4},{1,5},{2,6},{3,7},{4,0},{5,1},{6,2},{7,3},{8,12},{9,13},{10,... | collective-permute-start | bytes 884744 | tf_op jit(solution)/shard_map/ppermute | solution.py:86
  8.9 1.5 %collective-permute-start.1 = (bf16[96,1536]{1,0:T(8,128)(2,1)S(1)}, bf16[96,1536]{1,0:T(8,128)(2,1)S(1)}, u32[]{:S(2)}, u32[]{:S(2)}) collective-permute-start(bf16[96,1536]{1,0:T(8,128)(2,1)S(1)} %get-tuple-element.49.refs_0_), channel_id=1, source_target_pairs={{0,2},{1,3},{2,0},{3,1},{4,6},{5,7},{6,4},{7,5},{8,10},{9,11},{10,... | collective-permute-start | bytes 884744 | tf_op jit(solution)/shard_map/ppermute | solution.py:86
  10.4 5.5 %collective-permute-done.3.refs_4_ = bf16[96,1536]{1,0:T(8,128)(2,1)S(1)} collective-permute-done((bf16[96,1536]{1,0:T(8,128)(2,1)S(1)}, bf16[96,1536]{1,0:T(8,128)(2,1)S(1)}, u32[]{:S(2)}, u32[]{:S(2)}) %collective-permute-start.3) | collective-permute-done | bytes 294944 | tf_op jit(solution)/shard_map/ppermute | solution.py:86
  15.9 1.5 %collective-permute-start.5 = (bf16[96,1536]{1,0:T(8,128)(2,1)S(1)}, bf16[96,1536]{1,0:T(8,128)(2,1)S(1)}, u32[]{:S(2)}, u32[]{:S(2)}) collective-permute-start(bf16[96,1536]{1,0:T(8,128)(2,1)S(1)} %collective-permute-done.3.refs_4_), channel_id=1, source_target_pairs={{0,2},{1,3},{2,0},{3,1},{4,6},{5,7},{6,4},{7,5},{8,10},{9,11},{10,... | collective-permute-start | bytes 884744 | tf_op jit(solution)/shard_map/ppermute | solution.py:86
  17.9 5.7 %collective-permute-done.5.refs_6_ = bf16[96,1536]{1,0:T(8,128)(2,1)S(1)} collective-permute-done((bf16[96,1536]{1,0:T(8,128)(2,1)S(1)}, bf16[96,1536]{1,0:T(8,128)(2,1)S(1)}, u32[]{:S(2)}, u32[]{:S(2)}) %collective-permute-start.5) | collective-permute-done | bytes 294944 | tf_op jit(solution)/shard_map/ppermute | solution.py:86
  23.5 0.7 collective-permute-start.14
  24.3 1.3 %collective-permute-start.15 = (bf16[192,2048]{1,0:T(8,128)(2,1)}, bf16[192,2048]{1,0:T(8,128)(2,1)}, u32[]{:S(2)}, u32[]{:S(2)}) collective-permute-start(bf16[192,2048]{1,0:T(8,128)(2,1)} %collective-permute-done.8.refs_2_), channel_id=1, source_target_pairs={{8,0},{16,24},{9,1},{17,25},{10,2},{18,26},{11,3},{19,27},{12,4},{... | collective-permute-start | bytes 2359304 | tf_op jit(solution)/shard_map/ppermute | solution.py:69
  25.6 2.8 %hidden_grad_partials.2 = (bf16[384,512]{1,0:T(8,128)(2,1)S(1)}, bf16[384,1536]{1,0:T(8,128)(2,1)S(1)}) custom-call(s32[2]{0:T(128)S(1)} %pad_add_fusion.ids, bf16[96,1536]{1,0:T(8,128)(2,1)S(1)} %get-tuple-element.49.refs_0_, bf16[96,1536]{1,0:T(8,128)(2,1)S(1)} %collective-permute-done.refs_1_, bf16[96,1536]{1,0:T(8,128)(2,1)S(1)} %collective-permute-done.1.refs_2_, ...), custom_call_target="tpu_custom_call" | custom-call | flops 603979776 | bytes 3145728 | tf_op jit(solution)/shard_map/hidden_grad_partials/pallas_call | solution.py:193
  28.4 7.7 %collective-permute-start.9 = (bf16[384,512]{1,0:T(8,128)(2,1)S(1)}, bf16[384,512]{1,0:T(8,128)(2,1)S(1)}, u32[]{:S(2)}, u32[]{:S(2)}) collective-permute-start(bf16[384,512]{1,0:T(8,128)(2,1)S(1)} %get-tuple-element.56), channel_id=1, source_target_pairs={{0,8},{24,16},{1,9},{25,17},{2,10},{26,18},{3,11},{27,19},{4,12},{... | collective-permute-start | bytes 1179656 | tf_op jit(solution)/shard_map/ppermute | solution.py:507
  36.1 1.0 inputs_transposed.1.refs_8_.refs_9_.inputs
  37.1 5.4 %hidden_grad_partials.3 = (bf16[384,512]{1,0:T(8,128)(2,1)S(1)}, bf16[384,512]{1,0:T(8,128)(2,1)S(1)}, bf16[384,512]{1,0:T(8,128)(2,1)S(1)}) custom-call(s32[2]{0:T(128)S(1)} %pad_add_fusion.ids, bf16[384,1536]{1,0:T(8,128)(2,1)S(1)} %get-tuple-element.52.refs_0_.cotangent, bf16[2048,1536]{1,0:T(8,128)(2,1)} %refs_1_.3), custom_call_target="tpu_custom_call" | custom-call | flops 1811939328 | bytes 7077888 | tf_op jit(solution)/shard_map/hidden_grad_partials/pallas_call | solution.py:193
  42.5 2.4 %collective-permute-done.9 = bf16[384,512]{1,0:T(8,128)(2,1)S(1)} collective-permute-done((bf16[384,512]{1,0:T(8,128)(2,1)S(1)}, bf16[384,512]{1,0:T(8,128)(2,1)S(1)}, u32[]{:S(2)}, u32[]{:S(2)}) %collective-permute-start.9) | collective-permute-done | bytes 393248 | tf_op jit(solution)/shard_map/ppermute | solution.py:507
  44.8 4.4 %collective-permute-start.10 = (bf16[384,512]{1,0:T(8,128)(2,1)S(1)}, bf16[384,512]{1,0:T(8,128)(2,1)S(1)}, u32[]{:S(2)}, u32[]{:S(2)}) collective-permute-start(bf16[384,512]{1,0:T(8,128)(2,1)S(1)} %get-tuple-element.57), channel_id=1, source_target_pairs={{0,8},{24,16},{1,9},{25,17},{2,10},{26,18},{3,11},{27,19},{4,12},{... | collective-permute-start | bytes 1179656 | tf_op jit(solution)/shard_map/ppermute | solution.py:507
  49.3 1.3 %collective-permute-start.17 = (bf16[192,2048]{1,0:T(8,128)(2,1)S(1)}, bf16[192,2048]{1,0:T(8,128)(2,1)S(1)}, u32[]{:S(2)}, u32[]{:S(2)}) collective-permute-start(bf16[192,2048]{1,0:T(8,128)(2,1)S(1)} %collective-permute-done.14.refs_0_), channel_id=1, source_target_pairs={{8,0},{16,24},{9,1},{17,25},{10,2},{18,26},{11,3},{19,27},{12,4},{... | collective-permute-start | bytes 2359304 | tf_op jit(solution)/shard_map/ppermute | solution.py:69
  50.7 0.7 collective-permute-start.16
  51.4 5.8 %collective-permute-done.10 = bf16[384,512]{1,0:T(8,128)(2,1)S(1)} collective-permute-done((bf16[384,512]{1,0:T(8,128)(2,1)S(1)}, bf16[384,512]{1,0:T(8,128)(2,1)S(1)}, u32[]{:S(2)}, u32[]{:S(2)}) %collective-permute-start.10) | collective-permute-done | bytes 393248 | tf_op jit(solution)/shard_map/ppermute | solution.py:507
  57.1 4.4 %collective-permute-start.11 = (bf16[384,512]{1,0:T(8,128)(2,1)S(1)}, bf16[384,512]{1,0:T(8,128)(2,1)S(1)}, u32[]{:S(2)}, u32[]{:S(2)}) collective-permute-start(bf16[384,512]{1,0:T(8,128)(2,1)S(1)} %get-tuple-element.58), channel_id=1, source_target_pairs={{0,8},{24,16},{1,9},{25,17},{2,10},{26,18},{3,11},{27,19},{4,12},{... | collective-permute-start | bytes 1179656 | tf_op jit(solution)/shard_map/ppermute | solution.py:507
  61.6 4.1 %factors.2 = (bf16[288,2048]{1,0:T(8,128)(2,1)S(1)}, bf16[288,2048]{1,0:T(8,128)(2,1)S(1)}, bf16[288,2048]{1,0:T(8,128)(2,1)S(1)}) custom-call(s32[2]{0:T(128)S(1)} %pad_add_fusion.ids, bf16[192,2048]{1,0:T(8,128)(2,1)S(1)} %copy-done.1, bf16[192,2048]{1,0:T(8,128)(2,1)} %collective-permute-done.7.refs_1_, bf16[192,2048]{1,0:T(8,128)(2,1)} %collective-permute-done.8.refs_2_, ...), custom_call_target="tpu_custom_call" | custom-call | flops 5898240 | bytes 5898240 | tf_op jit(solution)/shard_map/factors/pallas_call | solution.py:262
  65.8 0.7 collective-permute-start.22
  66.5 2.1 %collective-permute-done.11 = bf16[384,512]{1,0:T(8,128)(2,1)S(1)} collective-permute-done((bf16[384,512]{1,0:T(8,128)(2,1)S(1)}, bf16[384,512]{1,0:T(8,128)(2,1)S(1)}, u32[]{:S(2)}, u32[]{:S(2)}) %collective-permute-start.11) | collective-permute-done | bytes 393248 | tf_op jit(solution)/shard_map/ppermute | solution.py:507
  68.5 4.4 %collective-permute-start.12 = (bf16[384,512]{1,0:T(8,128)(2,1)S(1)}, bf16[384,512]{1,0:T(8,128)(2,1)S(1)}, u32[]{:S(2)}, u32[]{:S(2)}) collective-permute-start(bf16[384,512]{1,0:T(8,128)(2,1)S(1)} %get-tuple-element.59), channel_id=1, source_target_pairs={{0,8},{24,16},{1,9},{25,17},{2,10},{26,18},{3,11},{27,19},{4,12},{... | collective-permute-start | bytes 1179656 | tf_op jit(solution)/shard_map/ppermute | solution.py:507
  73.1 0.8 collective-permute-start.19
  73.9 1.3 %factors.3 = (bf16[96,2048]{1,0:T(8,128)(2,1)S(1)}, bf16[96,2048]{1,0:T(8,128)(2,1)S(1)}, bf16[96,2048]{1,0:T(8,128)(2,1)S(1)}) custom-call(s32[2]{0:T(128)S(1)} %pad_add_fusion.ids, bf16[192,2048]{1,0:T(8,128)(2,1)S(1)} %collective-permute-done.14.refs_0_, bf16[192,2048]{1,0:T(8,128)(2,1)S(1)} %collective-permute-done.17.refs_1_), custom_call_target="tpu_custom_call" | custom-call | flops 1966080 | bytes 15728640 | tf_op jit(solution)/shard_map/factors/pallas_call | solution.py:262
  75.3 1.6 %collective-permute-start.18 = (bf16[384,512]{1,0:T(8,128)(2,1)S(1)}, bf16[384,512]{1,0:T(8,128)(2,1)S(1)}, u32[]{:S(2)}, u32[]{:S(2)}) collective-permute-start(bf16[384,512]{1,0:T(8,128)(2,1)S(1)} %add_convert_fusion.6.refs_0_), channel_id=1, source_target_pairs={{8,0},{16,24},{9,1},{17,25},{10,2},{18,26},{11,3},{19,27},{12,4},{... | collective-permute-start | bytes 1179656 | tf_op jit(solution)/shard_map/ppermute | solution.py:69
  76.9 2.1 %collective-permute-done.12 = bf16[384,512]{1,0:T(8,128)(2,1)S(1)} collective-permute-done((bf16[384,512]{1,0:T(8,128)(2,1)S(1)}, bf16[384,512]{1,0:T(8,128)(2,1)S(1)}, u32[]{:S(2)}, u32[]{:S(2)}) %collective-permute-start.12) | collective-permute-done | bytes 393248 | tf_op jit(solution)/shard_map/ppermute | solution.py:507
  79.1 0.7 collective-permute-start.13
  79.9 1.3 %collective-permute-start.23 = (bf16[384,512]{1,0:T(8,128)(2,1)S(1)}, bf16[384,512]{1,0:T(8,128)(2,1)S(1)}, u32[]{:S(2)}, u32[]{:S(2)}) collective-permute-start(bf16[384,512]{1,0:T(8,128)(2,1)S(1)} %add_convert_fusion.1.refs_0_), channel_id=1, source_target_pairs={{8,0},{16,24},{9,1},{17,25},{10,2},{18,26},{11,3},{19,27},{12,4},{... | collective-permute-start | bytes 1179656 | tf_op jit(solution)/shard_map/ppermute | solution.py:69
  81.3 1.4 %collective-permute-start.21 = (bf16[384,512]{1,0:T(8,128)(2,1)S(1)}, bf16[384,512]{1,0:T(8,128)(2,1)S(1)}, u32[]{:S(2)}, u32[]{:S(2)}) collective-permute-start(bf16[384,512]{1,0:T(8,128)(2,1)S(1)} %add_convert_fusion.4.refs_0_), channel_id=1, source_target_pairs={{8,0},{16,24},{9,1},{17,25},{10,2},{18,26},{11,3},{19,27},{12,4},{... | collective-permute-start | bytes 1179656 | tf_op jit(solution)/shard_map/ppermute | solution.py:69
  82.8 3.9 %down_grad.2.refs_0_ = bf16[2048,1536]{1,0:T(8,128)(2,1)} custom-call(s32[2]{0:T(128)S(1)} %pad_add_fusion.ids, bf16[288,2048]{1,0:T(8,128)(2,1)S(1)} %get-tuple-element.63.early, bf16[96,2048]{1,0:T(8,128)(2,1)S(1)} %get-tuple-element.79.late, bf16[384,1536]{1,0:T(8,128)(2,1)S(1)} %get-tuple-element.52.refs_0_.cotangent), custom_call_target="tpu_custom_call" | custom-call | flops 1207959552 | bytes 5111808 | tf_op jit(solution)/shard_map/down_grad/pallas_call | solution.py:298
  86.6 1.4 %collective-permute-done.18.refs_1_ = bf16[384,512]{1,0:T(8,128)(2,1)S(1)} collective-permute-done((bf16[384,512]{1,0:T(8,128)(2,1)S(1)}, bf16[384,512]{1,0:T(8,128)(2,1)S(1)}, u32[]{:S(2)}, u32[]{:S(2)}) %collective-permute-start.18) | collective-permute-done | bytes 393248 | tf_op jit(solution)/shard_map/ppermute | solution.py:69
  88.1 5.7 %chunk.4 = (f32[384,1536]{1,0:T(8,128)S(1)}, bf16[1536,2048]{1,0:T(8,128)(2,1)}, bf16[1536,2048]{1,0:T(8,128)(2,1)}) custom-call(s32[2]{0:T(128)S(1)} %pad_add_fusion.ids, bf16[384,512]{1,0:T(8,128)(2,1)S(1)} %add_convert_fusion.6.refs_0_, bf16[384,512]{1,0:T(8,128)(2,1)S(1)} %collective-permute-done.18.refs_1_, ...), custom_call_target="tpu_custom_call" | custom-call | tf_op jit(solution)/shard_map/chunk/pallas_call | solution.py:399
  93.9 1.5 %collective-permute-start.20 = (bf16[384,512]{1,0:T(8,128)(2,1)S(1)}, bf16[384,512]{1,0:T(8,128)(2,1)S(1)}, u32[]{:S(2)}, u32[]{:S(2)}) collective-permute-start(bf16[384,512]{1,0:T(8,128)(2,1)S(1)} %add_convert_fusion.3.refs_0_), channel_id=1, source_target_pairs={{8,0},{16,24},{9,1},{17,25},{10,2},{18,26},{11,3},{19,27},{12,4},{... | collective-permute-start | bytes 1179656 | tf_op jit(solution)/shard_map/ppermute | solution.py:69
  95.3 1.2 collective-permute-done.23.refs_1_
  96.6 5.8 %chunk.5 = (f32[384,1536]{1,0:T(8,128)S(1)}, bf16[1536,2048]{1,0:T(8,128)(2,1)}, bf16[1536,2048]{1,0:T(8,128)(2,1)}) custom-call(s32[2]{0:T(128)S(1)} %pad_add_fusion.ids, bf16[384,512]{1,0:T(8,128)(2,1)S(1)} %add_convert_fusion.1.refs_0_, bf16[384,512]{1,0:T(8,128)(2,1)S(1)} %collective-permute-done.23.refs_1_, ...), custom_call_target="tpu_custom_call", output_to_operand_aliasing={{1}: (11, {}), {2}: (12, {})} | custom-call | tf_op jit(solution)/shard_map/chunk/pallas_call | solution.py:399
  102.4 3.9 %down_grad.3 = bf16[2048,1536]{1,0:T(8,128)(2,1)} custom-call(s32[2]{0:T(128)S(1)} %pad_add_fusion.ids, bf16[288,2048]{1,0:T(8,128)(2,1)S(1)} %get-tuple-element.63.early, bf16[96,2048]{1,0:T(8,128)(2,1)S(1)} %get-tuple-element.79.late, bf16[384,1536]{1,0:T(8,128)(2,1)S(1)} %get-tuple-element.52.refs_0_.cotangent, ...), custom_call_target="tpu_custom_call", output_to_operand_aliasing={{}: (4, {})} | custom-call | flops 1207959552 | bytes 5111808 | tf_op jit(solution)/shard_map/down_grad/pallas_call | solution.py:298
  106.3 5.8 %chunk.6 = (f32[384,1536]{1,0:T(8,128)S(1)}, bf16[1536,2048]{1,0:T(8,128)(2,1)}, bf16[1536,2048]{1,0:T(8,128)(2,1)}) custom-call(s32[2]{0:T(128)S(1)} %pad_add_fusion.ids, bf16[384,512]{1,0:T(8,128)(2,1)S(1)} %add_convert_fusion.4.refs_0_, bf16[384,512]{1,0:T(8,128)(2,1)S(1)} %collective-permute-done.21.refs_1_, ...), custom_call_target="tpu_custom_call", output_to_operand_aliasing={{1}: (11, {}), {2}: (12, {})} | custom-call | tf_op jit(solution)/shard_map/chunk/pallas_call | solution.py:399
  112.1 3.1 %chunk.7 = (bf16[384,512]{1,0:T(8,128)(2,1)S(1)}, bf16[384,512]{1,0:T(8,128)(2,1)S(1)}, bf16[4,48,1536]{2,1,0:T(8,128)(2,1)S(1)}, bf16[4,48,1536]{2,1,0:T(8,128)(2,1)S(1)}) custom-call(s32[2]{0:T(128)S(1)} %pad_add_fusion.ids, bf16[384,512]{1,0:T(8,128)(2,1)S(1)} %add_convert_fusion.3.refs_0_, bf16[384,512]{1,0:T(8,128)(2,1)S(1)} %collective-permute-done.20.refs_1_, ...), custom_call_target="tpu_custom_call" | custom-call | tf_op jit(solution)/shard_map/chunk/pallas_call | solution.py:399
  115.4 2.0 %collective-permute-done.24 = bf16[4,48,1536]{2,1,0:T(8,128)(2,1)S(1)} collective-permute-done((bf16[4,48,1536]{2,1,0:T(8,128)(2,1)S(1)}, bf16[4,48,1536]{2,1,0:T(8,128)(2,1)S(1)}, u32[]{:S(2)}, u32[]{:S(2)}) %collective-permute-start.24) | collective-permute-done | bytes 589856 | tf_op jit(solution)/shard_map/ppermute | solution.py:536
  117.5 1.6 %collective-permute-start.25 = (bf16[48,1536]{1,0:T(8,128)(2,1)S(1)}, bf16[48,1536]{1,0:T(8,128)(2,1)S(1)}, u32[]{:S(2)}, u32[]{:S(2)}) collective-permute-start(bf16[48,1536]{1,0:T(8,128)(2,1)S(1)} %get-tuple-element.94), channel_id=1, source_target_pairs={{0,2},{1,3},{2,0},{3,1},{4,6},{5,7},{6,4},{7,5},{8,10},{9,11},{10,... | collective-permute-start | bytes 442376 | tf_op jit(solution)/shard_map/ppermute | solution.py:540
  119.1 1.4 %collective-permute-start.26 = (bf16[48,1536]{1,0:T(8,128)(2,1)S(1)}, bf16[48,1536]{1,0:T(8,128)(2,1)S(1)}, u32[]{:S(2)}, u32[]{:S(2)}) collective-permute-start(bf16[48,1536]{1,0:T(8,128)(2,1)S(1)} %get-tuple-element.96), channel_id=1, source_target_pairs={{0,4},{1,5},{2,6},{3,7},{4,0},{5,1},{6,2},{7,3},{8,12},{9,13},{10,... | collective-permute-start | bytes 442376 | tf_op jit(solution)/shard_map/ppermute | solution.py:540
  120.5 0.6 collective-permute-start.27
  121.1 3.0 %gate_and_up_grad.1 = (bf16[1536,2048]{1,0:T(8,128)(2,1)}, bf16[1536,2048]{1,0:T(8,128)(2,1)}) custom-call(bf16[1536,384]{1,0:T(8,128)(2,1)S(1)} %inputs_transposed.1.refs_8_.refs_9_.inputs, bf16[384,512]{1,0:T(8,128)(2,1)S(1)} %get-tuple-element.87.gate_delta, ...), custom_call_target="tpu_custom_call", output_to_operand_aliasing={{0}: (3, {}), {1}: (4, {})} | custom-call | flops 1207959552 | bytes 5111808 | tf_op jit(solution)/shard_map/gate_and_up_grad/pallas_call | solution.py:435
  124.2 3.7 %collective-permute-done.26 = bf16[48,1536]{1,0:T(8,128)(2,1)S(1)} collective-permute-done((bf16[48,1536]{1,0:T(8,128)(2,1)S(1)}, bf16[48,1536]{1,0:T(8,128)(2,1)S(1)}, u32[]{:S(2)}, u32[]{:S(2)}) %collective-permute-start.26) | collective-permute-done | bytes 147488 | tf_op jit(solution)/shard_map/ppermute | solution.py:540
  127.9 0.7 fusion.2
  (47 shorter events, 1.8 us)
Async XLA Ops:
  1.9 21.7 %collective-permute-start.7 = (bf16[192,2048]{1,0:T(8,128)(2,1)S(1)}, bf16[192,2048]{1,0:T(8,128)(2,1)}, u32[]{:S(2)}, u32[]{:S(2)}) collective-permute-start(bf16[192,2048]{1,0:T(8,128)(2,1)S(1)} %get-tuple-element.51.refs_0_), channel_id=1, source_target_pairs={{0,8},{24,16},{8,0},{16,24},{1,9},{25,17},{9,1},{17,25},{2,10},{26... | collective-permute-start | bytes 2359304 | tf_op jit(solution)/shard_map/ppermute | solution.py:55
  5.0 19.3 %collective-permute-start.8 = (bf16[192,2048]{1,0:T(8,128)(2,1)S(1)}, bf16[192,2048]{1,0:T(8,128)(2,1)}, u32[]{:S(2)}, u32[]{:S(2)}) collective-permute-start(bf16[192,2048]{1,0:T(8,128)(2,1)S(1)} %get-tuple-element.51.refs_0_), channel_id=1, source_target_pairs={{8,16},{16,8},{9,17},{17,9},{10,18},{18,10},{11,19},{19,11},{12,20... | collective-permute-start | bytes 2359304 | tf_op jit(solution)/shard_map/ppermute | solution.py:467
  6.5 0.9 copy-start
  7.4 8.5 %collective-permute-start.3 = (bf16[96,1536]{1,0:T(8,128)(2,1)S(1)}, bf16[96,1536]{1,0:T(8,128)(2,1)S(1)}, u32[]{:S(2)}, u32[]{:S(2)}) collective-permute-start(bf16[96,1536]{1,0:T(8,128)(2,1)S(1)} %get-tuple-element.49.refs_0_), channel_id=1, source_target_pairs={{0,4},{1,5},{2,6},{3,7},{4,0},{5,1},{6,2},{7,3},{8,12},{9,13},{10,... | collective-permute-start | bytes 884744 | tf_op jit(solution)/shard_map/ppermute | solution.py:86
  8.9 8.4 %collective-permute-start.1 = (bf16[96,1536]{1,0:T(8,128)(2,1)S(1)}, bf16[96,1536]{1,0:T(8,128)(2,1)S(1)}, u32[]{:S(2)}, u32[]{:S(2)}) collective-permute-start(bf16[96,1536]{1,0:T(8,128)(2,1)S(1)} %get-tuple-element.49.refs_0_), channel_id=1, source_target_pairs={{0,2},{1,3},{2,0},{3,1},{4,6},{5,7},{6,4},{7,5},{8,10},{9,11},{10,... | collective-permute-start | bytes 884744 | tf_op jit(solution)/shard_map/ppermute | solution.py:86
  10.4 7.0 %collective-permute-start = (bf16[96,1536]{1,0:T(8,128)(2,1)S(1)}, bf16[96,1536]{1,0:T(8,128)(2,1)S(1)}, u32[]{:S(2)}, u32[]{:S(2)}) collective-permute-start(bf16[96,1536]{1,0:T(8,128)(2,1)S(1)} %get-tuple-element.49.refs_0_), channel_id=1, source_target_pairs={{0,1},{1,0},{2,3},{3,2},{4,5},{5,4},{6,7},{7,6},{8,9},{9,8},{10,11... | collective-permute-start | bytes 884744 | tf_op jit(solution)/shard_map/ppermute | solution.py:86
  15.9 7.7 %collective-permute-start.5 = (bf16[96,1536]{1,0:T(8,128)(2,1)S(1)}, bf16[96,1536]{1,0:T(8,128)(2,1)S(1)}, u32[]{:S(2)}, u32[]{:S(2)}) collective-permute-start(bf16[96,1536]{1,0:T(8,128)(2,1)S(1)} %collective-permute-done.3.refs_4_), channel_id=1, source_target_pairs={{0,2},{1,3},{2,0},{3,1},{4,6},{5,7},{6,4},{7,5},{8,10},{9,11},{10,... | collective-permute-start | bytes 884744 | tf_op jit(solution)/shard_map/ppermute | solution.py:86
  17.4 8.3 %collective-permute-start.4 = (bf16[96,1536]{1,0:T(8,128)(2,1)S(1)}, bf16[96,1536]{1,0:T(8,128)(2,1)S(1)}, u32[]{:S(2)}, u32[]{:S(2)}) collective-permute-start(bf16[96,1536]{1,0:T(8,128)(2,1)S(1)} %collective-permute-done.3.refs_4_), channel_id=1, source_target_pairs={{0,1},{1,0},{2,3},{3,2},{4,5},{5,4},{6,7},{7,6},{8,9},{9,8},{10,11... | collective-permute-start | bytes 884744 | tf_op jit(solution)/shard_map/ppermute | solution.py:86
  17.4 8.3 %collective-permute-start.2 = (bf16[96,1536]{1,0:T(8,128)(2,1)S(1)}, bf16[96,1536]{1,0:T(8,128)(2,1)S(1)}, u32[]{:S(2)}, u32[]{:S(2)}) collective-permute-start(bf16[96,1536]{1,0:T(8,128)(2,1)S(1)} %collective-permute-done.1.refs_2_), channel_id=1, source_target_pairs={{0,1},{1,0},{2,3},{3,2},{4,5},{5,4},{6,7},{7,6},{8,9},{9,8},{10,11... | collective-permute-start | bytes 884744 | tf_op jit(solution)/shard_map/ppermute | solution.py:86
  23.5 2.1 %collective-permute-start.6 = (bf16[96,1536]{1,0:T(8,128)(2,1)S(1)}, bf16[96,1536]{1,0:T(8,128)(2,1)S(1)}, u32[]{:S(2)}, u32[]{:S(2)}) collective-permute-start(bf16[96,1536]{1,0:T(8,128)(2,1)S(1)} %collective-permute-done.5.refs_6_), channel_id=1, source_target_pairs={{0,1},{1,0},{2,3},{3,2},{4,5},{5,4},{6,7},{7,6},{8,9},{9,8},{10,11... | collective-permute-start | bytes 884744 | tf_op jit(solution)/shard_map/ppermute | solution.py:86
  23.5 25.7 %collective-permute-start.14 = (bf16[192,2048]{1,0:T(8,128)(2,1)}, bf16[192,2048]{1,0:T(8,128)(2,1)S(1)}, u32[]{:S(2)}, u32[]{:S(2)}) collective-permute-start(bf16[192,2048]{1,0:T(8,128)(2,1)} %collective-permute-done.7.refs_1_), channel_id=1, source_target_pairs={{8,16},{16,8},{9,17},{17,9},{10,18},{18,10},{11,19},{19,11},{12,20... | collective-permute-start | bytes 2359304 | tf_op jit(solution)/shard_map/ppermute | solution.py:467
  24.3 25.0 %collective-permute-start.15 = (bf16[192,2048]{1,0:T(8,128)(2,1)}, bf16[192,2048]{1,0:T(8,128)(2,1)}, u32[]{:S(2)}, u32[]{:S(2)}) collective-permute-start(bf16[192,2048]{1,0:T(8,128)(2,1)} %collective-permute-done.8.refs_2_), channel_id=1, source_target_pairs={{8,0},{16,24},{9,1},{17,25},{10,2},{18,26},{11,3},{19,27},{12,4},{... | collective-permute-start | bytes 2359304 | tf_op jit(solution)/shard_map/ppermute | solution.py:69
  28.4 33.1 %copy-start.1 = (bf16[192,2048]{1,0:T(8,128)(2,1)S(1)}, bf16[192,2048]{1,0:T(8,128)(2,1)}, u32[]{:S(2)}) copy-start(bf16[192,2048]{1,0:T(8,128)(2,1)} %copy-done) | copy-start | bytes 2359300
  28.4 16.4 %collective-permute-start.9 = (bf16[384,512]{1,0:T(8,128)(2,1)S(1)}, bf16[384,512]{1,0:T(8,128)(2,1)S(1)}, u32[]{:S(2)}, u32[]{:S(2)}) collective-permute-start(bf16[384,512]{1,0:T(8,128)(2,1)S(1)} %get-tuple-element.56), channel_id=1, source_target_pairs={{0,8},{24,16},{1,9},{25,17},{2,10},{26,18},{3,11},{27,19},{4,12},{... | collective-permute-start | bytes 1179656 | tf_op jit(solution)/shard_map/ppermute | solution.py:507
  37.1 50.9 %slice-start.2 = ((s8[6291456]{0:T(1024)(128)(4,1)}), s8[4194304]{0:T(1024)(128)(4,1)S(1)}, s32[]{:S(2)}) async-start(s8[6291456]{0:T(1024)(128)(4,1)} %bitcast.15), calls=%async_computation.2 | async-start | bytes 8388608
  44.8 12.3 %collective-permute-start.10 = (bf16[384,512]{1,0:T(8,128)(2,1)S(1)}, bf16[384,512]{1,0:T(8,128)(2,1)S(1)}, u32[]{:S(2)}, u32[]{:S(2)}) collective-permute-start(bf16[384,512]{1,0:T(8,128)(2,1)S(1)} %get-tuple-element.57), channel_id=1, source_target_pairs={{0,8},{24,16},{1,9},{25,17},{2,10},{26,18},{3,11},{27,19},{4,12},{... | collective-permute-start | bytes 1179656 | tf_op jit(solution)/shard_map/ppermute | solution.py:507
  49.3 24.6 %collective-permute-start.17 = (bf16[192,2048]{1,0:T(8,128)(2,1)S(1)}, bf16[192,2048]{1,0:T(8,128)(2,1)S(1)}, u32[]{:S(2)}, u32[]{:S(2)}) collective-permute-start(bf16[192,2048]{1,0:T(8,128)(2,1)S(1)} %collective-permute-done.14.refs_0_), channel_id=1, source_target_pairs={{8,0},{16,24},{9,1},{17,25},{10,2},{18,26},{11,3},{19,27},{12,4},{... | collective-permute-start | bytes 2359304 | tf_op jit(solution)/shard_map/ppermute | solution.py:69
  50.7 15.1 %collective-permute-start.16 = (bf16[384,512]{1,0:T(8,128)(2,1)S(1)}, bf16[384,512]{1,0:T(8,128)(2,1)S(1)}, u32[]{:S(2)}, u32[]{:S(2)}) collective-permute-start(bf16[384,512]{1,0:T(8,128)(2,1)S(1)} %add_convert_fusion.7), channel_id=1, source_target_pairs={{8,16},{16,8},{9,17},{17,9},{10,18},{18,10},{11,19},{19,11},{12,20... | collective-permute-start | bytes 1179656 | tf_op jit(solution)/shard_map/ppermute | solution.py:514
  57.1 11.4 %collective-permute-start.11 = (bf16[384,512]{1,0:T(8,128)(2,1)S(1)}, bf16[384,512]{1,0:T(8,128)(2,1)S(1)}, u32[]{:S(2)}, u32[]{:S(2)}) collective-permute-start(bf16[384,512]{1,0:T(8,128)(2,1)S(1)} %get-tuple-element.58), channel_id=1, source_target_pairs={{0,8},{24,16},{1,9},{25,17},{2,10},{26,18},{3,11},{27,19},{4,12},{... | collective-permute-start | bytes 1179656 | tf_op jit(solution)/shard_map/ppermute | solution.py:507
  65.8 14.0 %collective-permute-start.22 = (bf16[384,512]{1,0:T(8,128)(2,1)S(1)}, bf16[384,512]{1,0:T(8,128)(2,1)S(1)}, u32[]{:S(2)}, u32[]{:S(2)}) collective-permute-start(bf16[384,512]{1,0:T(8,128)(2,1)S(1)} %add_convert_fusion.2), channel_id=1, source_target_pairs={{8,16},{16,8},{9,17},{17,9},{10,18},{18,10},{11,19},{19,11},{12,20... | collective-permute-start | bytes 1179656 | tf_op jit(solution)/shard_map/ppermute | solution.py:514
  68.5 10.5 %collective-permute-start.12 = (bf16[384,512]{1,0:T(8,128)(2,1)S(1)}, bf16[384,512]{1,0:T(8,128)(2,1)S(1)}, u32[]{:S(2)}, u32[]{:S(2)}) collective-permute-start(bf16[384,512]{1,0:T(8,128)(2,1)S(1)} %get-tuple-element.59), channel_id=1, source_target_pairs={{0,8},{24,16},{1,9},{25,17},{2,10},{26,18},{3,11},{27,19},{4,12},{... | collective-permute-start | bytes 1179656 | tf_op jit(solution)/shard_map/ppermute | solution.py:507
  73.0 15.0 %slice-start.3 = ((s8[6291456]{0:T(1024)(128)(4,1)}), s8[2097152]{0:T(1024)(128)(4,1)S(1)}, s32[]{:S(2)}) async-start(s8[6291456]{0:T(1024)(128)(4,1)} %bitcast.15), calls=%async_computation.3 | async-start | bytes 4194304
  73.1 8.2 %collective-permute-start.19 = (bf16[384,512]{1,0:T(8,128)(2,1)S(1)}, bf16[384,512]{1,0:T(8,128)(2,1)S(1)}, u32[]{:S(2)}, u32[]{:S(2)}) collective-permute-start(bf16[384,512]{1,0:T(8,128)(2,1)S(1)} %add_convert_fusion.5), channel_id=1, source_target_pairs={{8,16},{16,8},{9,17},{17,9},{10,18},{18,10},{11,19},{19,11},{12,20... | collective-permute-start | bytes 1179656 | tf_op jit(solution)/shard_map/ppermute | solution.py:514
  75.3 12.7 %slice-start = ((s8[6291456]{0:T(1024)(128)(4,1)}), s8[4194304]{0:T(1024)(128)(4,1)S(1)}, s32[]{:S(2)}) async-start(s8[6291456]{0:T(1024)(128)(4,1)} %bitcast.13), calls=%async_computation | async-start | bytes 8388608
  75.3 12.7 %collective-permute-start.18 = (bf16[384,512]{1,0:T(8,128)(2,1)S(1)}, bf16[384,512]{1,0:T(8,128)(2,1)S(1)}, u32[]{:S(2)}, u32[]{:S(2)}) collective-permute-start(bf16[384,512]{1,0:T(8,128)(2,1)S(1)} %add_convert_fusion.6.refs_0_), channel_id=1, source_target_pairs={{8,0},{16,24},{9,1},{17,25},{10,2},{18,26},{11,3},{19,27},{12,4},{... | collective-permute-start | bytes 1179656 | tf_op jit(solution)/shard_map/ppermute | solution.py:69
  79.1 14.6 %collective-permute-start.13 = (bf16[384,512]{1,0:T(8,128)(2,1)S(1)}, bf16[384,512]{1,0:T(8,128)(2,1)S(1)}, u32[]{:S(2)}, u32[]{:S(2)}) collective-permute-start(bf16[384,512]{1,0:T(8,128)(2,1)S(1)} %add_convert_fusion.8), channel_id=1, source_target_pairs={{8,16},{16,8},{9,17},{17,9},{10,18},{18,10},{11,19},{19,11},{12,20... | collective-permute-start | bytes 1179656 | tf_op jit(solution)/shard_map/ppermute | solution.py:514
  79.9 16.6 %collective-permute-start.23 = (bf16[384,512]{1,0:T(8,128)(2,1)S(1)}, bf16[384,512]{1,0:T(8,128)(2,1)S(1)}, u32[]{:S(2)}, u32[]{:S(2)}) collective-permute-start(bf16[384,512]{1,0:T(8,128)(2,1)S(1)} %add_convert_fusion.1.refs_0_), channel_id=1, source_target_pairs={{8,0},{16,24},{9,1},{17,25},{10,2},{18,26},{11,3},{19,27},{12,4},{... | collective-permute-start | bytes 1179656 | tf_op jit(solution)/shard_map/ppermute | solution.py:69
  81.3 6.7 %slice-start.1 = ((s8[6291456]{0:T(1024)(128)(4,1)}), s8[2097152]{0:T(1024)(128)(4,1)S(1)}, s32[]{:S(2)}) async-start(s8[6291456]{0:T(1024)(128)(4,1)} %bitcast.13), calls=%async_computation.1 | async-start | bytes 4194304
  81.3 24.9 %collective-permute-start.21 = (bf16[384,512]{1,0:T(8,128)(2,1)S(1)}, bf16[384,512]{1,0:T(8,128)(2,1)S(1)}, u32[]{:S(2)}, u32[]{:S(2)}) collective-permute-start(bf16[384,512]{1,0:T(8,128)(2,1)S(1)} %add_convert_fusion.4.refs_0_), channel_id=1, source_target_pairs={{8,0},{16,24},{9,1},{17,25},{10,2},{18,26},{11,3},{19,27},{12,4},{... | collective-permute-start | bytes 1179656 | tf_op jit(solution)/shard_map/ppermute | solution.py:69
  93.9 18.3 %collective-permute-start.20 = (bf16[384,512]{1,0:T(8,128)(2,1)S(1)}, bf16[384,512]{1,0:T(8,128)(2,1)S(1)}, u32[]{:S(2)}, u32[]{:S(2)}) collective-permute-start(bf16[384,512]{1,0:T(8,128)(2,1)S(1)} %add_convert_fusion.3.refs_0_), channel_id=1, source_target_pairs={{8,0},{16,24},{9,1},{17,25},{10,2},{18,26},{11,3},{19,27},{12,4},{... | collective-permute-start | bytes 1179656 | tf_op jit(solution)/shard_map/ppermute | solution.py:69
  115.3 2.1 %collective-permute-start.24 = (bf16[4,48,1536]{2,1,0:T(8,128)(2,1)S(1)}, bf16[4,48,1536]{2,1,0:T(8,128)(2,1)S(1)}, u32[]{:S(2)}, u32[]{:S(2)}) collective-permute-start(bf16[4,48,1536]{2,1,0:T(8,128)(2,1)S(1)} %get-tuple-element.86), channel_id=1, source_target_pairs={{0,1},{1,0},{2,3},{3,2},{4,5},{5,4},{6,7},{7,6},{8,9},{9,8},{10,11... | collective-permute-start | bytes 1769480 | tf_op jit(solution)/shard_map/ppermute | solution.py:536
  117.5 6.6 %collective-permute-start.25 = (bf16[48,1536]{1,0:T(8,128)(2,1)S(1)}, bf16[48,1536]{1,0:T(8,128)(2,1)S(1)}, u32[]{:S(2)}, u32[]{:S(2)}) collective-permute-start(bf16[48,1536]{1,0:T(8,128)(2,1)S(1)} %get-tuple-element.94), channel_id=1, source_target_pairs={{0,2},{1,3},{2,0},{3,1},{4,6},{5,7},{6,4},{7,5},{8,10},{9,11},{10,... | collective-permute-start | bytes 442376 | tf_op jit(solution)/shard_map/ppermute | solution.py:540
  119.1 8.8 %collective-permute-start.26 = (bf16[48,1536]{1,0:T(8,128)(2,1)S(1)}, bf16[48,1536]{1,0:T(8,128)(2,1)S(1)}, u32[]{:S(2)}, u32[]{:S(2)}) collective-permute-start(bf16[48,1536]{1,0:T(8,128)(2,1)S(1)} %get-tuple-element.96), channel_id=1, source_target_pairs={{0,4},{1,5},{2,6},{3,7},{4,0},{5,1},{6,2},{7,3},{8,12},{9,13},{10,... | collective-permute-start | bytes 442376 | tf_op jit(solution)/shard_map/ppermute | solution.py:540
  120.5 7.4 %collective-permute-start.27 = (bf16[48,1536]{1,0:T(8,128)(2,1)S(1)}, bf16[48,1536]{1,0:T(8,128)(2,1)S(1)}, u32[]{:S(2)}, u32[]{:S(2)}) collective-permute-start(bf16[48,1536]{1,0:T(8,128)(2,1)S(1)} %get-tuple-element.95), channel_id=1, source_target_pairs={{0,6},{1,7},{2,4},{3,5},{4,2},{5,3},{6,0},{7,1},{8,14},{9,15},{10,... | collective-permute-start | bytes 442376 | tf_op jit(solution)/shard_map/ppermute | solution.py:540
